TPU v7x, 32 devices: a whole 2x2x4 slice. The times are simulated.
32 devices in a mesh: fsdp: 16 (over z, y, core), tp: 2 (over x).
Axes of the slice: x: 2, y: 2, z: 4, core: 2. Of those that a mesh axis runs over, the one named last changes fastest.
Arguments:
- entering_states: bfloat16 [35328, 1024], P(('fsdp', 'tp')), may hold values from -6 to 6
- bypass_states: bfloat16 [35328, 1024], P(('fsdp', 'tp')), may hold values from -6 to 6
- mentor_states: bfloat16 [35328, 1024], P(('fsdp', 'tp')), may hold values from -18 to 18
- occupancy_mask: int32 [32], P('fsdp'), may hold values from 0 to 1, as said below
- bypass_merge_matrix: bfloat16 [2048, 1024], P(('fsdp', 'tp')), may hold values from -0.125 to 0.125
- bypass_merge_offset: bfloat16 [1024], P(('fsdp', 'tp')), may hold values from -1.5 to 1.5
- mixer_layernorm_scale: bfloat16 [1024], P(('fsdp', 'tp')), may hold values from 0.25 to 1.75
- mixer_layernorm_offset: bfloat16 [1024], P(('fsdp', 'tp')), may hold values from -1.5 to 1.5
- asking_map_matrix: bfloat16 [1024, 1024], P('fsdp', 'tp'), may hold values from -0.3125 to 0.3125
- lookup_map_matrix: bfloat16 [1024, 1024], P('fsdp', 'tp'), may hold values from -0.3125 to 0.3125
- content_map_matrix: bfloat16 [1024, 1024], P('fsdp', 'tp'), may hold values from -0.1875 to 0.1875
- mixer_result_matrix: bfloat16 [1024, 1024], P('tp', 'fsdp'), may hold values from -0.25 to 0.25
- mixer_result_offset: bfloat16 [1024], P(('fsdp', 'tp')), may hold values from -1.5 to 1.5
- perceptron_layernorm_scale: bfloat16 [1024], P(('fsdp', 'tp')), may hold values from 0.25 to 1.75
- perceptron_layernorm_offset: bfloat16 [1024], P(('fsdp', 'tp')), may hold values from -1.5 to 1.5
- expand_layer_matrix: bfloat16 [1024, 4096], P('fsdp', 'tp'), may hold values from -0.1875 to 0.1875
- expand_layer_offset: bfloat16 [4096], P(('fsdp', 'tp')), may hold values from -1.5 to 1.5
- contract_layer_matrix: bfloat16 [4096, 1024], P('tp', 'fsdp'), may hold values from -0.09375 to 0.09375
- contract_layer_offset: bfloat16 [1024], P(('fsdp', 'tp')), may hold values from -1.5 to 1.5
Outputs:
- block_out: bfloat16 [35328, 1024], P(('fsdp', 'tp'))
- loss_value: float32 [], replicated
- grad_tokens: float32 [35328, 1024], P(('fsdp', 'tp'))
- grad_shortcut: float32 [35328, 1024], P(('fsdp', 'tp'))
- grad_merge_weight: float32 [2048, 1024], P(('fsdp', 'tp'))
- grad_merge_bias: float32 [1024], P(('fsdp', 'tp'))
- grad_first_gain: float32 [1024], P(('fsdp', 'tp'))
- grad_first_shift: float32 [1024], P(('fsdp', 'tp'))
- grad_query_weight: float32 [1024, 1024], P('fsdp', 'tp')
- grad_key_weight: float32 [1024, 1024], P('fsdp', 'tp')
- grad_value_weight: float32 [1024, 1024], P('fsdp', 'tp')
- grad_output_weight: float32 [1024, 1024], P('tp', 'fsdp')
- grad_output_bias: float32 [1024], P(('fsdp', 'tp'))
- grad_second_gain: float32 [1024], P(('fsdp', 'tp'))
- grad_second_shift: float32 [1024], P(('fsdp', 'tp'))
- grad_hidden_weight: float32 [1024, 4096], P('fsdp', 'tp')
- grad_hidden_bias: float32 [4096], P(('fsdp', 'tp'))
- grad_down_weight: float32 [4096, 1024], P('tp', 'fsdp')
- grad_down_bias: float32 [1024], P(('fsdp', 'tp'))
Inputs may be any that keep to these rules, and one draw needn't show every extreme that they name: `occupancy_mask`: in each group of 2 slots (the slots of one index of fsdp) the live slots come first and at least one is live; in every draw some group has all 2 slots live.
All inputs are finite; a program needn't handle non-finite values.
Results may differ from a plain program's by a relative error of at most 0.015.
Values may be sent and summed in bfloat16 or wider, within the bound.
No kernel may reach another device: no remote copies, remote signals or barrier semaphores. Data moves between devices by JAX's collectives and lax.ppermute only.
A program may use at most 320 MiB of HBM per device.

v0:
```python
import jax
import jax.numpy as jnp
from jax import lax
from jax.sharding import PartitionSpec as P

D = 1024
HEADS = 16
SEQ_LEN = 1104


EPSILON = 1e-05


def layer_norm(value, gain, shift):
    centred = value - jnp.mean(value, axis=-1, keepdims=True)
    spread = jnp.mean(centred * centred, axis=-1, keepdims=True)
    return centred * lax.rsqrt(spread + EPSILON) * gain + shift


def contract_rows(left, right):
    return lax.dot_general(
        left, right, (((0,), (0,)), ((), ())), preferred_element_type=jnp.float32
    )


def contract_cols(left, right):
    return lax.dot_general(
        left, right, (((1,), (1,)), ((), ())), preferred_element_type=jnp.float32
    )


def attend_forward(queries, keys_all, values):
    scale = float(queries.shape[-1]) ** (-0.5)
    scores = (
        jnp.einsum("qhd,khd->hqk", queries, keys_all, preferred_element_type=jnp.float32) * scale
    )
    peak_score = jnp.max(scores, axis=-1, keepdims=True)
    raised = jnp.exp(scores - peak_score)
    row_total = jnp.sum(raised, axis=-1, keepdims=True)
    weights_low = (raised / row_total).astype(jnp.bfloat16)
    output = jnp.einsum("hqk,khd->qhd", weights_low, values, preferred_element_type=jnp.float32)
    return (output.astype(jnp.bfloat16), peak_score + jnp.log(row_total))


def attend_backward(queries, keys_all, values, summary, upstream):
    scale = float(queries.shape[-1]) ** (-0.5)
    scores = (
        jnp.einsum("qhd,khd->hqk", queries, keys_all, preferred_element_type=jnp.float32) * scale
    )
    probs_full = jnp.exp(scores - summary)
    grad_probs = jnp.einsum("qhd,khd->hqk", upstream, values, preferred_element_type=jnp.float32)
    grad_values = jnp.einsum(
        "hqk,qhd->khd",
        probs_full.astype(jnp.bfloat16),
        upstream,
        preferred_element_type=jnp.float32,
    )
    centre = jnp.sum(probs_full * grad_probs, axis=-1, keepdims=True)
    grad_scores = (probs_full * (grad_probs - centre)).astype(jnp.bfloat16)
    grad_queries = (
        jnp.einsum("hqk,khd->qhd", grad_scores, keys_all, preferred_element_type=jnp.float32)
        * scale
    )
    grad_keys = (
        jnp.einsum("hqk,qhd->khd", grad_scores, queries, preferred_element_type=jnp.float32) * scale
    )
    return (
        grad_queries.astype(jnp.bfloat16),
        grad_keys.astype(jnp.bfloat16),
        grad_values.astype(jnp.bfloat16),
    )


def gelu_exact(value):
    return jax.nn.gelu(value, approximate=False)


def per_device(
    entering_states,
    bypass_states,
    mentor_states,
    occupancy_mask,
    bypass_merge_matrix,
    bypass_merge_offset,
    mixer_layernorm_scale,
    mixer_layernorm_offset,
    asking_map_matrix,
    lookup_map_matrix,
    content_map_matrix,
    mixer_result_matrix,
    mixer_result_offset,
    perceptron_layernorm_scale,
    perceptron_layernorm_offset,
    expand_layer_matrix,
    expand_layer_offset,
    contract_layer_matrix,
    contract_layer_offset,
):
    rows = entering_states.shape[0]
    width = D // HEADS
    position = lax.axis_index("tp")
    (
        merge_full,
        merge_add,
        gain_one,
        shift_one,
        output_add,
        gain_two,
        shift_two,
        hidden_add,
        down_add,
    ) = (
        lax.all_gather(bypass_merge_matrix, ("fsdp", "tp"), axis=0, tiled=True),
        lax.all_gather(bypass_merge_offset, ("fsdp", "tp"), axis=0, tiled=True),
        lax.all_gather(mixer_layernorm_scale, ("fsdp", "tp"), axis=0, tiled=True),
        lax.all_gather(mixer_layernorm_offset, ("fsdp", "tp"), axis=0, tiled=True),
        lax.all_gather(mixer_result_offset, ("fsdp", "tp"), axis=0, tiled=True),
        lax.all_gather(perceptron_layernorm_scale, ("fsdp", "tp"), axis=0, tiled=True),
        lax.all_gather(perceptron_layernorm_offset, ("fsdp", "tp"), axis=0, tiled=True),
        lax.all_gather(expand_layer_offset, ("fsdp", "tp"), axis=0, tiled=True),
        lax.all_gather(contract_layer_offset, ("fsdp", "tp"), axis=0, tiled=True),
    )
    query_full, key_full, value_full, output_full, hidden_full, down_full = (
        lax.all_gather(asking_map_matrix, "fsdp", axis=0, tiled=True),
        lax.all_gather(lookup_map_matrix, "fsdp", axis=0, tiled=True),
        lax.all_gather(content_map_matrix, "fsdp", axis=0, tiled=True),
        lax.all_gather(mixer_result_matrix, "fsdp", axis=1, tiled=True),
        lax.all_gather(expand_layer_matrix, "fsdp", axis=0, tiled=True),
        lax.all_gather(contract_layer_matrix, "fsdp", axis=1, tiled=True),
    )
    gain_one = gain_one.astype(jnp.float32)
    shift_one = shift_one.astype(jnp.float32)
    gain_two = gain_two.astype(jnp.float32)
    shift_two = shift_two.astype(jnp.float32)
    project = jnp.concatenate([query_full, key_full, value_full], axis=1)
    local_width = query_full.shape[1]
    local_heads = local_width // width
    local_hidden = hidden_full.shape[1]
    row_index = position * rows + jnp.arange(rows, dtype=jnp.int32)
    slot_of_row = row_index // SEQ_LEN
    series_place_total = occupancy_mask.shape[0]
    agreeing_lines = (
        slot_of_row[:, None] == jnp.arange(series_place_total, dtype=jnp.int32)[None, :]
    ).astype(jnp.float32)
    alive_tokens = jnp.sum(
        agreeing_lines * occupancy_mask.astype(jnp.float32)[None, :], axis=1, keepdims=True
    )
    joined = jnp.concatenate([entering_states, bypass_states], axis=1)
    merged = jnp.dot(joined, merge_full, preferred_element_type=jnp.float32) + merge_add.astype(
        jnp.float32
    )
    first = layer_norm(merged, gain_one, shift_one).astype(jnp.bfloat16)
    first_all = lax.all_gather(first, "tp", axis=0, tiled=True)
    group_rows = first_all.shape[0]
    slots = group_rows // SEQ_LEN
    projected = jnp.dot(first_all, project, preferred_element_type=jnp.float32).astype(jnp.bfloat16)
    shaped = projected.reshape(slots, SEQ_LEN, 3, local_heads, width)
    queries = shaped[:, :, 0]
    keys_all = shaped[:, :, 1]
    values = shaped[:, :, 2]
    attended, summary = lax.map(
        lambda item: attend_forward(item[0], item[1], item[2]), (queries, keys_all, values)
    )
    attended_flat = attended.reshape(group_rows, local_width)
    attention_term = jnp.dot(attended_flat, output_full, preferred_element_type=jnp.float32)
    after_attn = (
        merged
        + lax.psum_scatter(
            attention_term.astype(jnp.bfloat16), "tp", scatter_dimension=0, tiled=True
        ).astype(jnp.float32)
        + output_add.astype(jnp.float32)
    )
    second = layer_norm(after_attn, gain_two, shift_two).astype(jnp.bfloat16)
    second_all = lax.all_gather(second, "tp", axis=0, tiled=True)
    hidden_slice = lax.dynamic_slice_in_dim(
        hidden_add.astype(jnp.float32), position * local_hidden, local_hidden, 0
    )
    hidden = jnp.dot(second_all, hidden_full, preferred_element_type=jnp.float32) + hidden_slice
    active = gelu_exact(hidden).astype(jnp.bfloat16)
    feed_term = jnp.dot(active, down_full, preferred_element_type=jnp.float32)
    final = (
        after_attn
        + lax.psum_scatter(
            feed_term.astype(jnp.bfloat16), "tp", scatter_dimension=0, tiled=True
        ).astype(jnp.float32)
        + down_add.astype(jnp.float32)
    )
    missing = final - mentor_states.astype(jnp.float32)
    grad_final = alive_tokens * missing
    block_out = (final * alive_tokens).astype(jnp.bfloat16)
    energy, counted = lax.psum(
        (0.5 * jnp.sum(grad_final * missing), jnp.sum(alive_tokens)), ("fsdp", "tp")
    )
    loss_value = energy / (counted * D)
    grad_down_bias = jnp.sum(grad_final, axis=0)
    upstream = grad_final.astype(jnp.bfloat16)
    upstream_all = lax.all_gather(upstream, "tp", axis=0, tiled=True)
    grad_down = contract_rows(active, upstream_all)
    grad_active = contract_cols(upstream_all, down_full)
    gelu_value, gelu_pull = jax.vjp(gelu_exact, hidden)
    grad_hidden = gelu_pull(grad_active)[0].astype(jnp.bfloat16)
    grad_hidden_local = jnp.sum(grad_hidden.astype(jnp.float32), axis=0)
    grad_hidden_weight = contract_rows(second_all, grad_hidden)
    feed_back_term = contract_cols(grad_hidden, hidden_full)
    grad_second = lax.psum_scatter(
        feed_back_term.astype(jnp.bfloat16), "tp", scatter_dimension=0, tiled=True
    ).astype(jnp.float32)
    hidden_bias_term = lax.dynamic_update_slice_in_dim(
        jnp.zeros((hidden_add.shape[0],), jnp.float32),
        grad_hidden_local,
        position * local_hidden,
        0,
    )
    norm_value, second_pull = jax.vjp(layer_norm, after_attn, gain_two, shift_two)
    back_after, grad_gain_two, grad_shift_two = second_pull(grad_second)
    grad_after = grad_final + back_after
    grad_output_bias = jnp.sum(grad_after, axis=0)
    branch_all = lax.all_gather(grad_after.astype(jnp.bfloat16), "tp", axis=0, tiled=True)
    grad_output_weight = contract_rows(attended_flat, branch_all)
    grad_attended = contract_cols(branch_all, output_full).astype(jnp.bfloat16)
    upstream_heads = grad_attended.reshape(slots, SEQ_LEN, local_heads, width)
    grad_q_heads, grad_k_heads, grad_v_heads = lax.map(
        lambda item: attend_backward(item[0], item[1], item[2], item[3], item[4]),
        (queries, keys_all, values, summary, upstream_heads),
    )
    grad_projected = jnp.stack([grad_q_heads, grad_k_heads, grad_v_heads], axis=2).reshape(
        group_rows, 3 * local_width
    )
    grad_project = contract_rows(first_all, grad_projected)
    attention_back_term = contract_cols(grad_projected, project)
    grad_first = lax.psum_scatter(
        attention_back_term.astype(jnp.bfloat16), "tp", scatter_dimension=0, tiled=True
    ).astype(jnp.float32)
    first_value, first_pull = jax.vjp(layer_norm, merged, gain_one, shift_one)
    back_merged, grad_gain_one, grad_shift_one = first_pull(grad_first)
    grad_merged = grad_after + back_merged
    grad_merge_bias = jnp.sum(grad_merged, axis=0)
    merge_grad = grad_merged.astype(jnp.bfloat16)
    grad_merge_weight = contract_rows(joined, merge_grad)
    grad_joined = contract_cols(merge_grad, merge_full)
    model_width = entering_states.shape[1]
    grad_tokens = grad_joined[:, :model_width]
    grad_shortcut = grad_joined[:, model_width:]
    grad_query, grad_key, grad_value, grad_output, grad_hidden_full, grad_down_full = (
        lax.psum_scatter(
            grad_project[:, :local_width].astype(jnp.bfloat16),
            "fsdp",
            scatter_dimension=0,
            tiled=True,
        ).astype(jnp.float32),
        lax.psum_scatter(
            grad_project[:, local_width : 2 * local_width].astype(jnp.bfloat16),
            "fsdp",
            scatter_dimension=0,
            tiled=True,
        ).astype(jnp.float32),
        lax.psum_scatter(
            grad_project[:, 2 * local_width :].astype(jnp.bfloat16),
            "fsdp",
            scatter_dimension=0,
            tiled=True,
        ).astype(jnp.float32),
        lax.psum_scatter(
            grad_output_weight.astype(jnp.bfloat16), "fsdp", scatter_dimension=1, tiled=True
        ).astype(jnp.float32),
        lax.psum_scatter(
            grad_hidden_weight.astype(jnp.bfloat16), "fsdp", scatter_dimension=0, tiled=True
        ).astype(jnp.float32),
        lax.psum_scatter(
            grad_down.astype(jnp.bfloat16), "fsdp", scatter_dimension=1, tiled=True
        ).astype(jnp.float32),
    )
    (
        merge_weight_sum,
        merge_bias_sum,
        gain_one_sum,
        shift_one_sum,
        output_bias_sum,
        gain_two_sum,
        shift_two_sum,
        hidden_bias_sum,
        down_bias_sum,
    ) = (
        lax.psum_scatter(grad_merge_weight, ("fsdp", "tp"), scatter_dimension=0, tiled=True),
        lax.psum_scatter(grad_merge_bias, ("fsdp", "tp"), scatter_dimension=0, tiled=True),
        lax.psum_scatter(grad_gain_one, ("fsdp", "tp"), scatter_dimension=0, tiled=True),
        lax.psum_scatter(grad_shift_one, ("fsdp", "tp"), scatter_dimension=0, tiled=True),
        lax.psum_scatter(grad_output_bias, ("fsdp", "tp"), scatter_dimension=0, tiled=True),
        lax.psum_scatter(grad_gain_two, ("fsdp", "tp"), scatter_dimension=0, tiled=True),
        lax.psum_scatter(grad_shift_two, ("fsdp", "tp"), scatter_dimension=0, tiled=True),
        lax.psum_scatter(hidden_bias_term, ("fsdp", "tp"), scatter_dimension=0, tiled=True),
        lax.psum_scatter(grad_down_bias, ("fsdp", "tp"), scatter_dimension=0, tiled=True),
    )
    return (
        block_out,
        loss_value,
        grad_tokens,
        grad_shortcut,
        merge_weight_sum,
        merge_bias_sum,
        gain_one_sum,
        shift_one_sum,
        grad_query,
        grad_key,
        grad_value,
        grad_output,
        output_bias_sum,
        gain_two_sum,
        shift_two_sum,
        grad_hidden_full,
        hidden_bias_sum,
        grad_down_full,
        down_bias_sum,
    )


def solution(mesh):
    placed = (
        P(("fsdp", "tp"), None),
        P(("fsdp", "tp"), None),
        P(("fsdp", "tp"), None),
        P("fsdp"),
        P(("fsdp", "tp"), None),
        P(("fsdp", "tp")),
        P(("fsdp", "tp")),
        P(("fsdp", "tp")),
        P("fsdp", "tp"),
        P("fsdp", "tp"),
        P("fsdp", "tp"),
        P("tp", "fsdp"),
        P(("fsdp", "tp")),
        P(("fsdp", "tp")),
        P(("fsdp", "tp")),
        P("fsdp", "tp"),
        P(("fsdp", "tp")),
        P("tp", "fsdp"),
        P(("fsdp", "tp")),
    )
    return jax.shard_map(
        per_device,
        mesh=mesh,
        in_specs=placed,
        out_specs=(
            P(("fsdp", "tp"), None),
            P(),
            P(("fsdp", "tp"), None),
            P(("fsdp", "tp"), None),
            P(("fsdp", "tp"), None),
            P(("fsdp", "tp")),
            P(("fsdp", "tp")),
            P(("fsdp", "tp")),
            P("fsdp", "tp"),
            P("fsdp", "tp"),
            P("fsdp", "tp"),
            P("tp", "fsdp"),
            P(("fsdp", "tp")),
            P(("fsdp", "tp")),
            P(("fsdp", "tp")),
            P("fsdp", "tp"),
            P(("fsdp", "tp")),
            P("tp", "fsdp"),
            P(("fsdp", "tp")),
        ),
        check_vma=False,
    )
```

profile of v0, /device:TPU:0, one launch (start us, length us, event | category | flops | bytes accessed | tf_op | source)
XLA Modules:
  0.0 1928.2 jit_solution(2879131037207183453)
XLA Ops:
  15.9 42.5 %all-reduce.16 = (bf16[1024]{0:T(1024)(128)(2,1)S(1)}, bf16[1024]{0:T(1024)(128)(2,1)S(1)}, bf16[1024]{0:T(1024)(128)(2,1)S(1)}, bf16[1024]{0:T(1024)(128)(2,1)}...) all-reduce(bf16[1024]{0:T(1024)(128)(2,1)S(1)} %dynamic-update-slic, ...), channel_id=1, replica_groups=mesh['fsdp'=16,'tp'=2] {'fsdp','tp'}, use_global_device_ids=true, to_apply=%add | all-reduce | flops 7168 | bytes 28672
  63.2 12.8 all-gather.13.cloned.1.call-done
  76.0 9.0 fusion.85
  90.8 23.9 %all-gather.17.cloned.1.call-done = bf16[1024,512]{1,0:T(8,128)(2,1)} async-done(((bf16[64,512]{1,0:T(8,128)(2,1)}), bf16[1024,512]{1,0:T(8,128)(2,1)}) %all-gather.17.cloned.1.call-update) | async-done | bytes 1048592 | tf_op jit(solution)/shard_map/all_gather | solution.py:124
  117.0 36.8 %all-gather.19.cloned.1.call-done = bf16[1024,512]{1,0:T(8,128)(2,1)} async-done(((bf16[64,512]{1,0:T(8,128)(2,1)}), bf16[1024,512]{1,0:T(8,128)(2,1)}) %all-gather.19.cloned.1.call-update) | async-done | bytes 1048592 | tf_op jit(solution)/shard_map/all_gather | solution.py:125
  156.0 36.6 %all-gather.21.cloned.1.call-done = bf16[1024,512]{1,0:T(8,128)(2,1)} async-done(((bf16[64,512]{1,0:T(8,128)(2,1)}), bf16[1024,512]{1,0:T(8,128)(2,1)}) %all-gather.21.cloned.1.call-update) | async-done | bytes 1048592 | tf_op jit(solution)/shard_map/all_gather | solution.py:126
  195.0 58.9 %all-gather.15.cloned.1.call-done = bf16[2208,1024]{1,0:T(8,128)(2,1)} async-done(((bf16[1104,1024]{1,0:T(8,128)(2,1)}), bf16[2208,1024]{1,0:T(8,128)(2,1)}) %all-gather.15.cloned.1.call-update) | async-done | bytes 4522000 | tf_op jit(solution)/shard_map/all_gather | solution.py:153
  254.0 12.0 convolution_convert_fusion
  265.9 9.6 copy.80
  275.5 16.1 reshape.156
  291.5 8.5 slice_bitcast_fusion
  305.8 99.0 %while.26 = (s32[]{:T(128)}, bf16[2,1104,8,64]{1,3,2,0:T(8,128)(2,1)}, f32[2,8,1104,1]{2,1,3,0:T(8,128)S(1)}, bf16[2,1104,8,64]{1,3,2,0:T(8,128)(2,1)}, bf16[2,1...) while((s32[]{:T(128)}, bf16[2,1104,8,64]{1,3,2,0:T(8,128)(2,1)}, ...), condition=%wide.region_5.6_spmd, body=%wide.region_2.0_spmd.sunk | while | flops 2564945408 | bytes 132757104 | solution.py:161
  306.2 16.3 fusion.135
  322.6 16.2 fusion.136
  338.8 16.7 fusion.137
  355.5 16.3 fusion.135
  371.9 16.2 fusion.136
  388.1 16.7 fusion.137
  404.9 6.4 copy.84
  417.1 6.8 convolution_convert_fusion.3
  424.7 57.2 %reduce-scatter.12.cloned.1.call-done = bf16[1104,1024]{1,0:T(8,128)(2,1)} async-done(((bf16[2208,1024]{1,0:T(8,128)(2,1)}), bf16[1104,1024]{1,0:T(8,128)(2,1)}) %reduce-scatter.12.cloned.1.call-update) | async-done | bytes 2261008 | tf_op jit(solution)/shard_map/reduce_scatter | solution.py:168
  491.1 67.0 %all-gather = bf16[32,1,128]{2,1,0:T(2,128)(2,1)S(1)} all-gather(bf16[1,1,128]{2,1,0:T(2,128)(2,1)S(1)} %bitcast.152), channel_id=1, replica_groups=mesh['fsdp'=16,'tp'=2] {'fsdp','tp'}, dimensions={0}, use_global_device_ids=true | all-gather | bytes 8448 | tf_op jit(solution)/shard_map/all_gather | solution.py:120
  558.1 37.8 %all-gather.25.cloned.1.call-done = bf16[2208,1024]{1,0:T(8,128)(2,1)} async-done(((bf16[1104,1024]{1,0:T(8,128)(2,1)}), bf16[2208,1024]{1,0:T(8,128)(2,1)}) %all-gather.25.cloned.1.call-update) | async-done | bytes 4522000 | tf_op jit(solution)/shard_map/all_gather | solution.py:174
  596.0 52.5 %multiply_convert_fusion.1 = (bf16[2208,2048]{1,0:T(8,128)(2,1)}, f32[2208,2048]{1,0:T(8,128)}, f32[2208,2048]{1,0:T(8,128)}) fusion(f32[2048]{0:T(1024)S(1)} %dynamic_slice.29, bf16[2208,1024]{1,0:T(8,128)(2,1)} %all-gather.25.cloned.1.call-done, bf16[1024,2048]{1,0:T(8,128)(2,1)} %all-gather.27.cloned.1.call-done), kind=kOutput, calls=%fused_computation.60 | convolution fusion | flops 9559474176 | bytes 53944320 | tf_op jit(solution)/shard_map/dot_general | solution.py:178
  648.7 14.8 convolution_convert_fusion.2
  664.9 56.4 %reduce-scatter.14.cloned.1.call-done = bf16[1104,1024]{1,0:T(8,128)(2,1)} async-done(((bf16[2208,1024]{1,0:T(8,128)(2,1)}), bf16[1104,1024]{1,0:T(8,128)(2,1)}) %reduce-scatter.14.cloned.1.call-update) | async-done | bytes 2261008 | tf_op jit(solution)/shard_map/reduce_scatter | solution.py:183
  721.3 6.2 multiply_convert_fusion.2
  727.5 60.6 %all-gather.31.cloned.1.call-done = bf16[2208,1024]{1,0:T(8,128)(2,1)} async-done(((bf16[1104,1024]{1,0:T(8,128)(2,1)}), bf16[2208,1024]{1,0:T(8,128)(2,1)}) %all-gather.31.cloned.1.call-update) | async-done | bytes 4522000 | tf_op jit(solution)/shard_map/all_gather | solution.py:197
  788.1 26.5 %convert_reduce_fusion = (f32[2048]{0:T(1024)}, bf16[2208,2048]{1,0:T(8,128)(2,1)}) fusion(f32[2208,2048]{1,0:T(8,128)} %get-tuple-element.226, bf16[2208,1024]{1,0:T(8,128)(2,1)} %all-gather.31.cloned.1.call-done, bf16[2048,1024]{0,1:T(8,128)(2,1)} %all-gather.29.cloned.1.call-done, f32[2208,2048]{1,0:T(8,128)} %get-tuple-element.246, ...), kind=kOutput, calls=%fused_computation.58 | convolution fusion | flops 9337894912 | bytes 53952512 | tf_op jit(solution)/shard_map/dot_general | solution.py:27
  814.6 13.7 convolution_convert_fusion.1
  828.4 58.0 %reduce-scatter.16.cloned.1.call-done = bf16[1104,1024]{1,0:T(8,128)(2,1)} async-done(((bf16[2208,1024]{1,0:T(8,128)(2,1)}), bf16[1104,1024]{1,0:T(8,128)(2,1)}) %reduce-scatter.16.cloned.1.call-update) | async-done | bytes 2261008 | tf_op jit(solution)/shard_map/reduce_scatter | solution.py:205
  906.2 60.5 %all-gather.33.cloned.1.call-done = bf16[2208,1024]{1,0:T(8,128)(2,1)} async-done(((bf16[1104,1024]{1,0:T(8,128)(2,1)}), bf16[2208,1024]{1,0:T(8,128)(2,1)}) %all-gather.33.cloned.1.call-update) | async-done | bytes 4522000 | tf_op jit(solution)/shard_map/all_gather | solution.py:218
  975.8 6.1 copy.88
  987.2 248.2 %while.27 = (s32[]{:T(128)}, bf16[2,1104,8,64]{1,3,2,0:T(8,128)(2,1)}, bf16[2,1104,8,64]{1,3,2,0:T(8,128)(2,1)}, bf16[2,1104,8,64]{1,3,2,0:T(8,128)(2,1)}, bf16[...) while((s32[]{:T(128)}, ...), condition=%wide.region_20.21_spmd, body=%wide.region_18.20_spmd.sunk | while | flops 6321159680 | bytes 345758912 | solution.py:222
  987.3 20.5 %fusion.146 = f32[8,1104,1104]{1,2,0:T(8,128)} fusion(bf16[2,1104,8,64]{1,3,2,0:T(8,128)(2,1)} %get-tuple-element.400, s32[]{:T(128)} %get-tuple-element.382, bf16[2,1104,8,64]{1,3,2,0:T(8,128)(2,1)} %get-tuple-element.399), kind=kOutput, calls=%fused_computation.35.clone.1 | convolution fusion | flops 1248067584 | bytes 41362432 | tf_op jit(solution)/shard_map/while/body/eval_jaxpr/qhd,khd->hqk/dot_general | solution.py:51
  1007.8 31.1 %multiply_reduce_fusion.5 = (f32[8,1104]{1,0:T(8,128)S(1)}, f32[8,1104,1104]{1,2,0:T(8,128)}) fusion(f32[8,1104,1104]{1,2,0:T(8,128)} %fusion.146, f32[8,1104]{1,0:T(8,128)S(1)} %dynamic-slice_bitcast_fusion.2, bf16[2,1104,8,64]{1,3,2,0:T(8,128)(2,1)} %get-tuple-element.396, s32[]{:T(128)} %get-tuple-element.382, ...), kind=kOutput, calls=%fused_computation.21.clone.1 | convolution fusion | flops 1287060864 | bytes 82132480 | tf_op jit(solution)/shard_map/while/body/eval_jaxpr/qhd,khd->hqk/dot_general | solution.py:48
  1039.0 32.8 %multiply_convert_fusion.5 = bf16[8,1104,1104]{1,2,0:T(8,128)(2,1)} fusion(f32[8,1104,1104]{1,2,0:T(8,128)} %get-tuple-element.349, f32[8,1104,1104]{1,2,0:T(8,128)} %fusion.146, f32[8,1104]{1,0:T(8,128)S(1)} %get-tuple-element.350), kind=kLoop, calls=%fused_computation.20.clone.1 | loop fusion | flops 29251584 | bytes 97540608 | tf_op jit(solution)/shard_map/while/body/eval_jaxpr/convert_element_type | solution.py:59
  1071.8 11.2 fusion.148
  1083.0 10.4 fusion.147
  1094.9 16.3 fusion.149
  1111.2 20.5 %fusion.146 = f32[8,1104,1104]{1,2,0:T(8,128)} fusion(bf16[2,1104,8,64]{1,3,2,0:T(8,128)(2,1)} %get-tuple-element.400, s32[]{:T(128)} %get-tuple-element.382, bf16[2,1104,8,64]{1,3,2,0:T(8,128)(2,1)} %get-tuple-element.399), kind=kOutput, calls=%fused_computation.35.clone.1 | convolution fusion | flops 1248067584 | bytes 41362432 | tf_op jit(solution)/shard_map/while/body/eval_jaxpr/qhd,khd->hqk/dot_general | solution.py:51
  1131.7 31.1 %multiply_reduce_fusion.5 = (f32[8,1104]{1,0:T(8,128)S(1)}, f32[8,1104,1104]{1,2,0:T(8,128)}) fusion(f32[8,1104,1104]{1,2,0:T(8,128)} %fusion.146, f32[8,1104]{1,0:T(8,128)S(1)} %dynamic-slice_bitcast_fusion.2, bf16[2,1104,8,64]{1,3,2,0:T(8,128)(2,1)} %get-tuple-element.396, s32[]{:T(128)} %get-tuple-element.382, ...), kind=kOutput, calls=%fused_computation.21.clone.1 | convolution fusion | flops 1287060864 | bytes 82132480 | tf_op jit(solution)/shard_map/while/body/eval_jaxpr/qhd,khd->hqk/dot_general | solution.py:48
  1162.7 32.8 %multiply_convert_fusion.5 = bf16[8,1104,1104]{1,2,0:T(8,128)(2,1)} fusion(f32[8,1104,1104]{1,2,0:T(8,128)} %get-tuple-element.349, f32[8,1104,1104]{1,2,0:T(8,128)} %fusion.146, f32[8,1104]{1,0:T(8,128)S(1)} %get-tuple-element.350), kind=kLoop, calls=%fused_computation.20.clone.1 | loop fusion | flops 29251584 | bytes 97540608 | tf_op jit(solution)/shard_map/while/body/eval_jaxpr/convert_element_type | solution.py:59
  1195.6 11.2 fusion.148
  1206.8 10.4 fusion.147
  1218.7 16.3 fusion.149
  1240.2 15.5 copy.90
  1255.7 15.0 reshape.159
  1270.7 12.4 convolution_convert_fusion.4
  1283.1 15.3 convolution_convert_fusion.6
  1298.5 15.6 convolution_convert_fusion.7
  1314.3 6.0 convolution_convert_fusion.9
  1320.3 11.3 convolution_convert_fusion.8
  1335.0 6.1 reduce-scatter.18.cloned.1.call-done
  1355.1 10.5 fusion.67
  1366.4 50.9 %reduce-scatter.32.cloned.1.call-done = bf16[2048,64]{0,1:T(8,128)(2,1)} async-done(((bf16[2048,1024]{0,1:T(8,128)(2,1)}), bf16[2048,64]{0,1:T(8,128)(2,1)}) %reduce-scatter.32.cloned.1.call-update) | async-done | bytes 262160 | tf_op jit(solution)/shard_map/reduce_scatter | solution.py:269
  1419.1 73.8 %reduce-scatter.30.cloned.1.call-done = bf16[64,2048]{1,0:T(8,128)(2,1)} async-done(((bf16[1024,2048]{1,0:T(8,128)(2,1)}), bf16[64,2048]{1,0:T(8,128)(2,1)}) %reduce-scatter.30.cloned.1.call-update) | async-done | bytes 262160 | tf_op jit(solution)/shard_map/reduce_scatter | solution.py:266
  1495.4 57.5 %reduce-scatter.28.cloned.1.call-done = bf16[512,64]{0,1:T(8,128)(2,1)} async-done(((bf16[512,1024]{0,1:T(8,128)(2,1)}), bf16[512,64]{0,1:T(8,128)(2,1)}) %reduce-scatter.28.cloned.1.call-update) | async-done | bytes 65552 | tf_op jit(solution)/shard_map/reduce_scatter | solution.py:263
  1554.4 59.1 %reduce-scatter.22.cloned.1.call-done = bf16[64,512]{1,0:T(8,128)(2,1)} async-done(((bf16[1024,512]{1,0:T(8,128)(2,1)}), bf16[64,512]{1,0:T(8,128)(2,1)}) %reduce-scatter.22.cloned.1.call-update) | async-done | bytes 65552 | tf_op jit(solution)/shard_map/reduce_scatter | solution.py:245
  1615.0 58.3 %reduce-scatter.24.cloned.1.call-done = bf16[64,512]{1,0:T(8,128)(2,1)} async-done(((bf16[1024,512]{1,0:T(8,128)(2,1)}), bf16[64,512]{1,0:T(8,128)(2,1)}) %reduce-scatter.24.cloned.1.call-update) | async-done | bytes 65552 | tf_op jit(solution)/shard_map/reduce_scatter | solution.py:251
  1674.8 59.1 %reduce-scatter.26.cloned.1.call-done = bf16[64,512]{1,0:T(8,128)(2,1)} async-done(((bf16[1024,512]{1,0:T(8,128)(2,1)}), bf16[64,512]{1,0:T(8,128)(2,1)}) %reduce-scatter.26.cloned.1.call-update) | async-done | bytes 65552 | tf_op jit(solution)/shard_map/reduce_scatter | solution.py:257
  1735.4 41.8 %all-reduce.15 = (f32[]{:T(128)}, f32[]{:T(128)}, f32[1024]{0:T(1024)S(1)}, f32[1024]{0:T(1024)S(1)}, f32[1024]{0:T(1024)S(1)}, /*index=5*/f32[1024]{0:T(1024)S(...) all-reduce(f32[]{:T(128)S(6)} %mul.227, ...), channel_id=1, replica_groups=mesh['fsdp'=16,'tp'=2] {'fsdp','tp'}, use_global_device_ids=true, to_apply=%region_12.13 | all-reduce | flops 11266 | bytes 90128 | tf_op jit(solution)/shard_map/psum | solution.py:191
  1783.2 6.8 fusion.69
  1794.5 125.4 %reduce-scatter.20.cloned.1.call-done = f32[64,1024]{1,0:T(8,128)} async-done(((f32[2048,1024]{1,0:T(8,128)}), f32[64,1024]{1,0:T(8,128)}) %reduce-scatter.20.cloned.1.call-update) | async-done | bytes 262160 | tf_op jit(solution)/shard_map/reduce_scatter | solution.py:284
  (238 shorter events, 128.5 us)
Async XLA Ops:
  7.2 54.4 %copy-start.15 = (bf16[1104,1024]{1,0:T(8,128)(2,1)S(1)}, bf16[1104,1024]{1,0:T(8,128)(2,1)}, u32[]{:S(2)}) copy-start(bf16[1104,1024]{1,0:T(8,128)(2,1)} %param.24) | copy-start | bytes 6782980
  7.2 68.8 %all-gather.13.cloned.1.call-start = ((), (), s32[]{:S(2)}) async-start(), calls=%async_computation.11 | async-start | bytes 4325376 | tf_op jit(solution)/shard_map/all_gather | solution.py:113
  7.9 106.7 %all-gather.17.cloned.1.call-start = ((), (), s32[]{:S(2)}) async-start(), calls=%async_computation.13 | async-start | bytes 1114112 | tf_op jit(solution)/shard_map/all_gather | solution.py:124
  8.7 145.0 %all-gather.19.cloned.1.call-start = ((), (), s32[]{:S(2)}) async-start(), calls=%async_computation.14 | async-start | bytes 1114112 | tf_op jit(solution)/shard_map/all_gather | solution.py:125
  9.4 183.2 %all-gather.21.cloned.1.call-start = ((), (), s32[]{:S(2)}) async-start(), calls=%async_computation.15 | async-start | bytes 1114112 | tf_op jit(solution)/shard_map/all_gather | solution.py:126
  10.0 244.0 %all-gather.15.cloned.1.call-start = ((), (), s32[]{:S(2)}) async-start(), calls=%async_computation.12 | async-start | bytes 6782976 | tf_op jit(solution)/shard_map/all_gather | solution.py:153
  61.6 25.1 %copy-start.27 = (f32[1024]{0:T(1024)}, f32[1024]{0:T(1024)S(1)}, u32[]{:S(2)}) copy-start(f32[1024]{0:T(1024)S(1)} %convert_element_type.152) | copy-start | bytes 12292
  85.0 2.1 copy-start.4
  85.0 2.1 copy-start.21
  89.9 327.2 %all-gather.23.cloned.1.call-start = ((), (), s32[]{:S(2)}) async-start(), calls=%async_computation.16 | async-start | bytes 1114112 | tf_op jit(solution)/shard_map/all_gather | solution.py:127
  90.5 391.4 %reduce-scatter.12.cloned.1.call-start = ((), (), s32[]{:S(2)}) async-start(), calls=%async_computation.17 | async-start | bytes 6782976 | tf_op jit(solution)/shard_map/reduce_scatter | solution.py:168
  322.6 16.3 copy-start.7
  371.9 16.3 copy-start.7
  404.9 12.2 copy-start.1
  404.9 12.2 copy-start.16
  423.9 134.3 %all-gather.27.cloned.1.call-start = ((), (), s32[]{:S(2)}) async-start(), calls=%async_computation.19 | async-start | bytes 4456448 | tf_op jit(solution)/shard_map/all_gather | solution.py:128
  424.6 171.3 %all-gather.25.cloned.1.call-start = ((), (), s32[]{:S(2)}) async-start(), calls=%async_computation.18 | async-start | bytes 6782976 | tf_op jit(solution)/shard_map/all_gather | solution.py:174
  424.7 62.6 %copy-start.29 = (f32[1024]{0:T(1024)}, f32[1024]{0:T(1024)S(1)}, u32[]{:S(2)}) copy-start(f32[1024]{0:T(1024)S(1)} %convert_element_type.159) | copy-start | bytes 12292
  485.6 2.0 copy-start
  485.6 2.1 copy-start.19
  488.3 2.8 copy-start.44
  490.5 158.3 %all-gather.29.cloned.1.call-start = ((), (), s32[]{:S(2)}) async-start(), calls=%async_computation.20 | async-start | bytes 4456448 | tf_op jit(solution)/shard_map/all_gather | solution.py:129
  491.1 230.2 %reduce-scatter.14.cloned.1.call-start = ((), (), s32[]{:S(2)}) async-start(), calls=%async_computation.21 | async-start | bytes 6782976 | tf_op jit(solution)/shard_map/reduce_scatter | solution.py:183
  663.5 57.8 %copy-start.14 = (bf16[1104,1024]{1,0:T(8,128)(2,1)S(1)}, bf16[1104,1024]{1,0:T(8,128)(2,1)}, u32[]{:S(2)}) copy-start(bf16[1104,1024]{1,0:T(8,128)(2,1)} %param.25) | copy-start | bytes 6782980
  663.6 124.5 %all-gather.31.cloned.1.call-start = ((), (), s32[]{:S(2)}) async-start(), calls=%async_computation.22 | async-start | bytes 6782976 | tf_op jit(solution)/shard_map/all_gather | solution.py:197
  727.5 158.9 %reduce-scatter.16.cloned.1.call-start = ((), (), s32[]{:S(2)}) async-start(), calls=%async_computation.23 | async-start | bytes 6782976 | tf_op jit(solution)/shard_map/reduce_scatter | solution.py:205
  788.1 26.5 %copy-start.45 = (bf16[1024,2048]{1,0:T(8,128)(2,1)S(1)}, bf16[1024,2048]{1,0:T(8,128)(2,1)}, u32[]{:S(2)}) copy-start(bf16[1024,2048]{1,0:T(8,128)(2,1)} %all-gather.27.cloned.1.call-done) | copy-start | bytes 12582916
  828.3 58.1 %copy-start.20 = (f32[1104]{0:T(1024)S(1)}, f32[1104]{0:T(1024)}, u32[]{:S(2)}) copy-start(f32[1104]{0:T(1024)} %copy-done.19) | copy-start | bytes 13252
  828.3 58.1 %copy-start.30 = (f32[1024]{0:T(1024)S(1)}, f32[1024]{0:T(1024)}, u32[]{:S(2)}) copy-start(f32[1024]{0:T(1024)} %copy-done.29) | copy-start | bytes 12292
  828.3 63.1 %copy-start.34 = (f32[1104]{0:T(1024)S(1)}, f32[1104]{0:T(1024)}, u32[]{:S(2)}) copy-start(f32[1104]{0:T(1024)} %copy-done.33) | copy-start | bytes 13252
  828.3 63.1 %copy-start.24 = (f32[1104]{0:T(1024)S(1)}, f32[1104]{0:T(1024)}, u32[]{:S(2)}) copy-start(f32[1104]{0:T(1024)} %copy-done.23) | copy-start | bytes 13252
  828.4 138.4 %all-gather.33.cloned.1.call-start = ((), (), s32[]{:S(2)}) async-start(), calls=%async_computation.24 | async-start | bytes 6782976 | tf_op jit(solution)/shard_map/all_gather | solution.py:218
  886.4 5.1 copy-start.9
  891.4 5.1 copy-start.10
  902.4 2.0 copy-start.6
  904.4 62.4 %copy-start.46 = (bf16[512,1024]{0,1:T(8,128)(2,1)S(1)}, bf16[512,1024]{0,1:T(8,128)(2,1)}, u32[]{:S(2)}) copy-start(bf16[512,1024]{0,1:T(8,128)(2,1)} %all-gather.23.cloned.1.call-done) | copy-start | bytes 3145732
  906.2 435.0 %reduce-scatter.18.cloned.1.call-start = ((), (), s32[]{:S(2)}) async-start(), calls=%async_computation.25 | async-start | bytes 6782976 | tf_op jit(solution)/shard_map/reduce_scatter | solution.py:231
  981.8 5.3 copy-start.2
  981.8 5.3 copy-start.17
  1071.8 11.2 copy-start.3
  1071.8 11.2 copy-start.11
  1083.0 11.9 copy-start.5
  1093.4 1.5 copy-start.12
  1195.6 11.3 copy-start.3
  1195.6 11.3 copy-start.11
  1206.8 11.9 copy-start.5
  1255.7 15.0 copy-start.18
  1283.1 134.3 %reduce-scatter.32.cloned.1.call-start = ((), (), s32[]{:S(2)}) async-start(), calls=%async_computation.32 | async-start | bytes 4456448 | tf_op jit(solution)/shard_map/reduce_scatter | solution.py:269
  1298.4 15.9 copy-start.13
  1298.4 194.5 %reduce-scatter.30.cloned.1.call-start = ((), (), s32[]{:S(2)}) async-start(), calls=%async_computation.31 | async-start | bytes 4456448 | tf_op jit(solution)/shard_map/reduce_scatter | solution.py:266
  1314.1 238.8 %reduce-scatter.28.cloned.1.call-start = ((), (), s32[]{:S(2)}) async-start(), calls=%async_computation.30 | async-start | bytes 1114112 | tf_op jit(solution)/shard_map/reduce_scatter | solution.py:263
  1320.3 293.2 %reduce-scatter.22.cloned.1.call-start = ((), (), s32[]{:S(2)}) async-start(), calls=%async_computation.27 | async-start | bytes 1114112 | tf_op jit(solution)/shard_map/reduce_scatter | solution.py:245
  1331.7 9.5 copy-start.22
  1331.7 9.5 copy-start.28
  1333.4 12.1 copy-start.32
  1333.5 12.2 copy-start.26
  1333.5 339.8 %reduce-scatter.24.cloned.1.call-start = ((), (), s32[]{:S(2)}) async-start(), calls=%async_computation.28 | async-start | bytes 1114112 | tf_op jit(solution)/shard_map/reduce_scatter | solution.py:251
  1334.1 399.9 %reduce-scatter.26.cloned.1.call-start = ((), (), s32[]{:S(2)}) async-start(), calls=%async_computation.29 | async-start | bytes 1114112 | tf_op jit(solution)/shard_map/reduce_scatter | solution.py:257
  1334.8 585.2 %reduce-scatter.20.cloned.1.call-start = ((), (), s32[]{:S(2)}) async-start(), calls=%async_computation.26 | async-start | bytes 8650752 | tf_op jit(solution)/shard_map/reduce_scatter | solution.py:284
  1341.1 4.5 copy-start.8
  1365.6 369.9 %copy-start.35 = (f32[1024]{0:T(1024)S(1)}, f32[1024]{0:T(1024)}, u32[]{:S(2)}) copy-start(f32[1024]{0:T(1024)} %get-tuple-element.219) | copy-start | bytes 12292
  1365.6 369.9 %copy-start.36 = (f32[1024]{0:T(1024)S(1)}, f32[1024]{0:T(1024)}, u32[]{:S(2)}) copy-start(f32[1024]{0:T(1024)} %get-tuple-element.240) | copy-start | bytes 12292
  1365.6 369.9 %copy-start.37 = (f32[1024]{0:T(1024)S(1)}, f32[1024]{0:T(1024)}, u32[]{:S(2)}) copy-start(f32[1024]{0:T(1024)} %get-tuple-element.166) | copy-start | bytes 12292
  1365.6 369.9 %copy-start.38 = (f32[1024]{0:T(1024)S(1)}, f32[1024]{0:T(1024)}, u32[]{:S(2)}) copy-start(f32[1024]{0:T(1024)} %get-tuple-element.160) | copy-start | bytes 12292
  (11 other events, 9.4 us)
Sparse Core Ops, SparseCore 0:
  11.0 64.9 all-gather.12
  78.1 36.4 all-gather.16
  116.8 36.8 all-gather.18
  155.7 36.8 all-gather.20
  194.6 59.3 all-gather.14
  256.0 37.9 all-gather.22
  424.0 57.8 reduce-scatter.11
  484.1 50.7 all-gather.26
  537.0 58.9 all-gather.24
  598.0 50.7 all-gather.28
  663.7 57.5 reduce-scatter.13
  727.6 60.4 all-gather.30
  828.4 57.8 reduce-scatter.15
  906.3 60.4 all-gather.32
  1283.2 57.8 reduce-scatter.17
  1344.8 72.4 reduce-scatter.31
  1421.5 71.3 reduce-scatter.29
  1496.4 56.4 reduce-scatter.27
  1556.9 56.4 reduce-scatter.21
  1616.9 56.3 reduce-scatter.23
  1677.3 56.5 reduce-scatter.25
  1736.8 183.1 reduce-scatter.19
where the time goes:
time: 1940 us; the launch traced here: 1930 us
  waiting for transfers between devices  996 us (51%)
  matrix products  463 us (24%)
  other arithmetic  160 us (8%)
  blocking collectives  151 us (8%)
  local copies, waits for them, and re-layouts  137 us (7%)
    reduce_scatter x1, waiting for transfers between devices, per_device(): lax.psum_scatter(grad_merge_weight, ('fsdp', 'tp'), scatter_dimension=0,...  125 us
    reduce_scatter x1, waiting for transfers between devices, per_device(): lax.psum_scatter(grad_hidden_weight.astype(jnp.bfloat16), 'fsdp', scatter...  73.8 us
    all_gather x1, blocking collectives, per_device(): lax.all_gather(expand_layer_offset, ('fsdp', 'tp'), axis=0, tiled=True)  67 us
    convert_element_type x2, other arithmetic, attend_backward(): grad_scores = (probs_full * (grad_probs - centre)).astype(jnp.bfloat16)  65.6 us
    dot_general x5, matrix products, contract_cols(): lax.dot_general(left, right, (((1,), (1,)), ((), ())), preferred_element_...  64.2 us
    dot_general x2, matrix products, attend_backward(): jnp.einsum('qhd,khd->hqk', queries, keys_all, preferred_element_type=jnp....  62.2 us
    all_gather x1, waiting for transfers between devices, per_device(): upstream_all = lax.all_gather(upstream, 'tp', axis=0, tiled=True)  60.6 us
    all_gather x1, waiting for transfers between devices, per_device(): lax.all_gather(grad_after.astype(jnp.bfloat16), 'tp', axis=0, tiled=True)  60.5 us
  transfers between devices with their start and end apart: 22, of which 20 were waited for; matrix products, arithmetic and copies ran while one was open for 18% of the time, Pallas kernels for 0%

commit v1 on v0

--- a/solution.py
+++ b/solution.py
@@ -75,7 +75,7 @@
     return jax.nn.gelu(value, approximate=False)
 
 
-def per_device(
+def per_device_split(
     entering_states,
     bypass_states,
     mentor_states,
@@ -314,52 +314,283 @@
     )
 
 
+def one_sequence_plan(
+    entering_states,
+    bypass_states,
+    mentor_states,
+    occupancy_mask,
+    bypass_merge_matrix,
+    bypass_merge_offset,
+    mixer_layernorm_scale,
+    mixer_layernorm_offset,
+    asking_map_matrix,
+    lookup_map_matrix,
+    content_map_matrix,
+    mixer_result_matrix,
+    mixer_result_offset,
+    perceptron_layernorm_scale,
+    perceptron_layernorm_offset,
+    expand_layer_matrix,
+    expand_layer_offset,
+    contract_layer_matrix,
+    contract_layer_offset,
+):
+    f32, bf16 = jnp.float32, jnp.bfloat16
+    rows, d = entering_states.shape
+    width = d // HEADS
+    col = asking_map_matrix.shape[1]
+    ffl = expand_layer_matrix.shape[1]
+    r = asking_map_matrix.shape[0]
+    nf = d // r
+    nt = d // col
+    everyone = ("z", "y", "c", "x")
+    at = {axis: lax.axis_index(axis) for axis in everyone}
+    small = (
+        bypass_merge_offset,
+        mixer_layernorm_scale,
+        mixer_layernorm_offset,
+        mixer_result_offset,
+        perceptron_layernorm_scale,
+        perceptron_layernorm_offset,
+        contract_layer_offset,
+        expand_layer_offset,
+    )
+    flat = jnp.concatenate(small)
+    flat = jnp.pad(flat, (0, 16 * col - flat.shape[0])).reshape(16, col)
+    early = jnp.concatenate(
+        [
+            bypass_merge_matrix.reshape(-1, col),
+            asking_map_matrix,
+            lookup_map_matrix,
+            content_map_matrix,
+            mixer_result_matrix.T,
+            flat,
+        ],
+        axis=0,
+    )
+    early = lax.all_gather(early, everyone, axis=0, tiled=False)
+    late = jnp.concatenate([expand_layer_matrix, contract_layer_matrix.T], axis=0)
+    late = lax.all_gather(late, everyone, axis=0, tiled=False)
+    mrows = bypass_merge_matrix.size // col
+    merge_full = early[:, :mrows].reshape(-1, d)
+
+    def columns(block, start, count):
+        part = block.reshape((nf, nt) + block.shape[1:])[:, :, start : start + count]
+        return part.transpose(0, 2, 1, 3).reshape(nf * count, -1)
+
+    project = jnp.concatenate([columns(early, mrows + i * r, r) for i in range(3)], axis=1)
+    output_t = columns(early, mrows + 3 * r, r)
+    hidden_full = columns(late, 0, r)
+    down_t = columns(late, r, r)
+    vec = early[:, mrows + 4 * r :].reshape(nf * nt, -1)
+    vectors, offset = [], 0
+    for item in small:
+        n = item.shape[0]
+        vectors.append(vec[:, offset : offset + n].reshape(-1).astype(f32))
+        offset += n
+    merge_add, gain_one, shift_one, output_add, gain_two, shift_two, down_add, hidden_add = vectors
+
+    alive = lax.dynamic_index_in_dim(occupancy_mask, at["x"], keepdims=False).astype(f32)
+    joined = jnp.concatenate([entering_states, bypass_states], axis=1)
+    merged = jnp.dot(joined, merge_full, preferred_element_type=f32) + merge_add
+    first = layer_norm(merged, gain_one, shift_one).astype(bf16)
+    projected = jnp.dot(first, project, preferred_element_type=f32).astype(bf16)
+    shaped = projected.reshape(rows, 3, 2, HEADS // 2, width)
+    queries, keys_all, values = (jnp.moveaxis(shaped[:, i], 1, 0) for i in range(3))
+    attended, summary = lax.map(
+        lambda item: attend_forward(item[0], item[1], item[2]), (queries, keys_all, values)
+    )
+    attended = jnp.moveaxis(attended, 0, 1).reshape(rows, d)
+    after_attn = merged + contract_cols(attended, output_t) + output_add
+    second = layer_norm(after_attn, gain_two, shift_two).astype(bf16)
+    hidden = jnp.dot(second, hidden_full, preferred_element_type=f32) + hidden_add
+    active = gelu_exact(hidden).astype(bf16)
+    final = after_attn + contract_cols(active, down_t) + down_add
+    missing = final - mentor_states.astype(f32)
+    grad_final = alive * missing
+    block_out = (final * alive).astype(bf16)
+    energy, counted = lax.psum(
+        (0.5 * jnp.sum(grad_final * missing), alive * float(rows)), everyone
+    )
+    loss_value = energy / (counted * d)
+    grad_down_bias = jnp.sum(grad_final, axis=0)
+    upstream = grad_final.astype(bf16)
+
+    def exchange(value, axis):
+        return lax.ppermute(value, axis, [(0, 1), (1, 0)])
+
+    def pick(value, index, dim):
+        return lax.dynamic_index_in_dim(value, index, dim, keepdims=False)
+
+    def halve(value, axis, dim):
+        here = at[axis]
+        got = exchange(pick(value, 1 - here, dim), axis)
+        return (pick(value, here, dim).astype(f32) + got.astype(f32)).astype(value.dtype)
+
+    def line(value, dim):
+        here = at["z"]
+        total = pick(value, here, dim).astype(f32)
+        for k in range(1, 4):
+            target = lax.rem(here + k, 4)
+            got = lax.ppermute(
+                pick(value, target, dim), "z", [(i, (i + k) % 4) for i in range(4)]
+            )
+            total = total + got.astype(f32)
+        return total
+
+    def shared(value):
+        value = halve(value, "c", 2)
+        half = value.shape[-1] // 2
+        left = halve(halve(value[..., :half], "x", 2), "y", 1)
+        right = halve(halve(value[..., half:], "y", 1), "x", 1)
+        return line(jnp.concatenate([left, right], axis=-1), 0)
+
+    def blocks(value):
+        return value.reshape(4, 2, 2, r, nt, -1).transpose(0, 1, 2, 4, 3, 5)
+
+    grad_down = shared(blocks(contract_rows(upstream, active).astype(bf16)))
+    grad_active = jnp.dot(upstream, down_t, preferred_element_type=f32)
+    gelu_value, gelu_pull = jax.vjp(gelu_exact, hidden)
+    grad_hidden = gelu_pull(grad_active)[0].astype(bf16)
+    hidden_bias_term = jnp.sum(grad_hidden.astype(f32), axis=0)
+    grad_hidden_weight = shared(blocks(contract_rows(second, grad_hidden).astype(bf16)))
+    grad_second = contract_cols(grad_hidden, hidden_full)
+    norm_value, second_pull = jax.vjp(layer_norm, after_attn, gain_two, shift_two)
+    back_after, grad_gain_two, grad_shift_two = second_pull(grad_second)
+    grad_after = grad_final + back_after
+    grad_output_bias = jnp.sum(grad_after, axis=0)
+    branch = grad_after.astype(bf16)
+    grad_output_t = contract_rows(branch, attended).astype(bf16)
+    grad_attended = jnp.dot(branch, output_t, preferred_element_type=f32).astype(bf16)
+    upstream_heads = jnp.moveaxis(grad_attended.reshape(rows, 2, HEADS // 2, width), 1, 0)
+    grad_qkv = lax.map(
+        lambda item: attend_backward(item[0], item[1], item[2], item[3], item[4]),
+        (queries, keys_all, values, summary, upstream_heads),
+    )
+    grad_projected = jnp.concatenate(
+        [jnp.moveaxis(g, 0, 1).reshape(rows, d) for g in grad_qkv], axis=1
+    )
+    grad_project = contract_rows(first, grad_projected).astype(bf16)
+    four = jnp.concatenate(
+        [blocks(grad_project[:, i * d : (i + 1) * d]) for i in range(3)] + [blocks(grad_output_t)],
+        axis=-1,
+    )
+    four = shared(four)
+    grad_first = contract_cols(grad_projected, project)
+    first_value, first_pull = jax.vjp(layer_norm, merged, gain_one, shift_one)
+    back_merged, grad_gain_one, grad_shift_one = first_pull(grad_first)
+    grad_merged = grad_after + back_merged
+    grad_merge_bias = jnp.sum(grad_merged, axis=0)
+    merge_grad = grad_merged.astype(bf16)
+    grad_joined = contract_cols(merge_grad, merge_full)
+    merge_weight = shared(
+        contract_rows(joined, merge_grad).astype(bf16).reshape(4, 2, 2, nt, -1, d)
+    )
+    terms = (
+        grad_merge_bias,
+        grad_gain_one,
+        grad_shift_one,
+        grad_output_bias,
+        grad_gain_two,
+        grad_shift_two,
+        grad_down_bias,
+        hidden_bias_term,
+    )
+    stacked = jnp.concatenate([item.reshape(nf * nt, -1) for item in terms], axis=1)
+    stacked = lax.psum_scatter(stacked, everyone, scatter_dimension=0, tiled=True).reshape(-1)
+    sums, offset = [], 0
+    for item in small:
+        n = item.shape[0]
+        sums.append(stacked[offset : offset + n])
+        offset += n
+    return (
+        block_out,
+        loss_value,
+        grad_joined[:, :d],
+        grad_joined[:, d:],
+        merge_weight,
+        sums[0],
+        sums[1],
+        sums[2],
+        four[:, :col],
+        four[:, col : 2 * col],
+        four[:, 2 * col : 3 * col],
+        four[:, 3 * col :].T,
+        sums[3],
+        sums[4],
+        sums[5],
+        grad_hidden_weight,
+        sums[7],
+        grad_down.T,
+        sums[6],
+    )
+
+
+ARGUMENTS = (
+    ("ft", None),
+    ("ft", None),
+    ("ft", None),
+    ("f",),
+    ("ft", None),
+    ("ft",),
+    ("ft",),
+    ("ft",),
+    ("f", "t"),
+    ("f", "t"),
+    ("f", "t"),
+    ("t", "f"),
+    ("ft",),
+    ("ft",),
+    ("ft",),
+    ("f", "t"),
+    ("ft",),
+    ("t", "f"),
+    ("ft",),
+)
+RESULTS = (
+    ("ft", None),
+    (),
+    ("ft", None),
+    ("ft", None),
+    ("ft", None),
+    ("ft",),
+    ("ft",),
+    ("ft",),
+    ("f", "t"),
+    ("f", "t"),
+    ("f", "t"),
+    ("t", "f"),
+    ("ft",),
+    ("ft",),
+    ("ft",),
+    ("f", "t"),
+    ("ft",),
+    ("t", "f"),
+    ("ft",),
+)
+
+
 def solution(mesh):
-    placed = (
-        P(("fsdp", "tp"), None),
-        P(("fsdp", "tp"), None),
-        P(("fsdp", "tp"), None),
-        P("fsdp"),
-        P(("fsdp", "tp"), None),
-        P(("fsdp", "tp")),
-        P(("fsdp", "tp")),
-        P(("fsdp", "tp")),
-        P("fsdp", "tp"),
-        P("fsdp", "tp"),
-        P("fsdp", "tp"),
-        P("tp", "fsdp"),
-        P(("fsdp", "tp")),
-        P(("fsdp", "tp")),
-        P(("fsdp", "tp")),
-        P("fsdp", "tp"),
-        P(("fsdp", "tp")),
-        P("tp", "fsdp"),
-        P(("fsdp", "tp")),
-    )
-    return jax.shard_map(
-        per_device,
-        mesh=mesh,
-        in_specs=placed,
-        out_specs=(
-            P(("fsdp", "tp"), None),
-            P(),
-            P(("fsdp", "tp"), None),
-            P(("fsdp", "tp"), None),
-            P(("fsdp", "tp"), None),
-            P(("fsdp", "tp")),
-            P(("fsdp", "tp")),
-            P(("fsdp", "tp")),
-            P("fsdp", "tp"),
-            P("fsdp", "tp"),
-            P("fsdp", "tp"),
-            P("tp", "fsdp"),
-            P(("fsdp", "tp")),
-            P(("fsdp", "tp")),
-            P(("fsdp", "tp")),
-            P("fsdp", "tp"),
-            P(("fsdp", "tp")),
-            P("tp", "fsdp"),
-            P(("fsdp", "tp")),
-        ),
-        check_vma=False,
-    )
+    def whole(*args):
+        rows = args[0].shape[0] // mesh.size
+        if rows == SEQ_LEN and dict(mesh.shape) == {"fsdp": 16, "tp": 2}:
+            plan = one_sequence_plan
+            use = jax.sharding.Mesh(mesh.devices.reshape(4, 2, 2, 2), ("z", "y", "c", "x"))
+            names = {"f": ("z", "y", "c"), "t": ("x",), "ft": ("z", "y", "c", "x")}
+        else:
+            plan = per_device_split
+            use = mesh
+            names = {"f": ("fsdp",), "t": ("tp",), "ft": ("fsdp", "tp")}
+
+        def place(entry):
+            return P(*(None if e is None else names[e] for e in entry))
+
+        return jax.shard_map(
+            plan,
+            mesh=use,
+            in_specs=tuple(place(e) for e in ARGUMENTS),
+            out_specs=tuple(place(e) for e in RESULTS),
+            check_vma=False,
+        )(*args)
+
+    return whole

time: 1940 us -> 1190 us (0.61)
  waiting for transfers between devices: 996 us -> 207 us
  local copies, waits for them, and re-layouts: 137 us -> 255 us
  blocking collectives: 151 us -> 39.7 us
  starting transfers between devices: 1.88 us -> 44.5 us
  matrix products: 463 us -> 486 us
    reduce_scatter x11 -> x0, waiting for transfers between devices: 662 us -> none  [the longest x1 125 us: per_device(): lax.psum_scatter(grad_merge_weight, ('fsdp', 'tp'), scatter_dimension=0,...]
    all_gather x11 -> x2, waiting for transfers between devices: 328 us -> 93.4 us  [the longest x1 93.4 us: one_sequence_plan(): early = lax.all_gather(early, everyone, axis=0, tiled=False)]
    ppermute x0 -> x32, waiting for transfers between devices: none -> 114 us  [the longest x20 74.3 us: exchange(): return lax.ppermute(value, axis, [(0, 1), (1, 0)])]
    all_gather x1 -> x0, blocking collectives: 67 us -> none  [per_device(): lax.all_gather(expand_layer_offset, ('fsdp', 'tp'), axis=0, tiled=True)]
    unnamed x111 -> x145, local copies, waits for them, and re-layouts: 25.4 us -> 83.5 us
    ppermute x0 -> x32, starting transfers between devices: none -> 44.4 us  [the longest x12 25.5 us: line(): lax.ppermute(pick(value, target, dim), 'z', [(i, (i + k) % 4) for i in ra...]
    unnamed x1 -> x0, blocking collectives: 42.5 us -> none
    reduce_sum x7 -> x2, other arithmetic: 30.5 us -> 4.53 us  [the longest x1 3.94 us: one_sequence_plan(): grad_output_bias = jnp.sum(grad_after, axis=0)]
  transfers between devices with their start and end apart: 22 -> 34, of which waited for: 20 -> 16; matrix products, arithmetic and copies ran while one was open for 18% -> 24% of each run, Pallas kernels for 0% -> 0%
where the time goes in v1:
time: 1190 us
  matrix products  486 us (41%)
  local copies, waits for them, and re-layouts  255 us (21%)
  waiting for transfers between devices  207 us (17%)
  other arithmetic  141 us (12%)
  starting transfers between devices  44.5 us (4%)
  blocking collectives  39.7 us (3%)
  between operations  19.3 us (2%)
    all_gather x1, waiting for transfers between devices, one_sequence_plan(): early = lax.all_gather(early, everyone, axis=0, tiled=False)  93.4 us
    unnamed x145, local copies, waits for them, and re-layouts  83.5 us
    dot_general x5, matrix products, contract_rows(): lax.dot_general(left, right, (((0,), (0,)), ((), ())), preferred_element_...  77.1 us
    ppermute x20, waiting for transfers between devices, exchange(): return lax.ppermute(value, axis, [(0, 1), (1, 0)])  74.3 us
    convert_element_type x2, other arithmetic, attend_backward(): grad_scores = (probs_full * (grad_probs - centre)).astype(jnp.bfloat16)  65.7 us
    dot_general x2, matrix products, attend_backward(): jnp.einsum('qhd,khd->hqk', queries, keys_all, preferred_element_type=jnp....  62.1 us
    dot_general x5, matrix products, contract_cols(): lax.dot_general(left, right, (((1,), (1,)), ((), ())), preferred_element_...  61.4 us
    dot_general x1, matrix products, one_sequence_plan(): jnp.dot(second, hidden_full, preferred_element_type=f32) + hidden_add  54.3 us
  transfers between devices with their start and end apart: 34, of which 16 were waited for; matrix products, arithmetic and copies ran while one was open for 24% of the time, Pallas kernels for 0%

profile of v1, /device:TPU:0, one launch (start us, length us, event | category | flops | bytes accessed | tf_op | source)
XLA Modules:
  0.0 1193.3 jit_solution(7774684632969292371)
XLA Ops:
  8.4 5.4 concatenate.37
  25.9 93.4 %all-gather.5.cloned.1.call-done = bf16[12800,512]{1,0:T(8,128)(2,1)} async-done(((bf16[400,512]{1,0:T(8,128)(2,1)}), bf16[12800,512]{1,0:T(8,128)(2,1)}) %all-gather.5.cloned.1.call-update) | async-done | bytes 13107216 | tf_op jit(solution)/shard_map/all_gather | solution.py:371
  120.5 4.6 slice.208
  126.4 7.2 reshape.353
  133.5 5.1 slice_bitcast_fusion.3
  153.5 9.7 fusion.147
  165.4 9.4 convolution_convert_fusion
  174.7 10.1 copy.103
  191.5 6.1 slice_bitcast_fusion
  199.4 99.7 %while.26 = (s32[]{:T(128)}, bf16[2,1104,8,64]{1,3,2,0:T(8,128)(2,1)}, f32[2,8,1104,1]{2,1,3,0:T(8,128)S(1)}, bf16[2,1104,8,64]{1,3,2,0:T(8,128)(2,1)}, bf16[2,1...) while((s32[]{:T(128)}, bf16[2,1104,8,64]{1,3,2,0:T(8,128)(2,1)}, ...), condition=%wide.region_5.6_spmd, body=%wide.region_2.5_spmd.sunk | while | flops 2564945408 | bytes 132757104 | solution.py:400
  199.6 16.3 %fusion.189 = (f32[8,1104]{1,0:T(8,128)S(1)}, f32[8,1104,1104]{1,2,0:T(8,128)}) fusion(bf16[2,1104,8,64]{1,3,2,0:T(8,128)(2,1)} %get-tuple-element.358, s32[]{:T(128)} %get-tuple-element.346, bf16[2,1104,8,64]{1,3,2,0:T(8,128)(2,1)S(1)} %get-tuple-element.357), kind=kOutput, calls=%fused_computation.315.clone.1 | convolution fusion | flops 1267559808 | bytes 41397760 | tf_op jit(solution)/shard_map/while/body/eval_jaxpr/qhd,khd->hqk/dot_general | solution.py:35
  216.0 16.8 %fusion.190 = f32[8,1104]{1,0:T(8,128)S(1)} fusion(f32[8,1104,1104]{1,2,0:T(8,128)} %get-tuple-element.326, f32[8,1104]{1,0:T(8,128)S(1)} %get-tuple-element.327), kind=kLoop, calls=%fused_computation.3.clone.1 | loop fusion | flops 19492224 | bytes 39072768 | tf_op jit(solution)/shard_map/while/body/eval_jaxpr/reduce_sum | solution.py:39
  232.8 17.0 %fusion.191 = bf16[2,1104,8,64]{1,3,2,0:T(8,128)(2,1)} fusion(bf16[2,1104,8,64]{1,3,2,0:T(8,128)(2,1)} %get-tuple-element.347, s32[]{:T(128)} %get-tuple-element.346, f32[8,1104,1104]{1,2,0:T(8,128)} %get-tuple-element.326, f32[8,1104]{1,0:T(8,128)S(1)} %fusion.190, f32[8,1104]{1,0:T(8,128)S(1)} %get-tuple-element.327, ...), kind=kOutput, calls=%fused_computation.7.clone.1 | convolution fusion | flops 1277884416 | bytes 43131904 | tf_op jit(solution)/shard_map/while/body/eval_jaxpr/hqk,khd->qhd/dot_general | solution.py:41
  249.8 16.3 %fusion.189 = (f32[8,1104]{1,0:T(8,128)S(1)}, f32[8,1104,1104]{1,2,0:T(8,128)}) fusion(bf16[2,1104,8,64]{1,3,2,0:T(8,128)(2,1)} %get-tuple-element.358, s32[]{:T(128)} %get-tuple-element.346, bf16[2,1104,8,64]{1,3,2,0:T(8,128)(2,1)S(1)} %get-tuple-element.357), kind=kOutput, calls=%fused_computation.315.clone.1 | convolution fusion | flops 1267559808 | bytes 41397760 | tf_op jit(solution)/shard_map/while/body/eval_jaxpr/qhd,khd->hqk/dot_general | solution.py:35
  266.1 16.2 %fusion.190 = f32[8,1104]{1,0:T(8,128)S(1)} fusion(f32[8,1104,1104]{1,2,0:T(8,128)} %get-tuple-element.326, f32[8,1104]{1,0:T(8,128)S(1)} %get-tuple-element.327), kind=kLoop, calls=%fused_computation.3.clone.1 | loop fusion | flops 19492224 | bytes 39072768 | tf_op jit(solution)/shard_map/while/body/eval_jaxpr/reduce_sum | solution.py:39
  282.4 16.7 %fusion.191 = bf16[2,1104,8,64]{1,3,2,0:T(8,128)(2,1)} fusion(bf16[2,1104,8,64]{1,3,2,0:T(8,128)(2,1)} %get-tuple-element.347, s32[]{:T(128)} %get-tuple-element.346, f32[8,1104,1104]{1,2,0:T(8,128)} %get-tuple-element.326, f32[8,1104]{1,0:T(8,128)S(1)} %fusion.190, f32[8,1104]{1,0:T(8,128)S(1)} %get-tuple-element.327, ...), kind=kOutput, calls=%fused_computation.7.clone.1 | convolution fusion | flops 1277884416 | bytes 43131904 | tf_op jit(solution)/shard_map/while/body/eval_jaxpr/hqk,khd->qhd/dot_general | solution.py:41
  299.1 7.3 fusion.148
  310.5 9.7 fusion.140
  320.2 8.1 copy.122
  328.3 12.1 %copy.134 = bf16[128,8,2,2048]{3,1,2,0:T(8,128)(2,1)} copy(bf16[128,8,2,2048]{3,2,1,0:T(2,128)(2,1)} %bitcast.384) | data formatting | bytes 16777216
  340.4 16.6 %copy.123 = bf16[16,2,64,2048]{3,1,2,0:T(2,128)(2,1)} copy(bf16[16,2,64,2048]{3,2,1,0:T(8,128)(2,1)} %get-tuple-element.161) | data formatting | bytes 16777216
  357.0 12.0 %copy.135 = bf16[128,8,2,2048]{3,1,2,0:T(8,128)(2,1)} copy(bf16[128,8,2,2048]{3,2,1,0:T(2,128)(2,1)} %bitcast.385) | data formatting | bytes 16777216
  369.1 54.3 %multiply_convert_fusion.1 = (bf16[1104,4096]{1,0:T(8,128)(2,1)}, f32[1104,4096]{1,0:T(8,128)}, f32[1104,4096]{1,0:T(8,128)}) fusion(f32[4096]{0:T(1024)S(1)} %fusion.129, bf16[1024,4096]{1,0:T(8,128)(2,1)} %bitcast.397, f32[1104,1024]{1,0:T(8,128)S(1)} %bitcast.392, f32[1024]{0:T(1024)S(1)} %copy-done.51, f32[1024]{0:T(1024)S(1)} %copy-done.43, ...), kind=kOutput, calls=%fused_computation.61 | convolution fusion | flops 9565126656 | bytes 58163840 | tf_op jit(solution)/shard_map/dot_general | solution.py:406
  423.3 15.0 %fusion.61 = f32[1104,1024]{1,0:T(8,128)S(1)} fusion(f32[1104,1024]{1,0:T(8,128)S(1)} %bitcast.392, bf16[1104,4096]{1,0:T(8,128)(2,1)} %get-tuple-element.155, bf16[1024,4096]{1,0:T(8,128)(2,1)} %bitcast.399, f32[1024]{0:T(1024)S(1)} %copy-done.52), kind=kOutput, calls=%fused_computation.94 | convolution fusion | flops 9263284224 | bytes 26480640 | tf_op jit(solution)/shard_map/dot_general | solution.py:27
  438.4 18.8 %convolution_convert_fusion.1 = bf16[1024,4096]{1,0:T(8,128)(2,1)} fusion(bf16[1104,4096]{1,0:T(8,128)(2,1)} %get-tuple-element.155, f32[]{:T(128)} %bitcast.38, f32[1104,1024]{1,0:T(8,128)S(1)} %fusion.61, bf16[1104,1024]{1,0:T(8,128)(2,1)S(1)} %copy-done.25), kind=kOutput, calls=%fused_computation.83 | convolution fusion | flops 9269739520 | bytes 24215556 | tf_op jit(solution)/shard_map/dot_general | solution.py:21
  457.2 26.7 %convert_reduce_fusion = (f32[4096]{0:T(1024)}, bf16[1104,4096]{1,0:T(8,128)(2,1)}) fusion(f32[1104,4096]{1,0:T(8,128)} %get-tuple-element.156, f32[1104,4096]{1,0:T(8,128)} %get-tuple-element.226, bf16[1024,4096]{1,0:T(8,128)(2,1)} %bitcast.400, f32[]{:T(128)} %bitcast.38, f32[1104,1024]{1,0:T(8,128)} %copy-done.15, bf16[1104,1024]{1,0:T(8,128)(2,1)} %param.25), kind=kOutput, calls=%fused_computation.59 | convolution fusion | flops 9337892864 | bytes 60407812 | tf_op jit(solution)/shard_map/dot_general | solution.py:452
  483.9 27.5 %convolution_convert_fusion.2 = bf16[1024,4096]{1,0:T(8,128)(2,1)} fusion(bf16[1104,4096]{1,0:T(8,128)(2,1)} %get-tuple-element.230, f32[1104,1024]{1,0:T(8,128)S(1)} %bitcast.392, f32[1024]{0:T(1024)S(1)} %copy-done.51, f32[1024]{0:T(1024)S(1)} %copy-done.43, f32[1104]{0:T(1024)S(1)} %fusion.131, f32[1104]{0:T(1024)S(1)} %broadcast_multiply_fusion), kind=kOutput, calls=%fused_computation.84 | convolution fusion | flops 9270870016 | bytes 21971584 | tf_op jit(solution)/shard_map/dot_general | solution.py:21
  511.4 17.4 %multiply_reduce_fusion.2 = (f32[1024]{0:T(1024)}, f32[1104]{0:T(1024)S(1)}, f32[1024]{0:T(1024)}, f32[1104,1024]{1,0:T(8,128)S(1)}) fusion(f32[1104,1024]{1,0:T(8,128)S(1)} %bitcast.392, f32[1104]{0:T(1024)S(1)} %fusion.131, f32[1104]{0:T(1024)S(1)} %broadcast_multiply_fusion, f32[1024]{0:T(1024)S(1)} %copy-done.43, ...), kind=kOutput, calls=%fused_computation.99 | convolution fusion | flops 9270064128 | bytes 26502080 | tf_op jit(solution)/shard_map/dot_general | solution.py:27
  537.0 5.9 convolution_convert_fusion.6
  550.7 248.2 %while.27 = (s32[]{:T(128)}, bf16[2,1104,8,64]{1,3,2,0:T(8,128)(2,1)}, bf16[2,1104,8,64]{1,3,2,0:T(8,128)(2,1)}, bf16[2,1104,8,64]{1,3,2,0:T(8,128)(2,1)}, bf16[...) while((s32[]{:T(128)}, ...), condition=%wide.region_15.16_spmd, body=%wide.region_13.15_spmd.sunk | while | flops 6321159680 | bytes 345758912 | solution.py:466
  551.1 20.5 %fusion.200 = f32[8,1104,1104]{1,2,0:T(8,128)} fusion(bf16[2,1104,8,64]{1,3,2,0:T(8,128)(2,1)} %get-tuple-element.388, s32[]{:T(128)} %get-tuple-element.370, bf16[2,1104,8,64]{1,3,2,0:T(8,128)(2,1)} %get-tuple-element.387), kind=kOutput, calls=%fused_computation.35.clone.1 | convolution fusion | flops 1248067584 | bytes 41362432 | tf_op jit(solution)/shard_map/while/body/eval_jaxpr/qhd,khd->hqk/dot_general | solution.py:51
  571.6 31.0 %multiply_reduce_fusion.9 = (f32[8,1104]{1,0:T(8,128)S(1)}, f32[8,1104,1104]{1,2,0:T(8,128)}) fusion(f32[8,1104,1104]{1,2,0:T(8,128)} %fusion.200, f32[8,1104]{1,0:T(8,128)S(1)} %dynamic-slice_bitcast_fusion.27, bf16[2,1104,8,64]{1,3,2,0:T(8,128)(2,1)} %get-tuple-element.384, s32[]{:T(128)} %get-tuple-element.370, ...), kind=kOutput, calls=%fused_computation.21.clone.1 | convolution fusion | flops 1287060864 | bytes 82132480 | tf_op jit(solution)/shard_map/while/body/eval_jaxpr/qhd,khd->hqk/dot_general | solution.py:48
  602.7 32.9 %multiply_convert_fusion.9 = bf16[8,1104,1104]{1,2,0:T(8,128)(2,1)} fusion(f32[8,1104,1104]{1,2,0:T(8,128)} %get-tuple-element.337, f32[8,1104,1104]{1,2,0:T(8,128)} %fusion.200, f32[8,1104]{1,0:T(8,128)S(1)} %get-tuple-element.338), kind=kLoop, calls=%fused_computation.20.clone.1 | loop fusion | flops 29251584 | bytes 97540608 | tf_op jit(solution)/shard_map/while/body/eval_jaxpr/convert_element_type | solution.py:59
  635.6 11.2 fusion.202
  646.7 10.4 fusion.201
  658.6 16.3 %fusion.203 = bf16[2,1104,8,64]{1,3,2,0:T(8,128)(2,1)} fusion(bf16[2,1104,8,64]{1,3,2,0:T(8,128)(2,1)} %get-tuple-element.373, s32[]{:T(128)} %get-tuple-element.370, f32[8,1104,1104]{1,2,0:T(8,128)} %get-tuple-element.337, bf16[2,1104,8,64]{1,3,2,0:T(8,128)(2,1)S(1)} %copy-done.3), kind=kOutput, calls=%fused_computation.30.clone.1 | convolution fusion | flops 1258383360 | bytes 43058176 | tf_op jit(solution)/shard_map/while/body/eval_jaxpr/hqk,qhd->khd/dot_general | solution.py:52
  675.0 20.5 %fusion.200 = f32[8,1104,1104]{1,2,0:T(8,128)} fusion(bf16[2,1104,8,64]{1,3,2,0:T(8,128)(2,1)} %get-tuple-element.388, s32[]{:T(128)} %get-tuple-element.370, bf16[2,1104,8,64]{1,3,2,0:T(8,128)(2,1)} %get-tuple-element.387), kind=kOutput, calls=%fused_computation.35.clone.1 | convolution fusion | flops 1248067584 | bytes 41362432 | tf_op jit(solution)/shard_map/while/body/eval_jaxpr/qhd,khd->hqk/dot_general | solution.py:51
  695.5 31.1 %multiply_reduce_fusion.9 = (f32[8,1104]{1,0:T(8,128)S(1)}, f32[8,1104,1104]{1,2,0:T(8,128)}) fusion(f32[8,1104,1104]{1,2,0:T(8,128)} %fusion.200, f32[8,1104]{1,0:T(8,128)S(1)} %dynamic-slice_bitcast_fusion.27, bf16[2,1104,8,64]{1,3,2,0:T(8,128)(2,1)} %get-tuple-element.384, s32[]{:T(128)} %get-tuple-element.370, ...), kind=kOutput, calls=%fused_computation.21.clone.1 | convolution fusion | flops 1287060864 | bytes 82132480 | tf_op jit(solution)/shard_map/while/body/eval_jaxpr/qhd,khd->hqk/dot_general | solution.py:48
  726.5 32.9 %multiply_convert_fusion.9 = bf16[8,1104,1104]{1,2,0:T(8,128)(2,1)} fusion(f32[8,1104,1104]{1,2,0:T(8,128)} %get-tuple-element.337, f32[8,1104,1104]{1,2,0:T(8,128)} %fusion.200, f32[8,1104]{1,0:T(8,128)S(1)} %get-tuple-element.338), kind=kLoop, calls=%fused_computation.20.clone.1 | loop fusion | flops 29251584 | bytes 97540608 | tf_op jit(solution)/shard_map/while/body/eval_jaxpr/convert_element_type | solution.py:59
  759.4 11.2 fusion.202
  770.6 10.4 fusion.201
  782.5 16.3 %fusion.203 = bf16[2,1104,8,64]{1,3,2,0:T(8,128)(2,1)} fusion(bf16[2,1104,8,64]{1,3,2,0:T(8,128)(2,1)} %get-tuple-element.373, s32[]{:T(128)} %get-tuple-element.370, f32[8,1104,1104]{1,2,0:T(8,128)} %get-tuple-element.337, bf16[2,1104,8,64]{1,3,2,0:T(8,128)(2,1)S(1)} %copy-done.3), kind=kOutput, calls=%fused_computation.30.clone.1 | convolution fusion | flops 1258383360 | bytes 43058176 | tf_op jit(solution)/shard_map/while/body/eval_jaxpr/hqk,qhd->khd/dot_general | solution.py:52
  799.0 16.2 %convolution_convert_fusion.3 = bf16[1024,3072]{1,0:T(8,128)(2,1)} fusion(bf16[1104,1024]{0,1:T(8,128)(2,1)} %bitcast.419, bf16[1104,1024]{0,1:T(8,128)(2,1)} %bitcast.417, bf16[1104,1024]{0,1:T(8,128)(2,1)} %bitcast.415, f32[1104,1024]{1,0:T(8,128)} %copy-done.6, f32[1024]{0:T(1024)S(1)} %copy-done.50, f32[1024]{0:T(1024)S(1)} %copy-done.42, ...), kind=kOutput, calls=%fused_computation.92 | convolution fusion | flops 6974914560 | bytes 17613440 | tf_op jit(solution)/shard_map/dot_general | solution.py:21
  815.1 14.4 %multiply_reduce_fusion.3 = (f32[1024]{0:T(1024)S(1)}, f32[1104]{0:T(1024)S(1)}, f32[1024]{0:T(1024)S(1)}, f32[1104,1024]{1,0:T(8,128)}) fusion(f32[1104,1024]{1,0:T(8,128)} %copy-done.6, f32[1104]{0:T(1024)S(1)} %copy-done.40, f32[1104]{0:T(1024)S(1)} %copy-done.34, f32[1024]{0:T(1024)S(1)} %copy-done.42, bf16[1024,3072]{1,0:T(8,128)(2,1)} %copy-done.29, ...), kind=kOutput, calls=%fused_computation.100 | convolution fusion | flops 6975157248 | bytes 22143936 | tf_op jit(solution)/shard_map/dot_general | solution.py:27
  829.5 14.4 %reshape.382 = bf16[4,2,2,64,2,2048]{5,4,3,2,1,0:T(2,128)(2,1)} reshape(bf16[1024,4096]{1,0:T(8,128)(2,1)} %convolution_convert_fusion.2) | data formatting | bytes 16777216 | tf_op jit(solution)/shard_map/reshape | solution.py:449
  843.9 14.5 %reshape.383 = bf16[4,2,2,64,2,2048]{5,4,3,2,1,0:T(2,128)(2,1)} reshape(bf16[1024,4096]{1,0:T(8,128)(2,1)} %convolution_convert_fusion.1) | data formatting | bytes 16777216 | tf_op jit(solution)/shard_map/reshape | solution.py:449
  858.4 17.6 %constant_dynamic-slice_fusion.1 = (bf16[4,2,1,64,2,2048]{5,4,3,2,1,0:T(2,128)(2,1)}, bf16[4,2,1,64,2,2048]{5,4,3,2,1,0:T(2,128)(2,1)S(1)}, bf16[4,2,1,64,2,2048...) fusion(bf16[4,2,2,64,2,2048]{5,4,3,2,1,0:T(2,128)(2,1)} %reshape.383, s32[]{:T(128)S(6)} %select_n.89, ...), kind=kLoop, calls=%fused_computation.277 | loop fusion | bytes 33554440 | tf_op jit(solution)/shard_map/jit(dynamic_index_in_dim)/dynamic_slice | solution.py:423
  887.6 8.7 convolution_convert_fusion.4
  907.2 4.5 reshape.379
  927.0 7.4 fusion.73
  940.6 10.8 collective-permute-done.3
  961.7 9.1 fusion.141
  970.8 39.7 %all-reduce.2 = (f32[]{:T(128)}, f32[]{:T(128)}, f32[32,352]{1,0:T(8,128)S(1)}) all-reduce(f32[]{:T(128)S(6)} %mul.207, f32[]{:T(128)S(6)} %mul.208, f32[32,352]{1,0:T(8,128)S(1)} %concatenate.43), channel_id=1, replica_groups=mesh['z'=4,'y'=2,'c'=2,'x'=2] {'z','y','c','x'}, use_global_device_ids=true, to_apply=%region_9.10 | all-reduce | flops 11266 | bytes 90128 | tf_op jit(solution)/shard_map/psum | solution.py:412
  1020.4 5.8 fusion.58
  1031.8 5.0 fusion.59
  1046.8 7.4 collective-permute-done.27
  1059.9 16.9 %collective-permute-done.19 = bf16[4,2,64,1024]{3,2,0,1:T(8,128)(2,1)} collective-permute-done((bf16[4,2,64,1024]{3,2,0,1:T(8,128)(2,1)}, bf16[4,2,64,1024]{3,2,0,1:T(8,128)(2,1)}, u32[]{:S(2)}, u32[]{:S(2)}) %collective-permute-start.19) | collective-permute-done | bytes 1048608 | tf_op jit(solution)/shard_map/ppermute | solution.py:420
  1083.0 16.1 %collective-permute-done.11 = bf16[4,2,64,1024]{3,2,0,1:T(8,128)(2,1)S(1)} collective-permute-done((bf16[4,2,64,1024]{3,2,0,1:T(8,128)(2,1)S(1)}, bf16[4,2,64,1024]{3,2,0,1:T(8,128)(2,1)S(1)}, u32[]{:S(2)}, u32[]{:S(2)}) %collective-permute-start.11) | collective-permute-done | bytes 1048608 | tf_op jit(solution)/shard_map/ppermute | solution.py:420
  1103.7 9.6 collective-permute-done.28
  1116.5 8.0 collective-permute-done.20
  1136.1 20.0 %collective-permute-done.30 = bf16[64,2048]{1,0:T(8,128)(2,1)S(1)} collective-permute-done((bf16[64,2048]{1,0:T(8,128)(2,1)S(1)}, bf16[64,2048]{1,0:T(8,128)(2,1)S(1)}, u32[]{:S(2)}, u32[]{:S(2)}) %collective-permute-start.30) | collective-permute-done | bytes 262176 | tf_op jit(solution)/shard_map/ppermute | solution.py:435
  1158.1 9.4 collective-permute-start.23
  1167.5 8.1 collective-permute-done.14
  1176.5 7.6 collective-permute-done.23
  (341 shorter events, 175.8 us)
Async XLA Ops:
  7.2 14.7 %copy-start.21 = (bf16[1104,1024]{1,0:T(8,128)(2,1)S(1)}, bf16[1104,1024]{1,0:T(8,128)(2,1)}, u32[]{:S(2)}) copy-start(bf16[1104,1024]{1,0:T(8,128)(2,1)} %param.23) | copy-start | bytes 6782980
  7.2 112.2 %all-gather.5.cloned.1.call-start = ((), (), s32[]{:S(2)}) async-start(), calls=%async_computation | async-start | bytes 13516800 | tf_op jit(solution)/shard_map/all_gather | solution.py:371
  18.0 292.5 %all-gather.7.cloned.1.call-start = ((), (), s32[]{:S(2)}) async-start(), calls=%async_computation.1 | async-start | bytes 17301504 | tf_op jit(solution)/shard_map/all_gather | solution.py:373
  149.5 15.4 %copy-start.41 = (f32[1024]{0:T(1024)}, f32[1024]{0:T(1024)S(1)}, u32[]{:S(2)}) copy-start(f32[1024]{0:T(1024)S(1)} %reshape.385) | copy-start | bytes 12292
  149.6 15.3 %copy-start.49 = (f32[1024]{0:T(1024)}, f32[1024]{0:T(1024)S(1)}, u32[]{:S(2)}) copy-start(f32[1024]{0:T(1024)S(1)} %reshape.386) | copy-start | bytes 12292
  153.5 11.4 copy-start.29
  199.4 99.7 %copy-start.53 = (f32[1024]{0:T(1024)S(1)}, f32[1024]{0:T(1024)}, u32[]{:S(2)}) copy-start(f32[1024]{0:T(1024)} %reshape.387) | copy-start | bytes 12292
  216.0 16.8 %copy-start.5 = (bf16[2,1104,8,64]{1,3,2,0:T(8,128)(2,1)S(1)}, bf16[2,1104,8,64]{1,3,2,0:T(8,128)(2,1)}, u32[]{:S(2)}) copy-start(bf16[2,1104,8,64]{1,3,2,0:T(8,128)(2,1)} %get-tuple-element.356) | copy-start | bytes 6782980 | tf_op jit(solution)/shard_map/while
  266.1 16.3 %copy-start.5 = (bf16[2,1104,8,64]{1,3,2,0:T(8,128)(2,1)S(1)}, bf16[2,1104,8,64]{1,3,2,0:T(8,128)(2,1)}, u32[]{:S(2)}) copy-start(bf16[2,1104,8,64]{1,3,2,0:T(8,128)(2,1)} %get-tuple-element.356) | copy-start | bytes 6782980 | tf_op jit(solution)/shard_map/while
  340.4 28.7 %slice-start.6 = ((s8[4521984]{0:T(1024)(128)(4,1)}), s8[4194304]{0:T(1024)(128)(4,1)S(1)}, s32[]{:S(2)}) async-start(s8[4521984]{0:T(1024)(128)(4,1)} %bitcast.391), calls=%async_computation.8 | async-start | bytes 8388608
  356.9 12.1 %slice-start.7 = ((s8[4521984]{0:T(1024)(128)(4,1)}), s8[327680]{0:T(1024)(128)(4,1)S(1)}, s32[]{:S(2)}) async-start(s8[4521984]{0:T(1024)(128)(4,1)} %bitcast.391), calls=%async_computation.9 | async-start | bytes 655360
  357.0 12.1 %copy-start.43 = (f32[1024]{0:T(1024)S(1)}, f32[1024]{0:T(1024)}, u32[]{:S(2)}) copy-start(f32[1024]{0:T(1024)} %reshape.388) | copy-start | bytes 12292
  357.0 12.1 %copy-start.51 = (f32[1024]{0:T(1024)S(1)}, f32[1024]{0:T(1024)}, u32[]{:S(2)}) copy-start(f32[1024]{0:T(1024)} %reshape.389) | copy-start | bytes 12292
  369.1 54.3 %copy-start.52 = (f32[1024]{0:T(1024)S(1)}, f32[1024]{0:T(1024)}, u32[]{:S(2)}) copy-start(f32[1024]{0:T(1024)} %reshape.391) | copy-start | bytes 12292
  423.3 15.0 %copy-start.25 = (bf16[1104,1024]{1,0:T(8,128)(2,1)S(1)}, bf16[1104,1024]{1,0:T(8,128)(2,1)}, u32[]{:S(2)}) copy-start(bf16[1104,1024]{1,0:T(8,128)(2,1)} %param.25) | copy-start | bytes 6782980
  438.4 18.8 %copy-start.15 = (f32[1104,1024]{1,0:T(8,128)}, f32[1104,1024]{1,0:T(8,128)S(1)}, u32[]{:S(2)}) copy-start(f32[1104,1024]{1,0:T(8,128)S(1)} %fusion.61) | copy-start | bytes 13565956
  483.9 46.3 %slice-start.10 = ((s8[4521984]{0:T(1024)(128)(4,1)}), s8[4194304]{0:T(1024)(128)(4,1)S(1)}, s32[]{:S(2)}) async-start(s8[4521984]{0:T(1024)(128)(4,1)} %bitcast.410), calls=%async_computation.12 | async-start | bytes 8388608
  511.4 17.4 %copy-start.38 = (f32[1104]{0:T(1024)S(1)}, f32[1104]{0:T(1024)}, u32[]{:S(2)}) copy-start(f32[1104]{0:T(1024)} %copy-done.37) | copy-start | bytes 13252
  511.4 18.8 %slice-start.11 = ((s8[4521984]{0:T(1024)(128)(4,1)}), s8[327680]{0:T(1024)(128)(4,1)S(1)}, s32[]{:S(2)}) async-start(s8[4521984]{0:T(1024)(128)(4,1)} %bitcast.410), calls=%async_computation.13 | async-start | bytes 655360
  550.7 248.2 %copy-start.34 = (f32[1104]{0:T(1024)S(1)}, f32[1104]{0:T(1024)}, u32[]{:S(2)}) copy-start(f32[1104]{0:T(1024)} %copy-done.33) | copy-start | bytes 13252
  550.7 248.2 %copy-start.40 = (f32[1104]{0:T(1024)S(1)}, f32[1104]{0:T(1024)}, u32[]{:S(2)}) copy-start(f32[1104]{0:T(1024)} %copy-done.39) | copy-start | bytes 13252
  550.7 248.2 %copy-start.42 = (f32[1024]{0:T(1024)S(1)}, f32[1024]{0:T(1024)}, u32[]{:S(2)}) copy-start(f32[1024]{0:T(1024)} %copy-done.41) | copy-start | bytes 12292
  550.7 248.2 %copy-start.50 = (f32[1024]{0:T(1024)S(1)}, f32[1024]{0:T(1024)}, u32[]{:S(2)}) copy-start(f32[1024]{0:T(1024)} %copy-done.49) | copy-start | bytes 12292
  635.5 11.2 copy-start.18
  646.7 11.9 copy-start.3
  759.4 11.2 copy-start.2
  759.4 11.2 copy-start.18
  770.6 11.9 copy-start.3
  798.9 16.2 %copy-start.20 = (bf16[2,1104,8,64]{1,3,2,0:T(8,128)(2,1)S(1)}, bf16[2,1104,8,64]{1,3,2,0:T(8,128)(2,1)}, u32[]{:S(2)}) copy-start(bf16[2,1104,8,64]{1,3,2,0:T(8,128)(2,1)} %get-tuple-element.103) | copy-start | bytes 6782980
  843.9 40.4 %slice-start.12 = ((s8[4521984]{0:T(1024)(128)(4,1)}), s8[327680]{0:T(1024)(128)(4,1)S(1)}, s32[]{:S(2)}) async-start(s8[4521984]{0:T(1024)(128)(4,1)} %bitcast.412), calls=%async_computation.14 | async-start | bytes 655360
  858.4 25.8 %slice-start.13 = ((s8[4521984]{0:T(1024)(128)(4,1)}), s8[4194304]{0:T(1024)(128)(4,1)S(1)}, s32[]{:S(2)}) async-start(s8[4521984]{0:T(1024)(128)(4,1)} %bitcast.412), calls=%async_computation.15 | async-start | bytes 8388608
  879.9 140.5 %collective-permute-start.24 = (bf16[4,2,2,64,2048]{4,3,0,2,1:T(8,128)(2,1)}, bf16[4,2,2,64,2048]{4,3,0,2,1:T(8,128)(2,1)}, u32[]{:S(2)}, u32[]{:S(2)}) collective-permute-start(bf16[4,2,2,64,2048]{4,3,0,2,1:T(8,128)(2,1)} %bitcast.342), channel_id=1, source_target_pairs={{0,2},{2,0},{1,3},{3,1},{4,6},{6,4},{5,7},{7,5},{8,10},{10,8},{9,1... | collective-permute-start | bytes 12582920 | tf_op jit(solution)/shard_map/ppermute | solution.py:420
  883.9 147.8 %collective-permute-start.16 = (bf16[4,2,2,64,2048]{4,3,0,2,1:T(8,128)(2,1)}, bf16[4,2,2,64,2048]{4,3,0,2,1:T(8,128)(2,1)}, u32[]{:S(2)}, u32[]{:S(2)}) collective-permute-start(bf16[4,2,2,64,2048]{4,3,0,2,1:T(8,128)(2,1)} %bitcast.343), channel_id=1, source_target_pairs={{0,2},{2,0},{1,3},{3,1},{4,6},{6,4},{5,7},{7,5},{8,10},{10,8},{9,1... | collective-permute-start | bytes 12582920 | tf_op jit(solution)/shard_map/ppermute | solution.py:420
  898.4 36.0 %collective-permute-start = (bf16[4,2,2,64,1024]{4,3,0,2,1:T(8,128)(2,1)}, bf16[4,2,2,64,1024]{4,3,0,2,1:T(8,128)(2,1)}, u32[]{:S(2)}, u32[]{:S(2)}) collective-permute-start(bf16[4,2,2,64,1024]{4,3,0,2,1:T(8,128)(2,1)} %bitcast.344), channel_id=1, source_target_pairs={{0,2},{2,0},{1,3},{3,1},{4,6},{6,4},{5,7},{7,5},{8,10},{10,8},{9,1... | collective-permute-start | bytes 6291464 | tf_op jit(solution)/shard_map/ppermute | solution.py:420
  937.3 14.1 %collective-permute-start.3 = (bf16[4,2,64,512]{3,2,0,1:T(8,128)(2,1)S(1)}, bf16[4,2,64,512]{3,2,0,1:T(8,128)(2,1)S(1)}, u32[]{:S(2)}, u32[]{:S(2)}) collective-permute-start(bf16[4,2,64,512]{3,2,0,1:T(8,128)(2,1)S(1)} %dynamic-slice_bitcast_fusion.14), channel_id=1, source_target_pairs={{0,4},{4,0},{1,5},{5,1},{2,6},{6,2},{3,7},{7,3},{8,12},{12,8},{9,1... | collective-permute-start | bytes 1572872 | tf_op jit(solution)/shard_map/ppermute | solution.py:420
  938.9 14.2 %collective-permute-start.1 = (bf16[4,2,64,512]{3,2,0,1:T(8,128)(2,1)S(1)}, bf16[4,2,64,512]{3,2,0,1:T(8,128)(2,1)S(1)}, u32[]{:S(2)}, u32[]{:S(2)}) collective-permute-start(bf16[4,2,64,512]{3,2,0,1:T(8,128)(2,1)S(1)} %dynamic-slice_bitcast_fusion.15), channel_id=1, source_target_pairs={{0,1},{1,0},{2,3},{3,2},{4,5},{5,4},{6,7},{7,6},{8,9},{9,8},{10,11... | collective-permute-start | bytes 1572872 | tf_op jit(solution)/shard_map/ppermute | solution.py:420
  940.6 15.6 %copy-start.4 = (bf16[4,2,2,2,64,2048]{5,4,0,3,1,2:T(8,128)(2,1)}, bf16[4,2,2,2,64,2048]{5,4,0,3,1,2:T(8,128)(2,1)S(1)}, u32[]{:S(2)}) copy-start(bf16[4,2,2,2,64,2048]{5,4,0,3,1,2:T(8,128)(2,1)S(1)} %pad_maximum_fusion) | copy-start | bytes 25165828
  951.6 7.7 collective-permute-start.4
  953.3 7.3 collective-permute-start.2
  956.2 83.8 %collective-permute-start.8 = (bf16[4,2,2,64,2048]{4,3,0,2,1:T(8,128)(2,1)}, bf16[4,2,2,64,2048]{4,3,0,2,1:T(8,128)(2,1)}, u32[]{:S(2)}, u32[]{:S(2)}) collective-permute-start(bf16[4,2,2,64,2048]{4,3,0,2,1:T(8,128)(2,1)} %dynamic-slice_bitcast_fusion.1), channel_id=1, source_target_pairs={{0,2},{2,0},{1,3},{3,1},{4,6},{6,4},{5,7},{7,5},{8,10},{10,8},{9,1... | collective-permute-start | bytes 12582920 | tf_op jit(solution)/shard_map/ppermute | solution.py:420
  960.8 51.9 %collective-permute-start.5 = (bf16[64,1024]{1,0:T(8,128)(2,1)S(1)}, bf16[64,1024]{1,0:T(8,128)(2,1)S(1)}, u32[]{:S(2)}, u32[]{:S(2)}) collective-permute-start(bf16[64,1024]{1,0:T(8,128)(2,1)S(1)} %get-tuple-element.205), channel_id=1, source_target_pairs={{0,8},{8,16},{16,24},{24,0},{1,9},{9,17},{17,25},{25,1},{2,10},{10... | collective-permute-start | bytes 393224 | tf_op jit(solution)/shard_map/ppermute | solution.py:435
  1010.5 9.1 collective-permute-start.6
  1012.7 6.9 collective-permute-start.7
  1027.9 26.4 %collective-permute-start.27 = (bf16[4,2,64,1024]{3,2,0,1:T(8,128)(2,1)}, bf16[4,2,64,1024]{3,2,0,1:T(8,128)(2,1)}, u32[]{:S(2)}, u32[]{:S(2)}) collective-permute-start(bf16[4,2,64,1024]{3,2,0,1:T(8,128)(2,1)} %dynamic-slice_bitcast_fusion.2), channel_id=1, source_target_pairs={{0,4},{4,0},{1,5},{5,1},{2,6},{6,2},{3,7},{7,3},{8,12},{12,8},{9,1... | collective-permute-start | bytes 3145736 | tf_op jit(solution)/shard_map/ppermute | solution.py:420
  1030.8 27.0 %collective-permute-start.25 = (bf16[4,2,64,1024]{3,2,0,1:T(8,128)(2,1)}, bf16[4,2,64,1024]{3,2,0,1:T(8,128)(2,1)}, u32[]{:S(2)}, u32[]{:S(2)}) collective-permute-start(bf16[4,2,64,1024]{3,2,0,1:T(8,128)(2,1)} %dynamic-slice_bitcast_fusion.3), channel_id=1, source_target_pairs={{0,1},{1,0},{2,3},{3,2},{4,5},{5,4},{6,7},{7,6},{8,9},{9,8},{10,11... | collective-permute-start | bytes 3145736 | tf_op jit(solution)/shard_map/ppermute | solution.py:420
  1038.6 38.2 %collective-permute-start.19 = (bf16[4,2,64,1024]{3,2,0,1:T(8,128)(2,1)}, bf16[4,2,64,1024]{3,2,0,1:T(8,128)(2,1)}, u32[]{:S(2)}, u32[]{:S(2)}) collective-permute-start(bf16[4,2,64,1024]{3,2,0,1:T(8,128)(2,1)} %dynamic-slice_bitcast_fusion.4), channel_id=1, source_target_pairs={{0,4},{4,0},{1,5},{5,1},{2,6},{6,2},{3,7},{7,3},{8,12},{12,8},{9,1... | collective-permute-start | bytes 3145736 | tf_op jit(solution)/shard_map/ppermute | solution.py:420
  1039.7 40.6 %collective-permute-start.17 = (bf16[4,2,64,1024]{3,2,0,1:T(8,128)(2,1)S(1)}, bf16[4,2,64,1024]{3,2,0,1:T(8,128)(2,1)}, u32[]{:S(2)}, u32[]{:S(2)}) collective-permute-start(bf16[4,2,64,1024]{3,2,0,1:T(8,128)(2,1)S(1)} %dynamic-slice_bitcast_fusion.5), channel_id=1, source_target_pairs={{0,1},{1,0},{2,3},{3,2},{4,5},{5,4},{6,7},{7,6},{8,9},{9,8},{10,11... | collective-permute-start | bytes 3145736 | tf_op jit(solution)/shard_map/ppermute | solution.py:420
  1044.8 54.3 %collective-permute-start.11 = (bf16[4,2,64,1024]{3,2,0,1:T(8,128)(2,1)S(1)}, bf16[4,2,64,1024]{3,2,0,1:T(8,128)(2,1)S(1)}, u32[]{:S(2)}, u32[]{:S(2)}) collective-permute-start(bf16[4,2,64,1024]{3,2,0,1:T(8,128)(2,1)S(1)} %dynamic-slice_bitcast_fusion.6), channel_id=1, source_target_pairs={{0,4},{4,0},{1,5},{5,1},{2,6},{6,2},{3,7},{7,3},{8,12},{12,8},{9,1... | collective-permute-start | bytes 3145736 | tf_op jit(solution)/shard_map/ppermute | solution.py:420
  1054.3 47.8 %collective-permute-start.9 = (bf16[4,2,64,1024]{3,2,0,1:T(8,128)(2,1)S(1)}, bf16[4,2,64,1024]{3,2,0,1:T(8,128)(2,1)S(1)}, u32[]{:S(2)}, u32[]{:S(2)}) collective-permute-start(bf16[4,2,64,1024]{3,2,0,1:T(8,128)(2,1)S(1)} %dynamic-slice_bitcast_fusion.7), channel_id=1, source_target_pairs={{0,1},{1,0},{2,3},{3,2},{4,5},{5,4},{6,7},{7,6},{8,9},{9,8},{10,11... | collective-permute-start | bytes 3145736 | tf_op jit(solution)/shard_map/ppermute | solution.py:420
  1057.8 55.5 %collective-permute-start.28 = (bf16[4,64,1024]{2,1,0:T(8,128)(2,1)S(1)}, bf16[4,64,1024]{2,1,0:T(8,128)(2,1)S(1)}, u32[]{:S(2)}, u32[]{:S(2)}) collective-permute-start(bf16[4,64,1024]{2,1,0:T(8,128)(2,1)S(1)} %dynamic-slice_bitcast_fusion.8), channel_id=1, source_target_pairs={{0,1},{1,0},{2,3},{3,2},{4,5},{5,4},{6,7},{7,6},{8,9},{9,8},{10,11... | collective-permute-start | bytes 1572872 | tf_op jit(solution)/shard_map/ppermute | solution.py:420
  1076.8 36.9 %collective-permute-start.26 = (bf16[4,64,1024]{2,1,0:T(8,128)(2,1)S(1)}, bf16[4,64,1024]{2,1,0:T(8,128)(2,1)S(1)}, u32[]{:S(2)}, u32[]{:S(2)}) collective-permute-start(bf16[4,64,1024]{2,1,0:T(8,128)(2,1)S(1)} %dynamic-slice_bitcast_fusion.9), channel_id=1, source_target_pairs={{0,4},{4,0},{1,5},{5,1},{2,6},{6,2},{3,7},{7,3},{8,12},{12,8},{9,1... | collective-permute-start | bytes 1572872 | tf_op jit(solution)/shard_map/ppermute | solution.py:420
  1080.3 44.2 %collective-permute-start.20 = (bf16[4,64,1024]{2,1,0:T(8,128)(2,1)S(1)}, bf16[4,64,1024]{2,1,0:T(8,128)(2,1)S(1)}, u32[]{:S(2)}, u32[]{:S(2)}) collective-permute-start(bf16[4,64,1024]{2,1,0:T(8,128)(2,1)S(1)} %dynamic-slice_bitcast_fusion.10), channel_id=1, source_target_pairs={{0,1},{1,0},{2,3},{3,2},{4,5},{5,4},{6,7},{7,6},{8,9},{9,8},{10,11... | collective-permute-start | bytes 1572872 | tf_op jit(solution)/shard_map/ppermute | solution.py:420
  1099.1 26.6 %collective-permute-start.18 = (bf16[4,64,1024]{2,1,0:T(8,128)(2,1)S(1)}, bf16[4,64,1024]{2,1,0:T(8,128)(2,1)S(1)}, u32[]{:S(2)}, u32[]{:S(2)}) collective-permute-start(bf16[4,64,1024]{2,1,0:T(8,128)(2,1)S(1)} %dynamic-slice_bitcast_fusion.11), channel_id=1, source_target_pairs={{0,4},{4,0},{1,5},{5,1},{2,6},{6,2},{3,7},{7,3},{8,12},{12,8},{9,1... | collective-permute-start | bytes 1572872 | tf_op jit(solution)/shard_map/ppermute | solution.py:420
  1102.0 29.0 %collective-permute-start.12 = (bf16[4,64,1024]{2,1,0:T(8,128)(2,1)S(1)}, bf16[4,64,1024]{2,1,0:T(8,128)(2,1)S(1)}, u32[]{:S(2)}, u32[]{:S(2)}) collective-permute-start(bf16[4,64,1024]{2,1,0:T(8,128)(2,1)S(1)} %dynamic-slice_bitcast_fusion.12), channel_id=1, source_target_pairs={{0,1},{1,0},{2,3},{3,2},{4,5},{5,4},{6,7},{7,6},{8,9},{9,8},{10,11... | collective-permute-start | bytes 1572872 | tf_op jit(solution)/shard_map/ppermute | solution.py:420
  1113.3 22.3 %collective-permute-start.10 = (bf16[4,64,1024]{2,1,0:T(8,128)(2,1)S(1)}, bf16[4,64,1024]{2,1,0:T(8,128)(2,1)S(1)}, u32[]{:S(2)}, u32[]{:S(2)}) collective-permute-start(bf16[4,64,1024]{2,1,0:T(8,128)(2,1)S(1)} %dynamic-slice_bitcast_fusion.13), channel_id=1, source_target_pairs={{0,4},{4,0},{1,5},{5,1},{2,6},{6,2},{3,7},{7,3},{8,12},{12,8},{9,1... | collective-permute-start | bytes 1572872 | tf_op jit(solution)/shard_map/ppermute | solution.py:420
  1114.0 22.0 %collective-permute-start.29 = (bf16[64,2048]{1,0:T(8,128)(2,1)S(1)}, bf16[64,2048]{1,0:T(8,128)(2,1)S(1)}, u32[]{:S(2)}, u32[]{:S(2)}) collective-permute-start(bf16[64,2048]{1,0:T(8,128)(2,1)S(1)} %get-tuple-element.192), channel_id=1, source_target_pairs={{0,8},{8,16},{16,24},{24,0},{1,9},{9,17},{17,25},{25,1},{2,10},{10... | collective-permute-start | bytes 786440 | tf_op jit(solution)/shard_map/ppermute | solution.py:435
  1124.5 31.6 %collective-permute-start.30 = (bf16[64,2048]{1,0:T(8,128)(2,1)S(1)}, bf16[64,2048]{1,0:T(8,128)(2,1)S(1)}, u32[]{:S(2)}, u32[]{:S(2)}) collective-permute-start(bf16[64,2048]{1,0:T(8,128)(2,1)S(1)} %get-tuple-element.193), channel_id=1, source_target_pairs={{0,16},{8,24},{16,0},{24,8},{1,17},{9,25},{17,1},{25,9},{2,18},{10... | collective-permute-start | bytes 786440 | tf_op jit(solution)/shard_map/ppermute | solution.py:435
  1125.7 30.5 %collective-permute-start.31 = (bf16[64,2048]{1,0:T(8,128)(2,1)S(1)}, bf16[64,2048]{1,0:T(8,128)(2,1)S(1)}, u32[]{:S(2)}, u32[]{:S(2)}) collective-permute-start(bf16[64,2048]{1,0:T(8,128)(2,1)S(1)} %get-tuple-element.194), channel_id=1, source_target_pairs={{0,24},{8,0},{16,8},{24,16},{1,25},{9,1},{17,9},{25,17},{2,26},{10... | collective-permute-start | bytes 786440 | tf_op jit(solution)/shard_map/ppermute | solution.py:435
  1131.1 45.4 %collective-permute-start.21 = (bf16[64,2048]{1,0:T(8,128)(2,1)S(1)}, bf16[64,2048]{1,0:T(8,128)(2,1)S(1)}, u32[]{:S(2)}, u32[]{:S(2)}) collective-permute-start(bf16[64,2048]{1,0:T(8,128)(2,1)S(1)} %get-tuple-element.195), channel_id=1, source_target_pairs={{0,8},{8,16},{16,24},{24,0},{1,9},{9,17},{17,25},{25,1},{2,10},{10... | collective-permute-start | bytes 786440 | tf_op jit(solution)/shard_map/ppermute | solution.py:435
  1135.6 41.0 %collective-permute-start.22 = (bf16[64,2048]{1,0:T(8,128)(2,1)S(1)}, bf16[64,2048]{1,0:T(8,128)(2,1)S(1)}, u32[]{:S(2)}, u32[]{:S(2)}) collective-permute-start(bf16[64,2048]{1,0:T(8,128)(2,1)S(1)} %get-tuple-element.196), channel_id=1, source_target_pairs={{0,16},{8,24},{16,0},{24,8},{1,17},{9,25},{17,1},{25,9},{2,18},{10... | collective-permute-start | bytes 786440 | tf_op jit(solution)/shard_map/ppermute | solution.py:435
  1135.9 22.2 %collective-permute-start.13 = (bf16[64,2048]{1,0:T(8,128)(2,1)S(1)}, bf16[64,2048]{1,0:T(8,128)(2,1)S(1)}, u32[]{:S(2)}, u32[]{:S(2)}) collective-permute-start(bf16[64,2048]{1,0:T(8,128)(2,1)S(1)} %get-tuple-element.198), channel_id=1, source_target_pairs={{0,8},{8,16},{16,24},{24,0},{1,9},{9,17},{17,25},{25,1},{2,10},{10... | collective-permute-start | bytes 786440 | tf_op jit(solution)/shard_map/ppermute | solution.py:435
  1156.1 19.4 %collective-permute-start.14 = (bf16[64,2048]{1,0:T(8,128)(2,1)S(1)}, bf16[64,2048]{1,0:T(8,128)(2,1)S(1)}, u32[]{:S(2)}, u32[]{:S(2)}) collective-permute-start(bf16[64,2048]{1,0:T(8,128)(2,1)S(1)} %get-tuple-element.199), channel_id=1, source_target_pairs={{0,16},{8,24},{16,0},{24,8},{1,17},{9,25},{17,1},{25,9},{2,18},{10... | collective-permute-start | bytes 786440 | tf_op jit(solution)/shard_map/ppermute | solution.py:435
  1156.1 19.4 %collective-permute-start.15 = (bf16[64,2048]{1,0:T(8,128)(2,1)S(1)}, bf16[64,2048]{1,0:T(8,128)(2,1)S(1)}, u32[]{:S(2)}, u32[]{:S(2)}) collective-permute-start(bf16[64,2048]{1,0:T(8,128)(2,1)S(1)} %get-tuple-element.200), channel_id=1, source_target_pairs={{0,24},{8,0},{16,8},{24,16},{1,25},{9,1},{17,9},{25,17},{2,26},{10... | collective-permute-start | bytes 786440 | tf_op jit(solution)/shard_map/ppermute | solution.py:435
  1158.1 26.0 %collective-permute-start.23 = (bf16[64,2048]{1,0:T(8,128)(2,1)S(1)}, bf16[64,2048]{1,0:T(8,128)(2,1)S(1)}, u32[]{:S(2)}, u32[]{:S(2)}) collective-permute-start(bf16[64,2048]{1,0:T(8,128)(2,1)S(1)} %get-tuple-element.197), channel_id=1, source_target_pairs={{0,24},{8,0},{16,8},{24,16},{1,25},{9,1},{17,9},{25,17},{2,26},{10... | collective-permute-start | bytes 786440 | tf_op jit(solution)/shard_map/ppermute | solution.py:435
  (43 other events, 161.8 us)
Sparse Core Ops, SparseCore 0:
  18.1 101.2 all-gather.4
  122.9 113.0 all-gather.6

commit v2 on v1

--- a/solution.py
+++ b/solution.py
@@ -1,6 +1,11 @@
+import functools
+import math
+
 import jax
 import jax.numpy as jnp
 from jax import lax
+from jax.experimental import pallas as pl
+from jax.experimental.pallas import tpu as pltpu
 from jax.sharding import PartitionSpec as P
 
 D = 1024
@@ -314,6 +319,142 @@
     )
 
 
+LOG2E = math.log2(math.e)
+PAIR = 128
+CHUNK = 368
+
+
+def nn(a, b):
+    return lax.dot_general(a, b, (((1,), (0,)), ((), ())), preferred_element_type=jnp.float32)
+
+
+def nt(a, b):
+    return lax.dot_general(a, b, (((1,), (1,)), ((), ())), preferred_element_type=jnp.float32)
+
+
+def tn(a, b):
+    return lax.dot_general(a, b, (((0,), (0,)), ((), ())), preferred_element_type=jnp.float32)
+
+
+def vmem(mib):
+    return pltpu.CompilerParams(vmem_limit_bytes=mib * 2**20)
+
+
+def attention_forward_kernel(q_ref, k_ref, v_ref, o_ref, l_ref):
+    count = q_ref.shape[0]
+    scale = (PAIR // 2) ** -0.5 * LOG2E
+    low = lax.broadcasted_iota(jnp.int32, (1, PAIR), 1) < PAIR // 2
+    keys, values = k_ref[...], v_ref[...]
+    zero = jnp.zeros_like(keys)
+    heads = (jnp.where(low, keys, zero), jnp.where(low, zero, keys))
+    wide = jnp.concatenate([values, jnp.ones_like(values)], axis=1)
+    for start in range(0, count, CHUNK):
+        part = slice(start, min(start + CHUNK, count))
+        queries = q_ref[part, :]
+        outs, sums = [], []
+        for head in heads:
+            scores = nt(queries, head)
+            peak = jnp.max(scores, axis=1, keepdims=True) * scale
+            raised = jnp.exp2(scores * scale - peak).astype(jnp.bfloat16)
+            both = nn(raised, wide)
+            total = both[:, PAIR:]
+            outs.append(both[:, :PAIR] / total)
+            sums.append(peak + jnp.log2(total))
+        o_ref[part, :] = jnp.where(low, outs[0], outs[1]).astype(jnp.bfloat16)
+        l_ref[part, :] = jnp.where(low, sums[0], sums[1])
+
+
+def attention_backward_kernel(q_ref, k_ref, v_ref, o_ref, l_ref, u_ref, out_ref, total_ref):
+    count = q_ref.shape[0]
+    plain = (PAIR // 2) ** -0.5
+    scale = plain * LOG2E
+    low = lax.broadcasted_iota(jnp.int32, (1, PAIR), 1) < PAIR // 2
+    queries, upstream = q_ref[...], u_ref[...]
+    product = upstream.astype(jnp.float32) * o_ref[...].astype(jnp.float32)
+    left = jnp.sum(jnp.where(low, product, 0.0), axis=1, keepdims=True)
+    right = jnp.sum(jnp.where(low, 0.0, product), axis=1, keepdims=True)
+    centres = jnp.transpose(jnp.where(low, left, right))
+    logs = jnp.transpose(l_ref[...])
+    for head in range(2):
+
+        def own(value):
+            zero = jnp.zeros_like(value)
+            return jnp.where(low, value, zero) if head == 0 else jnp.where(low, zero, value)
+
+        row = head * (PAIR // 2)
+        own_queries, own_upstream = own(queries), own(upstream)
+        log_row, centre = logs[row : row + 1, :], centres[row : row + 1, :]
+        for start in range(0, count, CHUNK):
+            part = slice(start, min(start + CHUNK, count))
+            keys, values = k_ref[part, :], v_ref[part, :]
+            probs = jnp.exp2(nt(keys, own_queries) * scale - log_row)
+            slopes = (probs * (nt(values, own_upstream) - centre)).astype(jnp.bfloat16)
+            grad_v = nn(probs.astype(jnp.bfloat16), own_upstream).astype(jnp.bfloat16)
+            grad_k = (nn(slopes, own_queries) * plain).astype(jnp.bfloat16)
+            grad_q = tn(slopes, own(keys))
+            if head == 0:
+                out_ref[1, part, :] = grad_k
+                out_ref[2, part, :] = grad_v
+            else:
+                out_ref[1, part, :] = jnp.where(low, out_ref[1, part, :], grad_k)
+                out_ref[2, part, :] = jnp.where(low, out_ref[2, part, :], grad_v)
+            if head == 0 and start == 0:
+                total_ref[...] = grad_q
+            else:
+                total_ref[...] += grad_q
+    out_ref[0] = (total_ref[...] * plain).astype(jnp.bfloat16)
+
+
+def attention_cost(rows, pairs, products):
+    return pl.CostEstimate(
+        flops=products * 2 * rows * rows * PAIR * 2 * pairs,
+        bytes_accessed=8 * rows * PAIR * pairs * 2,
+        transcendentals=rows * rows * 2 * pairs,
+    )
+
+
+def attention_forward(projected):
+    rows, columns = projected.shape
+    pairs = columns // 3 // PAIR
+
+    def block(offset):
+        return pl.BlockSpec((rows, PAIR), lambda j: (0, offset + j))
+
+    return pl.pallas_call(
+        attention_forward_kernel,
+        grid=(pairs,),
+        in_specs=[block(0), block(pairs), block(2 * pairs)],
+        out_specs=[block(0), block(0)],
+        out_shape=[
+            jax.ShapeDtypeStruct((rows, pairs * PAIR), jnp.bfloat16),
+            jax.ShapeDtypeStruct((rows, pairs * PAIR), jnp.float32),
+        ],
+        compiler_params=vmem(48),
+        cost_estimate=attention_cost(rows, pairs, 2),
+        name="attention_forward",
+    )(projected, projected, projected)
+
+
+def attention_backward(projected, attended, logs, upstream):
+    rows, columns = projected.shape
+    pairs = columns // 3 // PAIR
+
+    def block(offset):
+        return pl.BlockSpec((rows, PAIR), lambda j: (0, offset + j))
+
+    return pl.pallas_call(
+        attention_backward_kernel,
+        grid=(pairs,),
+        in_specs=[block(0), block(pairs), block(2 * pairs), block(0), block(0), block(0)],
+        out_specs=pl.BlockSpec((3, rows, PAIR), lambda j: (0, 0, j)),
+        out_shape=jax.ShapeDtypeStruct((3, rows, pairs * PAIR), jnp.bfloat16),
+        scratch_shapes=[pltpu.VMEM((rows, PAIR), jnp.float32)],
+        compiler_params=vmem(48),
+        cost_estimate=attention_cost(rows, pairs, 5),
+        name="attention_backward",
+    )(projected, projected, projected, attended, logs, upstream)
+
+
 def one_sequence_plan(
     entering_states,
     bypass_states,
@@ -337,7 +478,6 @@
 ):
     f32, bf16 = jnp.float32, jnp.bfloat16
     rows, d = entering_states.shape
-    width = d // HEADS
     col = asking_map_matrix.shape[1]
     ffl = expand_layer_matrix.shape[1]
     r = asking_map_matrix.shape[0]
@@ -395,12 +535,7 @@
     merged = jnp.dot(joined, merge_full, preferred_element_type=f32) + merge_add
     first = layer_norm(merged, gain_one, shift_one).astype(bf16)
     projected = jnp.dot(first, project, preferred_element_type=f32).astype(bf16)
-    shaped = projected.reshape(rows, 3, 2, HEADS // 2, width)
-    queries, keys_all, values = (jnp.moveaxis(shaped[:, i], 1, 0) for i in range(3))
-    attended, summary = lax.map(
-        lambda item: attend_forward(item[0], item[1], item[2]), (queries, keys_all, values)
-    )
-    attended = jnp.moveaxis(attended, 0, 1).reshape(rows, d)
+    attended, summary = attention_forward(projected)
     after_attn = merged + contract_cols(attended, output_t) + output_add
     second = layer_norm(after_attn, gain_two, shift_two).astype(bf16)
     hidden = jnp.dot(second, hidden_full, preferred_element_type=f32) + hidden_add
@@ -462,14 +597,8 @@
     branch = grad_after.astype(bf16)
     grad_output_t = contract_rows(branch, attended).astype(bf16)
     grad_attended = jnp.dot(branch, output_t, preferred_element_type=f32).astype(bf16)
-    upstream_heads = jnp.moveaxis(grad_attended.reshape(rows, 2, HEADS // 2, width), 1, 0)
-    grad_qkv = lax.map(
-        lambda item: attend_backward(item[0], item[1], item[2], item[3], item[4]),
-        (queries, keys_all, values, summary, upstream_heads),
-    )
-    grad_projected = jnp.concatenate(
-        [jnp.moveaxis(g, 0, 1).reshape(rows, d) for g in grad_qkv], axis=1
-    )
+    grad_qkv = attention_backward(projected, attended, summary, grad_attended)
+    grad_projected = jnp.concatenate([grad_qkv[i] for i in range(3)], axis=1)
     grad_project = contract_rows(first, grad_projected).astype(bf16)
     four = jnp.concatenate(
         [blocks(grad_project[:, i * d : (i + 1) * d]) for i in range(3)] + [blocks(grad_output_t)],

time: 1190 us -> 923 us (0.78)
  matrix products: 486 us -> 219 us
  Pallas kernels: 0 us -> 103 us
  other arithmetic: 141 us -> 41.3 us
  local copies, waits for them, and re-layouts: 255 us -> 227 us
  waiting for transfers between devices: 207 us -> 223 us
    dot_general x14 -> x0, matrix products: 245 us -> none  [the longest x2 62.1 us: attend_backward(): jnp.einsum('qhd,khd->hqk', queries, keys_all, preferred_element_type=jnp....]
    pallas_call x0 -> x2, Pallas kernels: none -> 103 us  [the longest x1 67.9 us: attention_backward(): pl.pallas_call(attention_backward_kernel, grid=(pairs,), in_specs=[block(...]
    convert_element_type x2 -> x0, other arithmetic: 65.7 us -> none  [attend_backward(): grad_scores = (probs_full * (grad_probs - centre)).astype(jnp.bfloat16)]
    reduce_sum x2 -> x0, other arithmetic: 33 us -> none  [attend_forward(): row_total = jnp.sum(raised, axis=-1, keepdims=True)]
    all_gather x1, waiting for transfers between devices: 0.01 us -> 16.8 us  [one_sequence_plan(): late = lax.all_gather(late, everyone, axis=0, tiled=False)]
    dot_general x5, matrix products: 77.1 us -> 61.6 us  [contract_rows(): lax.dot_general(left, right, (((0,), (0,)), ((), ())), preferred_element_...]
    convert_element_type x2 -> x0, local copies, waits for them, and re-layouts: 12.6 us -> none  [the longest x1 10.1 us: one_sequence_plan(): projected = jnp.dot(first, project, preferred_element_type=f32).astype(bf16)]
    unnamed x145 -> x131, local copies, waits for them, and re-layouts: 83.5 us -> 80.7 us
  transfers between devices with their start and end apart: 34 -> 34, of which waited for: 16 -> 17; matrix products, arithmetic and copies ran while one was open for 24% -> 18% of each run, Pallas kernels for 0% -> 4%
where the time goes in v2:
time: 923 us; the launch traced here: 918 us
  local copies, waits for them, and re-layouts  227 us (25%)
  waiting for transfers between devices  223 us (24%)
  matrix products  219 us (24%)
  Pallas kernels  103 us (11%)
  starting transfers between devices  44.3 us (5%)
  other arithmetic  41.3 us (4%)
  blocking collectives  40.1 us (4%)
  between operations  19.3 us (2%)
    all_gather x1, waiting for transfers between devices, one_sequence_plan(): early = lax.all_gather(early, everyone, axis=0, tiled=False)  93.4 us
    unnamed x131, local copies, waits for them, and re-layouts  80.7 us
    ppermute x20, waiting for transfers between devices, exchange(): return lax.ppermute(value, axis, [(0, 1), (1, 0)])  73.7 us
    pallas_call x1, Pallas kernels, attention_backward(): pl.pallas_call(attention_backward_kernel, grid=(pairs,), in_specs=[block(...  67.9 us
    dot_general x5, matrix products, contract_rows(): lax.dot_general(left, right, (((0,), (0,)), ((), ())), preferred_element_...  61.6 us
    dot_general x5, matrix products, contract_cols(): lax.dot_general(left, right, (((1,), (1,)), ((), ())), preferred_element_...  55.3 us
    dot_general x1, matrix products, one_sequence_plan(): jnp.dot(second, hidden_full, preferred_element_type=f32) + hidden_add  54.1 us
    reshape x6, local copies, waits for them, and re-layouts, blocks(): return value.reshape(4, 2, 2, r, nt, -1).transpose(0, 1, 2, 4, 3, 5)  47.3 us
  transfers between devices with their start and end apart: 34, of which 17 were waited for; matrix products, arithmetic and copies ran while one was open for 18% of the time, Pallas kernels for 4%

profile of v2, /device:TPU:0, one launch (start us, length us, event | category | flops | bytes accessed | tf_op | source)
XLA Modules:
  0.0 917.6 jit_solution(15135260949763388793)
XLA Ops:
  8.4 5.4 concatenate.37
  25.9 93.4 %all-gather.5.cloned.1.call-done = bf16[12800,512]{1,0:T(8,128)(2,1)} async-done(((bf16[400,512]{1,0:T(8,128)(2,1)}), bf16[12800,512]{1,0:T(8,128)(2,1)}) %all-gather.5.cloned.1.call-update) | async-done | bytes 13107216 | tf_op jit(solution)/shard_map/all_gather | solution.py:511
  120.5 4.6 slice.208
  125.6 7.2 reshape.311
  132.8 5.0 slice_bitcast_fusion.3
  148.9 3.8 copy.79
  158.9 9.7 %fusion.94 = (f32[1104]{0:T(1024)S(1)}, f32[1104,1024]{1,0:T(8,128)S(1)}) fusion(f32[1024]{0:T(1024)S(1)} %reshape.336, bf16[1104,2048]{1,0:T(8,128)(2,1)} %constant_dynamic-update-slice_fusion, bf16[2048,1024]{1,0:T(8,128)(2,1)S(1)} %copy-done.12), kind=kOutput, calls=%fused_computation.266 | convolution fusion | flops 4632771584 | bytes 13246784 | tf_op jit(solution)/shard_map/dot_general | solution.py:535
  169.3 9.4 %convolution_convert_fusion.q_ref.k_ref.v_ref = bf16[1104,3072]{1,0:T(8,128)(2,1)} fusion(bf16[1024,3072]{1,0:T(8,128)(2,1)S(1)} %constant_dynamic-update-slice_fusion.7, f32[1104,1024]{1,0:T(8,128)S(1)} %get-tuple-element.106, f32[1024]{0:T(1024)S(1)} %reshape.338, f32[1024]{0:T(1024)S(1)} %reshape.337, f32[1104]{0:T(1024)S(1)} %fusion.78, ...), kind=kOutput, calls=%fused_computation.19 | convolution fusion | flops 6954811392 | bytes 17613440 | tf_op jit(solution)/shard_map/dot_general | solution.py:537
  178.7 35.0 %attention_forward.1 = (bf16[1104,1024]{1,0:T(8,128)(2,1)S(1)}, f32[1104,1024]{1,0:T(8,128)}) custom-call(bf16[1104,3072]{1,0:T(8,128)(2,1)} %convolution_convert_fusion.q_ref.k_ref.v_ref, bf16[1104,3072]{1,0:T(8,128)(2,1)} %convolution_convert_fusion.q_ref.k_ref.v_ref, bf16[1104,3072]{1,0:T(8,128)(2,1)} %convolution_convert_fusion.q_ref.k_ref.v_ref), custom_call_target="tpu_custom_call" | custom-call | flops 9984540672 | bytes 18087936 | tf_op jit(solution)/shard_map/attention_forward/pallas_call | solution.py:423
  213.7 2.7 fusion.95
  219.3 16.8 %all-gather.7.cloned.1.call-done = bf16[4096,2048]{1,0:T(8,128)(2,1)} async-done(((bf16[128,2048]{1,0:T(8,128)(2,1)}), bf16[4096,2048]{1,0:T(8,128)(2,1)}) %all-gather.7.cloned.1.call-update) | async-done | bytes 16777232 | tf_op jit(solution)/shard_map/all_gather | solution.py:513
  236.1 9.7 %fusion.87 = (bf16[16,2,64,2048]{3,2,1,0:T(8,128)(2,1)}, bf16[16,2,64,2048]{3,2,1,0:T(8,128)(2,1)S(1)}) fusion(bf16[16,2,128,2048]{3,2,1,0:T(8,128)(2,1)} %bitcast.270), kind=kLoop, calls=%fused_computation.259 | loop fusion | bytes 33554432 | tf_op jit(solution)/shard_map/slice | solution.py:518
  245.7 7.7 copy.92
  253.5 12.0 %copy.104 = bf16[128,8,2,2048]{3,1,2,0:T(8,128)(2,1)} copy(bf16[128,8,2,2048]{3,2,1,0:T(2,128)(2,1)} %bitcast.260) | data formatting | bytes 16777216
  265.5 16.6 %copy.93 = bf16[16,2,64,2048]{3,1,2,0:T(2,128)(2,1)} copy(bf16[16,2,64,2048]{3,2,1,0:T(8,128)(2,1)} %get-tuple-element.44) | data formatting | bytes 16777216
  282.0 12.1 %copy.105 = bf16[128,8,2,2048]{3,1,2,0:T(8,128)(2,1)} copy(bf16[128,8,2,2048]{3,2,1,0:T(2,128)(2,1)} %bitcast.261) | data formatting | bytes 16777216
  294.1 54.1 %multiply_convert_fusion = (bf16[1104,4096]{1,0:T(8,128)(2,1)}, f32[1104,4096]{1,0:T(8,128)}, f32[1104,4096]{1,0:T(8,128)}) fusion(f32[4096]{0:T(1024)S(1)} %fusion.77, bf16[1024,4096]{1,0:T(8,128)(2,1)} %bitcast.274, f32[1104,1024]{1,0:T(8,128)S(1)} %bitcast.269, f32[1024]{0:T(1024)S(1)} %reshape.341, f32[1024]{0:T(1024)S(1)} %reshape.340, ...), kind=kOutput, calls=%fused_computation.5 | convolution fusion | flops 9565126656 | bytes 58163840 | tf_op jit(solution)/shard_map/dot_general | solution.py:541
  348.3 14.9 %fusion.9 = f32[1104,1024]{1,0:T(8,128)S(1)} fusion(f32[1104,1024]{1,0:T(8,128)S(1)} %bitcast.269, bf16[1104,4096]{1,0:T(8,128)(2,1)} %get-tuple-element.42, bf16[1024,4096]{1,0:T(8,128)(2,1)} %bitcast.276, f32[1024]{0:T(1024)S(1)} %copy-done.39), kind=kOutput, calls=%fused_computation.38 | convolution fusion | flops 9263284224 | bytes 26480640 | tf_op jit(solution)/shard_map/dot_general | solution.py:32
  363.2 18.8 %convolution_convert_fusion.1 = bf16[1024,4096]{1,0:T(8,128)(2,1)} fusion(bf16[1104,4096]{1,0:T(8,128)(2,1)} %get-tuple-element.42, f32[]{:T(128)} %bitcast.12, f32[1104,1024]{1,0:T(8,128)S(1)} %fusion.9, bf16[1104,1024]{1,0:T(8,128)(2,1)S(1)} %copy-done.18), kind=kOutput, calls=%fused_computation.27 | convolution fusion | flops 9269739520 | bytes 24215556 | tf_op jit(solution)/shard_map/dot_general | solution.py:26
  382.0 26.6 %convert_reduce_fusion = (f32[4096]{0:T(1024)}, bf16[1104,4096]{1,0:T(8,128)(2,1)}) fusion(f32[1104,4096]{1,0:T(8,128)} %get-tuple-element.43, f32[1104,4096]{1,0:T(8,128)} %get-tuple-element.109, bf16[1024,4096]{1,0:T(8,128)(2,1)} %bitcast.277, f32[]{:T(128)} %bitcast.12, f32[1104,1024]{1,0:T(8,128)} %copy-done.11, bf16[1104,1024]{1,0:T(8,128)(2,1)} %param.21), kind=kOutput, calls=%fused_computation.3 | convolution fusion | flops 9337892864 | bytes 60407812 | tf_op jit(solution)/shard_map/dot_general | solution.py:587
  408.6 18.3 %convolution_convert_fusion.2 = bf16[1024,4096]{1,0:T(8,128)(2,1)} fusion(bf16[1104,4096]{1,0:T(8,128)(2,1)} %get-tuple-element.113, f32[1104,1024]{1,0:T(8,128)S(1)} %bitcast.269, f32[1024]{0:T(1024)S(1)} %reshape.341, f32[1024]{0:T(1024)S(1)} %reshape.340, f32[1104]{0:T(1024)S(1)} %fusion.79, f32[1104]{0:T(1024)S(1)} %broadcast_multiply_fusion), kind=kOutput, calls=%fused_computation.28 | convolution fusion | flops 9270870016 | bytes 21971584 | tf_op jit(solution)/shard_map/dot_general | solution.py:26
  426.9 17.4 %multiply_reduce_fusion.1 = (f32[1024]{0:T(1024)}, f32[1104]{0:T(1024)S(1)}, f32[1024]{0:T(1024)}, f32[1104,1024]{1,0:T(8,128)S(1)}) fusion(f32[1104,1024]{1,0:T(8,128)S(1)} %bitcast.269, f32[1104]{0:T(1024)S(1)} %fusion.79, f32[1104]{0:T(1024)S(1)} %broadcast_multiply_fusion, f32[1024]{0:T(1024)S(1)} %reshape.340, ...), kind=kOutput, calls=%fused_computation.43 | convolution fusion | flops 9270064128 | bytes 26502080 | tf_op jit(solution)/shard_map/dot_general | solution.py:32
  446.0 4.0 fusion.82
  450.0 2.5 convolution_convert_fusion.5.u_ref
  453.3 4.1 convolution_convert_fusion.6
  457.4 67.9 %attention_backward.1 = bf16[3,1104,1024]{2,1,0:T(8,128)(2,1)} custom-call(bf16[1104,3072]{1,0:T(8,128)(2,1)} %convolution_convert_fusion.q_ref.k_ref.v_ref, bf16[1104,3072]{1,0:T(8,128)(2,1)} %convolution_convert_fusion.q_ref.k_ref.v_ref, bf16[1104,3072]{1,0:T(8,128)(2,1)} %convolution_convert_fusion.q_ref.k_ref.v_ref, bf16[1104,1024]{1,0:T(8,128)(2,1)S(1)} %copy-done.1, ...), custom_call_target="tpu_custom_call" | custom-call | flops 24961351680 | bytes 18087936 | tf_op jit(solution)/shard_map/attention_backward/pallas_call | solution.py:445
  525.3 3.8 slice_bitcast_fusion.2
  529.1 12.0 %convolution_convert_fusion.3 = bf16[1024,3072]{1,0:T(8,128)(2,1)} fusion(bf16[1104,1024]{1,0:T(8,128)(2,1)S(1)} %get-tuple-element.57, bf16[1104,1024]{1,0:T(8,128)(2,1)S(1)} %get-tuple-element.58, bf16[1104,1024]{1,0:T(8,128)(2,1)S(1)} %get-tuple-element.56, f32[1104,1024]{1,0:T(8,128)S(1)} %bitcast.263, f32[1024]{0:T(1024)S(1)} %copy-done.38, ...), kind=kOutput, calls=%fused_computation.36 | convolution fusion | flops 6974914560 | bytes 17613440 | tf_op jit(solution)/shard_map/dot_general | solution.py:26
  541.1 12.9 %multiply_reduce_fusion.2 = (f32[1024]{0:T(1024)S(1)}, f32[1104]{0:T(1024)S(1)}, f32[1024]{0:T(1024)S(1)}, f32[1104,1024]{1,0:T(8,128)}) fusion(f32[1104,1024]{1,0:T(8,128)S(1)} %bitcast.263, f32[1104]{0:T(1024)S(1)} %copy-done.31, f32[1104]{0:T(1024)S(1)} %copy-done.25, f32[1024]{0:T(1024)S(1)} %copy-done.33, bf16[1024,3072]{1,0:T(8,128)(2,1)} %copy-done.23, ...), kind=kOutput, calls=%fused_computation.44 | convolution fusion | flops 6975157248 | bytes 22143936 | tf_op jit(solution)/shard_map/dot_general | solution.py:32
  554.1 14.4 %reshape.334 = bf16[4,2,2,64,2,2048]{5,4,3,2,1,0:T(2,128)(2,1)} reshape(bf16[1024,4096]{1,0:T(8,128)(2,1)} %convolution_convert_fusion.2) | data formatting | bytes 16777216 | tf_op jit(solution)/shard_map/reshape | solution.py:584
  568.5 14.8 %reshape.335 = bf16[4,2,2,64,2,2048]{5,4,3,2,1,0:T(2,128)(2,1)} reshape(bf16[1024,4096]{1,0:T(8,128)(2,1)} %convolution_convert_fusion.1) | data formatting | bytes 16777216 | tf_op jit(solution)/shard_map/reshape | solution.py:584
  583.3 17.6 %constant_dynamic-slice_fusion.1 = (bf16[4,2,1,64,2,2048]{5,4,3,2,1,0:T(2,128)(2,1)}, bf16[4,2,1,64,2,2048]{5,4,3,2,1,0:T(2,128)(2,1)S(1)}, bf16[4,2,1,64,2,2048...) fusion(bf16[4,2,2,64,2,2048]{5,4,3,2,1,0:T(2,128)(2,1)} %reshape.335, s32[]{:T(128)S(6)} %select_n.89, ...), kind=kLoop, calls=%fused_computation.221 | loop fusion | bytes 33554440 | tf_op jit(solution)/shard_map/jit(dynamic_index_in_dim)/dynamic_slice | solution.py:558
  600.9 3.9 copy.118
  605.0 3.9 copy.119
  612.6 8.4 convolution_convert_fusion.4
  624.6 2.8 fusion.89
  627.4 4.5 reshape.330
  631.9 4.5 reshape.331
  636.4 4.5 reshape.332
  640.9 4.5 reshape.333
  645.4 3.3 copy_bitcast_fusion.5
  651.8 7.3 fusion.21
  659.2 2.5 fusion.12
  665.5 10.7 %collective-permute-done.3 = bf16[4,2,64,512]{3,2,0,1:T(8,128)(2,1)S(1)} collective-permute-done((bf16[4,2,64,512]{3,2,0,1:T(8,128)(2,1)S(1)}, bf16[4,2,64,512]{3,2,0,1:T(8,128)(2,1)S(1)}, u32[]{:S(2)}, u32[]{:S(2)}) %collective-permute-start.3) | collective-permute-done | bytes 524320 | tf_op jit(solution)/shard_map/ppermute | solution.py:555
  678.7 2.3 dynamic-slice_bitcast_fusion
  686.0 9.1 fusion.88
  695.1 40.1 %all-reduce.2 = (f32[]{:T(128)}, f32[]{:T(128)}, f32[32,352]{1,0:T(8,128)S(1)}) all-reduce(f32[]{:T(128)S(6)} %mul.187, f32[]{:T(128)S(6)} %mul.188, f32[32,352]{1,0:T(8,128)S(1)} %concatenate.43), channel_id=1, replica_groups=mesh['z'=4,'y'=2,'c'=2,'x'=2] {'z','y','c','x'}, use_global_device_ids=true, to_apply=%region_5.6 | all-reduce | flops 11266 | bytes 90128 | tf_op jit(solution)/shard_map/psum | solution.py:547
  735.1 2.5 collective-permute-start.6
  741.8 2.7 collective-permute-done.6
  745.2 5.8 fusion.6
  756.7 5.0 fusion.7
  764.9 4.1 fusion.8
  771.5 7.7 collective-permute-done.27
  784.8 16.9 %collective-permute-done.19 = bf16[4,2,64,1024]{3,2,0,1:T(8,128)(2,1)} collective-permute-done((bf16[4,2,64,1024]{3,2,0,1:T(8,128)(2,1)}, bf16[4,2,64,1024]{3,2,0,1:T(8,128)(2,1)}, u32[]{:S(2)}, u32[]{:S(2)}) %collective-permute-start.19) | collective-permute-done | bytes 1048608 | tf_op jit(solution)/shard_map/ppermute | solution.py:555
  807.9 16.1 %collective-permute-done.11 = bf16[4,2,64,1024]{3,2,0,1:T(8,128)(2,1)S(1)} collective-permute-done((bf16[4,2,64,1024]{3,2,0,1:T(8,128)(2,1)S(1)}, bf16[4,2,64,1024]{3,2,0,1:T(8,128)(2,1)S(1)}, u32[]{:S(2)}, u32[]{:S(2)}) %collective-permute-start.11) | collective-permute-done | bytes 1048608 | tf_op jit(solution)/shard_map/ppermute | solution.py:555
  828.7 9.3 %collective-permute-done.28 = bf16[4,64,1024]{2,1,0:T(8,128)(2,1)S(1)} collective-permute-done((bf16[4,64,1024]{2,1,0:T(8,128)(2,1)S(1)}, bf16[4,64,1024]{2,1,0:T(8,128)(2,1)S(1)}, u32[]{:S(2)}, u32[]{:S(2)}) %collective-permute-start.28) | collective-permute-done | bytes 524320 | tf_op jit(solution)/shard_map/ppermute | solution.py:555
  838.9 2.3 collective-permute-start.29
  841.2 8.0 collective-permute-done.20
  850.3 3.4 collective-permute-start.31
  855.6 4.2 collective-permute-start.21
  860.6 20.1 %collective-permute-done.30 = bf16[64,2048]{1,0:T(8,128)(2,1)S(1)} collective-permute-done((bf16[64,2048]{1,0:T(8,128)(2,1)S(1)}, bf16[64,2048]{1,0:T(8,128)(2,1)S(1)}, u32[]{:S(2)}, u32[]{:S(2)}) %collective-permute-start.30) | collective-permute-done | bytes 262176 | tf_op jit(solution)/shard_map/ppermute | solution.py:570
  883.0 9.2 %collective-permute-start.23 = (bf16[64,2048]{1,0:T(8,128)(2,1)S(1)}, bf16[64,2048]{1,0:T(8,128)(2,1)S(1)}, u32[]{:S(2)}, u32[]{:S(2)}) collective-permute-start(bf16[64,2048]{1,0:T(8,128)(2,1)S(1)} %get-tuple-element.80), channel_id=1, source_target_pairs={{0,24},{8,0},{16,8},{24,16},{1,25},{9,1},{17,9},{25,17},{2,26},{10... | collective-permute-start | bytes 786440 | tf_op jit(solution)/shard_map/ppermute | solution.py:570
  892.2 8.3 collective-permute-done.14
  901.5 6.9 collective-permute-done.23
  (279 shorter events, 98.1 us)
Async XLA Ops:
  7.2 14.7 %copy-start.14 = (bf16[1104,1024]{1,0:T(8,128)(2,1)S(1)}, bf16[1104,1024]{1,0:T(8,128)(2,1)}, u32[]{:S(2)}) copy-start(bf16[1104,1024]{1,0:T(8,128)(2,1)} %param.19) | copy-start | bytes 6782980
  7.2 112.2 %all-gather.5.cloned.1.call-start = ((), (), s32[]{:S(2)}) async-start(), calls=%async_computation | async-start | bytes 13516800 | tf_op jit(solution)/shard_map/all_gather | solution.py:511
  18.0 218.0 %all-gather.7.cloned.1.call-start = ((), (), s32[]{:S(2)}) async-start(), calls=%async_computation.1 | async-start | bytes 17301504 | tf_op jit(solution)/shard_map/all_gather | solution.py:513
  148.8 20.5 %copy-start.32 = (f32[1024]{0:T(1024)}, f32[1024]{0:T(1024)S(1)}, u32[]{:S(2)}) copy-start(f32[1024]{0:T(1024)S(1)} %reshape.337) | copy-start | bytes 12292
  148.8 20.5 %copy-start.37 = (f32[1024]{0:T(1024)}, f32[1024]{0:T(1024)S(1)}, u32[]{:S(2)}) copy-start(f32[1024]{0:T(1024)S(1)} %reshape.338) | copy-start | bytes 12292
  158.9 10.4 %copy-start.23 = (bf16[1024,3072]{1,0:T(8,128)(2,1)}, bf16[1024,3072]{1,0:T(8,128)(2,1)S(1)}, u32[]{:S(2)}) copy-start(bf16[1024,3072]{1,0:T(8,128)(2,1)S(1)} %constant_dynamic-update-slice_fusion.7) | copy-start | bytes 18874372
  168.6 45.1 %copy-start.3 = (f32[1104,1024]{1,0:T(8,128)}, f32[1104,1024]{1,0:T(8,128)S(1)}, u32[]{:S(2)}) copy-start(f32[1104,1024]{1,0:T(8,128)S(1)} %get-tuple-element.106) | copy-start | bytes 13565956
  168.6 10.1 %copy-start.24 = (f32[1104]{0:T(1024)}, f32[1104]{0:T(1024)S(1)}, u32[]{:S(2)}) copy-start(f32[1104]{0:T(1024)S(1)} %broadcast_multiply_fusion.1) | copy-start | bytes 13252
  169.3 9.4 %copy-start.26 = (f32[1104]{0:T(1024)}, f32[1104]{0:T(1024)S(1)}, u32[]{:S(2)}) copy-start(f32[1104]{0:T(1024)S(1)} %multiply_reduce_fusion.6) | copy-start | bytes 13252
  169.3 9.4 %copy-start.30 = (f32[1104]{0:T(1024)}, f32[1104]{0:T(1024)S(1)}, u32[]{:S(2)}) copy-start(f32[1104]{0:T(1024)S(1)} %fusion.78) | copy-start | bytes 13252
  178.7 35.0 %copy-start.20 = (bf16[128,8,2,512]{3,1,2,0:T(8,128)(2,1)S(1)}, bf16[128,8,2,512]{3,1,2,0:T(8,128)(2,1)}, u32[]{:S(2)}) copy-start(bf16[128,8,2,512]{3,1,2,0:T(8,128)(2,1)} %copy.103) | copy-start | bytes 6291460
  219.2 26.5 %copy-start.28 = (f32[1104]{0:T(1024)}, f32[1104]{0:T(1024)S(1)}, u32[]{:S(2)}) copy-start(f32[1104]{0:T(1024)S(1)} %multiply_reduce_fusion.5) | copy-start | bytes 13252
  265.5 28.6 %slice-start.8 = ((s8[4521984]{0:T(1024)(128)(4,1)}), s8[4194304]{0:T(1024)(128)(4,1)S(1)}, s32[]{:S(2)}) async-start(s8[4521984]{0:T(1024)(128)(4,1)} %bitcast.268), calls=%async_computation.10 | async-start | bytes 8388608
  282.0 12.1 %slice-start.9 = ((s8[4521984]{0:T(1024)(128)(4,1)}), s8[327680]{0:T(1024)(128)(4,1)S(1)}, s32[]{:S(2)}) async-start(s8[4521984]{0:T(1024)(128)(4,1)} %bitcast.268), calls=%async_computation.11 | async-start | bytes 655360
  294.1 54.1 %copy-start.39 = (f32[1024]{0:T(1024)S(1)}, f32[1024]{0:T(1024)}, u32[]{:S(2)}) copy-start(f32[1024]{0:T(1024)} %reshape.343) | copy-start | bytes 12292
  348.3 14.9 %copy-start.18 = (bf16[1104,1024]{1,0:T(8,128)(2,1)S(1)}, bf16[1104,1024]{1,0:T(8,128)(2,1)}, u32[]{:S(2)}) copy-start(bf16[1104,1024]{1,0:T(8,128)(2,1)} %param.21) | copy-start | bytes 6782980
  363.2 18.8 %copy-start.11 = (f32[1104,1024]{1,0:T(8,128)}, f32[1104,1024]{1,0:T(8,128)S(1)}, u32[]{:S(2)}) copy-start(f32[1104,1024]{1,0:T(8,128)S(1)} %fusion.9) | copy-start | bytes 13565956
  408.6 37.1 %slice-start.12 = ((s8[4521984]{0:T(1024)(128)(4,1)}), s8[4194304]{0:T(1024)(128)(4,1)S(1)}, s32[]{:S(2)}) async-start(s8[4521984]{0:T(1024)(128)(4,1)} %bitcast.287), calls=%async_computation.14 | async-start | bytes 8388608
  426.9 17.4 %copy-start.29 = (f32[1104]{0:T(1024)S(1)}, f32[1104]{0:T(1024)}, u32[]{:S(2)}) copy-start(f32[1104]{0:T(1024)} %copy-done.28) | copy-start | bytes 13252
  426.9 18.8 %slice-start.13 = ((s8[4521984]{0:T(1024)(128)(4,1)}), s8[327680]{0:T(1024)(128)(4,1)S(1)}, s32[]{:S(2)}) async-start(s8[4521984]{0:T(1024)(128)(4,1)} %bitcast.287), calls=%async_computation.15 | async-start | bytes 655360
  453.3 75.8 %slice-start.2 = ((s8[4521984]{0:T(1024)(128)(4,1)}), s8[4194304]{0:T(1024)(128)(4,1)S(1)}, s32[]{:S(2)}) async-start(s8[4521984]{0:T(1024)(128)(4,1)} %bitcast.262), calls=%async_computation.4 | async-start | bytes 8388608
  457.4 71.7 %slice-start.3 = ((s8[4521984]{0:T(1024)(128)(4,1)}), s8[327680]{0:T(1024)(128)(4,1)S(1)}, s32[]{:S(2)}) async-start(s8[4521984]{0:T(1024)(128)(4,1)} %bitcast.262), calls=%async_computation.5 | async-start | bytes 655360
  568.5 40.7 %slice-start.14 = ((s8[4521984]{0:T(1024)(128)(4,1)}), s8[327680]{0:T(1024)(128)(4,1)S(1)}, s32[]{:S(2)}) async-start(s8[4521984]{0:T(1024)(128)(4,1)} %bitcast.289), calls=%async_computation.16 | async-start | bytes 655360
  583.3 25.9 %slice-start.15 = ((s8[4521984]{0:T(1024)(128)(4,1)}), s8[4194304]{0:T(1024)(128)(4,1)S(1)}, s32[]{:S(2)}) async-start(s8[4521984]{0:T(1024)(128)(4,1)} %bitcast.289), calls=%async_computation.17 | async-start | bytes 8388608
  604.8 4.5 copy-start.27
  604.8 4.5 slice-start.4
  604.8 140.4 %collective-permute-start.24 = (bf16[4,2,2,64,2048]{4,3,0,2,1:T(8,128)(2,1)}, bf16[4,2,2,64,2048]{4,3,0,2,1:T(8,128)(2,1)}, u32[]{:S(2)}, u32[]{:S(2)}) collective-permute-start(bf16[4,2,2,64,2048]{4,3,0,2,1:T(8,128)(2,1)} %bitcast.255), channel_id=1, source_target_pairs={{0,2},{2,0},{1,3},{3,1},{4,6},{6,4},{5,7},{7,5},{8,10},{10,8},{9,1... | collective-permute-start | bytes 12582920 | tf_op jit(solution)/shard_map/ppermute | solution.py:555
  605.0 4.3 slice-start.5
  605.0 5.6 slice-start.6
  609.0 147.7 %collective-permute-start.16 = (bf16[4,2,2,64,2048]{4,3,0,2,1:T(8,128)(2,1)}, bf16[4,2,2,64,2048]{4,3,0,2,1:T(8,128)(2,1)}, u32[]{:S(2)}, u32[]{:S(2)}) collective-permute-start(bf16[4,2,2,64,2048]{4,3,0,2,1:T(8,128)(2,1)} %bitcast.256), channel_id=1, source_target_pairs={{0,2},{2,0},{1,3},{3,1},{4,6},{6,4},{5,7},{7,5},{8,10},{10,8},{9,1... | collective-permute-start | bytes 12582920 | tf_op jit(solution)/shard_map/ppermute | solution.py:555
  623.1 36.1 %collective-permute-start = (bf16[4,2,2,64,1024]{4,3,0,2,1:T(8,128)(2,1)}, bf16[4,2,2,64,1024]{4,3,0,2,1:T(8,128)(2,1)}, u32[]{:S(2)}, u32[]{:S(2)}) collective-permute-start(bf16[4,2,2,64,1024]{4,3,0,2,1:T(8,128)(2,1)} %bitcast.257), channel_id=1, source_target_pairs={{0,2},{2,0},{1,3},{3,1},{4,6},{6,4},{5,7},{7,5},{8,10},{10,8},{9,1... | collective-permute-start | bytes 6291464 | tf_op jit(solution)/shard_map/ppermute | solution.py:555
  662.0 14.1 %collective-permute-start.3 = (bf16[4,2,64,512]{3,2,0,1:T(8,128)(2,1)S(1)}, bf16[4,2,64,512]{3,2,0,1:T(8,128)(2,1)S(1)}, u32[]{:S(2)}, u32[]{:S(2)}) collective-permute-start(bf16[4,2,64,512]{3,2,0,1:T(8,128)(2,1)S(1)} %dynamic-slice_bitcast_fusion.13), channel_id=1, source_target_pairs={{0,4},{4,0},{1,5},{5,1},{2,6},{6,2},{3,7},{7,3},{8,12},{12,8},{9,1... | collective-permute-start | bytes 1572872 | tf_op jit(solution)/shard_map/ppermute | solution.py:555
  663.6 14.1 %collective-permute-start.1 = (bf16[4,2,64,512]{3,2,0,1:T(8,128)(2,1)S(1)}, bf16[4,2,64,512]{3,2,0,1:T(8,128)(2,1)S(1)}, u32[]{:S(2)}, u32[]{:S(2)}) collective-permute-start(bf16[4,2,64,512]{3,2,0,1:T(8,128)(2,1)S(1)} %dynamic-slice_bitcast_fusion.14), channel_id=1, source_target_pairs={{0,1},{1,0},{2,3},{3,2},{4,5},{5,4},{6,7},{7,6},{8,9},{9,8},{10,11... | collective-permute-start | bytes 1572872 | tf_op jit(solution)/shard_map/ppermute | solution.py:555
  665.5 15.6 %copy-start.2 = (bf16[4,2,2,2,64,2048]{5,4,0,3,1,2:T(8,128)(2,1)}, bf16[4,2,2,2,64,2048]{5,4,0,3,1,2:T(8,128)(2,1)S(1)}, u32[]{:S(2)}) copy-start(bf16[4,2,2,2,64,2048]{5,4,0,3,1,2:T(8,128)(2,1)S(1)} %pad_maximum_fusion) | copy-start | bytes 25165828
  676.4 7.7 collective-permute-start.4
  677.9 4.4 copy-start.34
  677.9 7.4 collective-permute-start.2
  681.1 83.8 %collective-permute-start.8 = (bf16[4,2,2,64,2048]{4,3,0,2,1:T(8,128)(2,1)}, bf16[4,2,2,64,2048]{4,3,0,2,1:T(8,128)(2,1)}, u32[]{:S(2)}, u32[]{:S(2)}) collective-permute-start(bf16[4,2,2,64,2048]{4,3,0,2,1:T(8,128)(2,1)} %dynamic-slice_bitcast_fusion), channel_id=1, source_target_pairs={{0,2},{2,0},{1,3},{3,1},{4,6},{6,4},{5,7},{7,5},{8,10},{10,8},{9,1... | collective-permute-start | bytes 12582920 | tf_op jit(solution)/shard_map/ppermute | solution.py:555
  685.5 52.1 %collective-permute-start.5 = (bf16[64,1024]{1,0:T(8,128)(2,1)S(1)}, bf16[64,1024]{1,0:T(8,128)(2,1)S(1)}, u32[]{:S(2)}, u32[]{:S(2)}) collective-permute-start(bf16[64,1024]{1,0:T(8,128)(2,1)S(1)} %get-tuple-element.88), channel_id=1, source_target_pairs={{0,8},{8,16},{16,24},{24,0},{1,9},{9,17},{17,25},{25,1},{2,10},{10... | collective-permute-start | bytes 393224 | tf_op jit(solution)/shard_map/ppermute | solution.py:570
  735.1 9.3 %collective-permute-start.6 = (bf16[64,1024]{1,0:T(8,128)(2,1)S(1)}, bf16[64,1024]{1,0:T(8,128)(2,1)S(1)}, u32[]{:S(2)}, u32[]{:S(2)}) collective-permute-start(bf16[64,1024]{1,0:T(8,128)(2,1)S(1)} %get-tuple-element.89), channel_id=1, source_target_pairs={{0,16},{8,24},{16,0},{24,8},{1,17},{9,25},{17,1},{25,9},{2,18},{10... | collective-permute-start | bytes 393224 | tf_op jit(solution)/shard_map/ppermute | solution.py:570
  737.6 6.9 collective-permute-start.7
  751.0 5.7 copy-start.6
  752.8 26.4 %collective-permute-start.27 = (bf16[4,2,64,1024]{3,2,0,1:T(8,128)(2,1)}, bf16[4,2,64,1024]{3,2,0,1:T(8,128)(2,1)}, u32[]{:S(2)}, u32[]{:S(2)}) collective-permute-start(bf16[4,2,64,1024]{3,2,0,1:T(8,128)(2,1)} %dynamic-slice_bitcast_fusion.1), channel_id=1, source_target_pairs={{0,4},{4,0},{1,5},{5,1},{2,6},{6,2},{3,7},{7,3},{8,12},{12,8},{9,1... | collective-permute-start | bytes 3145736 | tf_op jit(solution)/shard_map/ppermute | solution.py:555
  755.5 27.0 %collective-permute-start.25 = (bf16[4,2,64,1024]{3,2,0,1:T(8,128)(2,1)}, bf16[4,2,64,1024]{3,2,0,1:T(8,128)(2,1)}, u32[]{:S(2)}, u32[]{:S(2)}) collective-permute-start(bf16[4,2,64,1024]{3,2,0,1:T(8,128)(2,1)} %dynamic-slice_bitcast_fusion.2), channel_id=1, source_target_pairs={{0,1},{1,0},{2,3},{3,2},{4,5},{5,4},{6,7},{7,6},{8,9},{9,8},{10,11... | collective-permute-start | bytes 3145736 | tf_op jit(solution)/shard_map/ppermute | solution.py:555
  756.7 8.2 slice-start
  763.5 38.2 %collective-permute-start.19 = (bf16[4,2,64,1024]{3,2,0,1:T(8,128)(2,1)}, bf16[4,2,64,1024]{3,2,0,1:T(8,128)(2,1)}, u32[]{:S(2)}, u32[]{:S(2)}) collective-permute-start(bf16[4,2,64,1024]{3,2,0,1:T(8,128)(2,1)} %dynamic-slice_bitcast_fusion.3), channel_id=1, source_target_pairs={{0,4},{4,0},{1,5},{5,1},{2,6},{6,2},{3,7},{7,3},{8,12},{12,8},{9,1... | collective-permute-start | bytes 3145736 | tf_op jit(solution)/shard_map/ppermute | solution.py:555
  764.4 40.6 %collective-permute-start.17 = (bf16[4,2,64,1024]{3,2,0,1:T(8,128)(2,1)S(1)}, bf16[4,2,64,1024]{3,2,0,1:T(8,128)(2,1)}, u32[]{:S(2)}, u32[]{:S(2)}) collective-permute-start(bf16[4,2,64,1024]{3,2,0,1:T(8,128)(2,1)S(1)} %dynamic-slice_bitcast_fusion.4), channel_id=1, source_target_pairs={{0,1},{1,0},{2,3},{3,2},{4,5},{5,4},{6,7},{7,6},{8,9},{9,8},{10,11... | collective-permute-start | bytes 3145736 | tf_op jit(solution)/shard_map/ppermute | solution.py:555
  769.8 54.3 %collective-permute-start.11 = (bf16[4,2,64,1024]{3,2,0,1:T(8,128)(2,1)S(1)}, bf16[4,2,64,1024]{3,2,0,1:T(8,128)(2,1)S(1)}, u32[]{:S(2)}, u32[]{:S(2)}) collective-permute-start(bf16[4,2,64,1024]{3,2,0,1:T(8,128)(2,1)S(1)} %dynamic-slice_bitcast_fusion.5), channel_id=1, source_target_pairs={{0,4},{4,0},{1,5},{5,1},{2,6},{6,2},{3,7},{7,3},{8,12},{12,8},{9,1... | collective-permute-start | bytes 3145736 | tf_op jit(solution)/shard_map/ppermute | solution.py:555
  779.2 47.5 %collective-permute-start.9 = (bf16[4,2,64,1024]{3,2,0,1:T(8,128)(2,1)S(1)}, bf16[4,2,64,1024]{3,2,0,1:T(8,128)(2,1)S(1)}, u32[]{:S(2)}, u32[]{:S(2)}) collective-permute-start(bf16[4,2,64,1024]{3,2,0,1:T(8,128)(2,1)S(1)} %dynamic-slice_bitcast_fusion.6), channel_id=1, source_target_pairs={{0,1},{1,0},{2,3},{3,2},{4,5},{5,4},{6,7},{7,6},{8,9},{9,8},{10,11... | collective-permute-start | bytes 3145736 | tf_op jit(solution)/shard_map/ppermute | solution.py:555
  782.5 55.5 %collective-permute-start.28 = (bf16[4,64,1024]{2,1,0:T(8,128)(2,1)S(1)}, bf16[4,64,1024]{2,1,0:T(8,128)(2,1)S(1)}, u32[]{:S(2)}, u32[]{:S(2)}) collective-permute-start(bf16[4,64,1024]{2,1,0:T(8,128)(2,1)S(1)} %dynamic-slice_bitcast_fusion.7), channel_id=1, source_target_pairs={{0,1},{1,0},{2,3},{3,2},{4,5},{5,4},{6,7},{7,6},{8,9},{9,8},{10,11... | collective-permute-start | bytes 1572872 | tf_op jit(solution)/shard_map/ppermute | solution.py:555
  801.6 36.9 %collective-permute-start.26 = (bf16[4,64,1024]{2,1,0:T(8,128)(2,1)S(1)}, bf16[4,64,1024]{2,1,0:T(8,128)(2,1)S(1)}, u32[]{:S(2)}, u32[]{:S(2)}) collective-permute-start(bf16[4,64,1024]{2,1,0:T(8,128)(2,1)S(1)} %dynamic-slice_bitcast_fusion.8), channel_id=1, source_target_pairs={{0,4},{4,0},{1,5},{5,1},{2,6},{6,2},{3,7},{7,3},{8,12},{12,8},{9,1... | collective-permute-start | bytes 1572872 | tf_op jit(solution)/shard_map/ppermute | solution.py:555
  804.9 44.2 %collective-permute-start.20 = (bf16[4,64,1024]{2,1,0:T(8,128)(2,1)S(1)}, bf16[4,64,1024]{2,1,0:T(8,128)(2,1)S(1)}, u32[]{:S(2)}, u32[]{:S(2)}) collective-permute-start(bf16[4,64,1024]{2,1,0:T(8,128)(2,1)S(1)} %dynamic-slice_bitcast_fusion.9), channel_id=1, source_target_pairs={{0,1},{1,0},{2,3},{3,2},{4,5},{5,4},{6,7},{7,6},{8,9},{9,8},{10,11... | collective-permute-start | bytes 1572872 | tf_op jit(solution)/shard_map/ppermute | solution.py:555
  824.0 26.3 %collective-permute-start.18 = (bf16[4,64,1024]{2,1,0:T(8,128)(2,1)S(1)}, bf16[4,64,1024]{2,1,0:T(8,128)(2,1)S(1)}, u32[]{:S(2)}, u32[]{:S(2)}) collective-permute-start(bf16[4,64,1024]{2,1,0:T(8,128)(2,1)S(1)} %dynamic-slice_bitcast_fusion.10), channel_id=1, source_target_pairs={{0,4},{4,0},{1,5},{5,1},{2,6},{6,2},{3,7},{7,3},{8,12},{12,8},{9,1... | collective-permute-start | bytes 1572872 | tf_op jit(solution)/shard_map/ppermute | solution.py:555
  826.7 28.9 %collective-permute-start.12 = (bf16[4,64,1024]{2,1,0:T(8,128)(2,1)S(1)}, bf16[4,64,1024]{2,1,0:T(8,128)(2,1)S(1)}, u32[]{:S(2)}, u32[]{:S(2)}) collective-permute-start(bf16[4,64,1024]{2,1,0:T(8,128)(2,1)S(1)} %dynamic-slice_bitcast_fusion.11), channel_id=1, source_target_pairs={{0,1},{1,0},{2,3},{3,2},{4,5},{5,4},{6,7},{7,6},{8,9},{9,8},{10,11... | collective-permute-start | bytes 1572872 | tf_op jit(solution)/shard_map/ppermute | solution.py:555
  837.9 22.1 %collective-permute-start.10 = (bf16[4,64,1024]{2,1,0:T(8,128)(2,1)S(1)}, bf16[4,64,1024]{2,1,0:T(8,128)(2,1)S(1)}, u32[]{:S(2)}, u32[]{:S(2)}) collective-permute-start(bf16[4,64,1024]{2,1,0:T(8,128)(2,1)S(1)} %dynamic-slice_bitcast_fusion.12), channel_id=1, source_target_pairs={{0,4},{4,0},{1,5},{5,1},{2,6},{6,2},{3,7},{7,3},{8,12},{12,8},{9,1... | collective-permute-start | bytes 1572872 | tf_op jit(solution)/shard_map/ppermute | solution.py:555
  838.9 21.5 %collective-permute-start.29 = (bf16[64,2048]{1,0:T(8,128)(2,1)S(1)}, bf16[64,2048]{1,0:T(8,128)(2,1)S(1)}, u32[]{:S(2)}, u32[]{:S(2)}) collective-permute-start(bf16[64,2048]{1,0:T(8,128)(2,1)S(1)} %get-tuple-element.75), channel_id=1, source_target_pairs={{0,8},{8,16},{16,24},{24,0},{1,9},{9,17},{17,25},{25,1},{2,10},{10... | collective-permute-start | bytes 786440 | tf_op jit(solution)/shard_map/ppermute | solution.py:570
  849.2 31.5 %collective-permute-start.30 = (bf16[64,2048]{1,0:T(8,128)(2,1)S(1)}, bf16[64,2048]{1,0:T(8,128)(2,1)S(1)}, u32[]{:S(2)}, u32[]{:S(2)}) collective-permute-start(bf16[64,2048]{1,0:T(8,128)(2,1)S(1)} %get-tuple-element.76), channel_id=1, source_target_pairs={{0,16},{8,24},{16,0},{24,8},{1,17},{9,25},{17,1},{25,9},{2,18},{10... | collective-permute-start | bytes 786440 | tf_op jit(solution)/shard_map/ppermute | solution.py:570
  850.3 30.3 %collective-permute-start.31 = (bf16[64,2048]{1,0:T(8,128)(2,1)S(1)}, bf16[64,2048]{1,0:T(8,128)(2,1)S(1)}, u32[]{:S(2)}, u32[]{:S(2)}) collective-permute-start(bf16[64,2048]{1,0:T(8,128)(2,1)S(1)} %get-tuple-element.77), channel_id=1, source_target_pairs={{0,24},{8,0},{16,8},{24,16},{1,25},{9,1},{17,9},{25,17},{2,26},{10... | collective-permute-start | bytes 786440 | tf_op jit(solution)/shard_map/ppermute | solution.py:570
  855.6 45.9 %collective-permute-start.21 = (bf16[64,2048]{1,0:T(8,128)(2,1)S(1)}, bf16[64,2048]{1,0:T(8,128)(2,1)S(1)}, u32[]{:S(2)}, u32[]{:S(2)}) collective-permute-start(bf16[64,2048]{1,0:T(8,128)(2,1)S(1)} %get-tuple-element.78), channel_id=1, source_target_pairs={{0,8},{8,16},{16,24},{24,0},{1,9},{9,17},{17,25},{25,1},{2,10},{10... | collective-permute-start | bytes 786440 | tf_op jit(solution)/shard_map/ppermute | solution.py:570
  860.0 41.4 %collective-permute-start.22 = (bf16[64,2048]{1,0:T(8,128)(2,1)S(1)}, bf16[64,2048]{1,0:T(8,128)(2,1)S(1)}, u32[]{:S(2)}, u32[]{:S(2)}) collective-permute-start(bf16[64,2048]{1,0:T(8,128)(2,1)S(1)} %get-tuple-element.79), channel_id=1, source_target_pairs={{0,16},{8,24},{16,0},{24,8},{1,17},{9,25},{17,1},{25,9},{2,18},{10... | collective-permute-start | bytes 786440 | tf_op jit(solution)/shard_map/ppermute | solution.py:570
  860.4 22.6 %collective-permute-start.13 = (bf16[64,2048]{1,0:T(8,128)(2,1)S(1)}, bf16[64,2048]{1,0:T(8,128)(2,1)S(1)}, u32[]{:S(2)}, u32[]{:S(2)}) collective-permute-start(bf16[64,2048]{1,0:T(8,128)(2,1)S(1)} %get-tuple-element.81), channel_id=1, source_target_pairs={{0,8},{8,16},{16,24},{24,0},{1,9},{9,17},{17,25},{25,1},{2,10},{10... | collective-permute-start | bytes 786440 | tf_op jit(solution)/shard_map/ppermute | solution.py:570
  880.7 19.9 %collective-permute-start.14 = (bf16[64,2048]{1,0:T(8,128)(2,1)S(1)}, bf16[64,2048]{1,0:T(8,128)(2,1)S(1)}, u32[]{:S(2)}, u32[]{:S(2)}) collective-permute-start(bf16[64,2048]{1,0:T(8,128)(2,1)S(1)} %get-tuple-element.82), channel_id=1, source_target_pairs={{0,16},{8,24},{16,0},{24,8},{1,17},{9,25},{17,1},{25,9},{2,18},{10... | collective-permute-start | bytes 786440 | tf_op jit(solution)/shard_map/ppermute | solution.py:570
  880.7 19.9 %collective-permute-start.15 = (bf16[64,2048]{1,0:T(8,128)(2,1)S(1)}, bf16[64,2048]{1,0:T(8,128)(2,1)S(1)}, u32[]{:S(2)}, u32[]{:S(2)}) collective-permute-start(bf16[64,2048]{1,0:T(8,128)(2,1)S(1)} %get-tuple-element.83), channel_id=1, source_target_pairs={{0,24},{8,0},{16,8},{24,16},{1,25},{9,1},{17,9},{25,17},{2,26},{10... | collective-permute-start | bytes 786440 | tf_op jit(solution)/shard_map/ppermute | solution.py:570
  883.0 25.4 %collective-permute-start.23 = (bf16[64,2048]{1,0:T(8,128)(2,1)S(1)}, bf16[64,2048]{1,0:T(8,128)(2,1)S(1)}, u32[]{:S(2)}, u32[]{:S(2)}) collective-permute-start(bf16[64,2048]{1,0:T(8,128)(2,1)S(1)} %get-tuple-element.80), channel_id=1, source_target_pairs={{0,24},{8,0},{16,8},{24,16},{1,25},{9,1},{17,9},{25,17},{2,26},{10... | collective-permute-start | bytes 786440 | tf_op jit(solution)/shard_map/ppermute | solution.py:570
  (26 other events, 73.7 us)
Sparse Core Ops, SparseCore 0:
  18.1 101.2 all-gather.4
  122.9 113.0 all-gather.6

commit v3 on v2

--- a/solution.py
+++ b/solution.py
@@ -336,8 +336,8 @@
     return lax.dot_general(a, b, (((0,), (0,)), ((), ())), preferred_element_type=jnp.float32)
 
 
-def vmem(mib):
-    return pltpu.CompilerParams(vmem_limit_bytes=mib * 2**20)
+def vmem():
+    return pltpu.CompilerParams(vmem_limit_bytes=60 * 2**20)
 
 
 def attention_forward_kernel(q_ref, k_ref, v_ref, o_ref, l_ref):
@@ -405,54 +405,659 @@
     out_ref[0] = (total_ref[...] * plain).astype(jnp.bfloat16)
 
 
-def attention_cost(rows, pairs, products):
-    return pl.CostEstimate(
-        flops=products * 2 * rows * rows * PAIR * 2 * pairs,
-        bytes_accessed=8 * rows * PAIR * pairs * 2,
-        transcendentals=rows * rows * 2 * pairs,
-    )
-
-
-def attention_forward(projected):
+def gelu_both(value):
+    t = 1.0 / (1.0 + 0.3275911 * math.sqrt(0.5) * jnp.abs(value))
+    bell = jnp.exp2(value * value * (-0.5 * LOG2E))
+    poly = 0.5 * 1.061405429 * t - 0.5 * 1.453152027
+    poly = poly * t + 0.5 * 1.421413741
+    poly = poly * t - 0.5 * 0.284496736
+    poly = poly * t + 0.5 * 0.254829592
+    rest = poly * t * bell
+    below = jnp.where(value >= 0, 1.0 - rest, rest)
+    return value * below, below + value * bell * (1.0 / math.sqrt(2.0 * math.pi))
+
+
+def normalized(value):
+    centred = value - jnp.mean(value, axis=-1, keepdims=True)
+    spread = jnp.mean(centred * centred, axis=-1, keepdims=True)
+    inverse = lax.rsqrt(spread + EPSILON)
+    return centred * inverse, inverse
+
+
+def place_at(where_ref, hi, lo, y_rel, c_rel, rows):
+    y = jnp.bitwise_xor(where_ref[0], y_rel)
+    c = jnp.bitwise_xor(where_ref[1], c_rel)
+    return pl.multiple_of(((hi * 2 + lo) * 4 + y * 2 + c) * rows, rows)
+
+
+BITS = (0, 1)
+
+
+def once(block, index):
+    return pl.BlockSpec(block, index, pipeline_mode=pl.Buffered(1))
+
+
+def call(kernel, grid, where, ins, outs, scratch, name, after=(), aliases=()):
+    first, count = len(ins), len(after)
+
+    def ordered_kernel(where_ref, *refs):
+        kernel(where_ref, *refs[:first], *refs[first + count :])
+
+    anywhere = pl.BlockSpec(memory_space=pl.ANY)
+    return pl.pallas_call(
+        ordered_kernel,
+        grid_spec=pltpu.PrefetchScalarGridSpec(
+            num_scalar_prefetch=1,
+            grid=grid,
+            in_specs=[spec for _, spec in ins] + [anywhere] * count,
+            out_specs=[spec for _, _, spec in outs],
+            scratch_shapes=scratch,
+        ),
+        out_shape=[jax.ShapeDtypeStruct(s, t) for s, t, _ in outs],
+        input_output_aliases={1 + i: o for i, o in aliases},
+        compiler_params=vmem(),
+        cost_estimate=pl.CostEstimate(flops=0, bytes_accessed=0, transcendentals=0),
+        name=name,
+    )(where, *(x for x, _ in ins), *after)
+
+
+def resident(shape):
+    return once(shape, lambda *_: (0,) * len(shape))
+
+
+def attention_forward(where, projected):
     rows, columns = projected.shape
     pairs = columns // 3 // PAIR
 
     def block(offset):
-        return pl.BlockSpec((rows, PAIR), lambda j: (0, offset + j))
-
-    return pl.pallas_call(
-        attention_forward_kernel,
-        grid=(pairs,),
-        in_specs=[block(0), block(pairs), block(2 * pairs)],
-        out_specs=[block(0), block(0)],
-        out_shape=[
-            jax.ShapeDtypeStruct((rows, pairs * PAIR), jnp.bfloat16),
-            jax.ShapeDtypeStruct((rows, pairs * PAIR), jnp.float32),
+        return pl.BlockSpec((rows, PAIR), lambda j, s: (0, offset + j))
+
+    return call(
+        lambda where_ref, *refs: attention_forward_kernel(*refs),
+        (pairs,),
+        where,
+        [(projected, block(0)), (projected, block(pairs)), (projected, block(2 * pairs))],
+        [
+            ((rows, pairs * PAIR), jnp.bfloat16, block(0)),
+            ((rows, pairs * PAIR), jnp.float32, block(0)),
         ],
-        compiler_params=vmem(48),
-        cost_estimate=attention_cost(rows, pairs, 2),
-        name="attention_forward",
-    )(projected, projected, projected)
-
-
-def attention_backward(projected, attended, logs, upstream):
+        [],
+        "attention_forward",
+    )
+
+
+def attention_backward(where, projected, attended, logs, upstream, index, of, grads):
     rows, columns = projected.shape
     pairs = columns // 3 // PAIR
+    here = index * (pairs // of)
 
     def block(offset):
-        return pl.BlockSpec((rows, PAIR), lambda j: (0, offset + j))
-
-    return pl.pallas_call(
-        attention_backward_kernel,
-        grid=(pairs,),
-        in_specs=[block(0), block(pairs), block(2 * pairs), block(0), block(0), block(0)],
-        out_specs=pl.BlockSpec((3, rows, PAIR), lambda j: (0, 0, j)),
-        out_shape=jax.ShapeDtypeStruct((3, rows, pairs * PAIR), jnp.bfloat16),
-        scratch_shapes=[pltpu.VMEM((rows, PAIR), jnp.float32)],
-        compiler_params=vmem(48),
-        cost_estimate=attention_cost(rows, pairs, 5),
-        name="attention_backward",
-    )(projected, projected, projected, attended, logs, upstream)
+        return pl.BlockSpec((rows, PAIR), lambda j, s: (0, offset + here + j))
+
+    ins = [
+        (projected, block(0)),
+        (projected, block(pairs)),
+        (projected, block(2 * pairs)),
+        (attended, block(0)),
+        (logs, block(0)),
+        (upstream, block(0)),
+    ]
+    aliases = ()
+    if grads is not None:
+        ins.append((grads, pl.BlockSpec(memory_space=pl.ANY)))
+        aliases = ((6, 0),)
+
+    def kernel(where_ref, *refs):
+        attention_backward_kernel(*refs[:6], *refs[-2:])
+
+    return call(
+        kernel,
+        (pairs // of,),
+        where,
+        ins,
+        [((3, rows, pairs * PAIR), jnp.bfloat16, pl.BlockSpec((3, rows, PAIR), lambda j, s: (0, 0, here + j)))],
+        [pltpu.VMEM((rows, PAIR), jnp.float32)],
+        "attention_backward",
+        (),
+        aliases,
+    )[0]
+
+
+def gate(where, values, after):
+    anywhere = pl.BlockSpec(memory_space=pl.ANY)
+    return call(
+        lambda *refs: None,
+        (1,),
+        where,
+        [(v, anywhere) for v in values],
+        [(v.shape, v.dtype, anywhere) for v in values],
+        [],
+        "gate",
+        after,
+        tuple((i, i) for i in range(len(values))),
+    )
+
+
+def pile_kernel(slot, axis, where, mine, other, out):
+    here = 0 if slot is None else where[slot]
+    there = 1 - here
+    if axis == 0:
+        out[here] = mine[...]
+        out[there] = other[...]
+    else:
+        for i in range(out.shape[0]):
+            out[i, here] = mine[i]
+            out[i, there] = other[i]
+
+
+def pile(where, slot, mine, other, axis, after=()):
+    shape = mine.shape[:axis] + (2,) + mine.shape[axis:]
+    return call(
+        functools.partial(pile_kernel, slot, axis),
+        (1,),
+        where,
+        [(mine, resident(mine.shape)), (other, resident(mine.shape))],
+        [(shape, mine.dtype, resident(shape))],
+        [],
+        "pile",
+        after,
+    )[0]
+
+
+def merge_kernel(where, ent, byp, full, out):
+    half = ent.shape[1]
+    weight = full[...].reshape(2 * half, half)
+    out[...] = nn(ent[...], weight[:half, :]) + nn(byp[...], weight[half:, :])
+
+
+def merge_forward(where, ent, byp, gathered, r):
+    rows, d = ent.shape
+    part = pl.BlockSpec((CHUNK, d), lambda i, w: (i, 0))
+    return call(
+        merge_kernel,
+        (rows // CHUNK,),
+        where,
+        [(ent, part), (byp, part), (gathered, resident((2, 2, 2, 2, 2, r, d)))],
+        [((rows, d), jnp.float32, part)],
+        [],
+        "merge_forward",
+    )[0]
+
+
+def project_kernel(rows, where, raw, vec, b00, b01, b10, b11, v00, v01, v10, v11, merged, first, out, natural):
+    w, x_rel = pl.program_id(0), pl.program_id(1)
+
+    @pl.when((w == 0) & (x_rel == 0))
+    def _():
+        for start in range(0, raw.shape[0], CHUNK):
+            part = slice(start, start + CHUNK)
+            total = raw[part, :] + vec[0:1, :]
+            merged[part, :] = total
+            norm, _ = normalized(total)
+            first[part, :] = (norm * vec[1:2, :] + vec[2:3, :]).astype(jnp.bfloat16)
+
+    @pl.when(w < 2)
+    def _():
+        fill_by_core_and_y(where, natural, ((b00, b01), (b10, b11)), rows)
+
+    @pl.when((w == 2) & (x_rel == 0))
+    def _():
+        fill_by_core(where, natural, (v00, v10), rows)
+
+    @pl.when((w == 2) & (x_rel == 1))
+    def _():
+        fill_by_core(where, natural, (v01, v11), rows)
+
+    out[...] = nn(first[...], natural[...]).astype(jnp.bfloat16)
+
+
+def project_forward(where, raw, vec, early, late, r, col):
+    rows, d = raw.shape
+    f32, bf16 = jnp.float32, jnp.bfloat16
+    by_x = pl.BlockSpec(
+        (pl.squeezed, 2, 2, r, col),
+        lambda w, x, s: (jnp.where(w < 2, x, 1), 0, 0, jnp.minimum(w, 1), 0),
+    )
+    by_y = once((2, 2, 2, r, col), lambda w, x, s: (0, 0, 0, 0, 0))
+    return call(
+        functools.partial(project_kernel, r),
+        (3, 2),
+        where,
+        [(raw, resident((rows, d))), (vec, resident(vec.shape))]
+        + [(p, by_x) for p in early]
+        + [(p, by_y) for p in late],
+        [
+            ((rows, d), f32, resident((rows, d))),
+            ((rows, d), bf16, resident((rows, d))),
+            ((rows, 6 * col), bf16, pl.BlockSpec((rows, col), lambda w, x, s: (0, w * 2 + x))),
+            ((3, 2, d, col), bf16, pl.BlockSpec((pl.squeezed, pl.squeezed, d, col), lambda w, x, s: (w, x, 0, 0))),
+        ],
+        [],
+        "project_forward",
+    )
+
+
+def result_kernel(rows, where, attended, merged, vec, v00, v01, v10, v11, after, second, natural, total):
+    step = pl.program_id(0)
+
+    @pl.when(step == 0)
+    def _():
+        fill_by_core(where, natural, (v00, v10), rows)
+        total[...] = nt(attended[...], natural[...])
+
+    @pl.when(step == 1)
+    def _():
+        fill_by_core(where, natural, (v01, v11), rows)
+        for start in range(0, after.shape[0], CHUNK):
+            here = slice(start, start + CHUNK)
+            part = nt(attended[here, :], natural[...])
+            value = merged[here, :] + vec[3:4, :] + (total[here, :] + part)
+            after[here, :] = value
+            norm, _ = normalized(value)
+            second[here, :] = (norm * vec[4:5, :] + vec[5:6, :]).astype(jnp.bfloat16)
+
+
+def result_forward(where, attended, merged, vec, late, r, col):
+    rows, d = merged.shape
+    by_y = once((2, 2, 2, r, col), lambda x, s: (0, 0, 0, 1, 0))
+    return call(
+        functools.partial(result_kernel, r),
+        (2,),
+        where,
+        [
+            (attended, pl.BlockSpec((rows, col), lambda x, s: (0, x))),
+            (merged, resident((rows, d))),
+            (vec, resident(vec.shape)),
+        ]
+        + [(p, by_y) for p in late],
+        [
+            ((rows, d), jnp.float32, resident((rows, d))),
+            ((rows, d), jnp.bfloat16, resident((rows, d))),
+            ((2, d, col), jnp.bfloat16, pl.BlockSpec((pl.squeezed, d, col), lambda x, s: (x, 0, 0))),
+        ],
+        [pltpu.VMEM((rows, d), jnp.float32)],
+        "result_forward",
+    )
+
+
+def fill_by_core(where, full, refs, rows):
+    for c_rel, ref in enumerate(refs):
+        for y_rel in BITS:
+            for hi in BITS:
+                for lo in BITS:
+                    at = place_at(where, hi, lo, y_rel, c_rel, rows)
+                    full[pl.ds(at, rows), :] = ref[y_rel, hi, lo]
+
+
+def fill_by_core_and_y(where, full, refs, rows):
+    for c_rel, pair in enumerate(refs):
+        for y_rel, ref in enumerate(pair):
+            for hi in BITS:
+                for lo in BITS:
+                    at = place_at(where, hi, lo, y_rel, c_rel, rows)
+                    full[pl.ds(at, rows), :] = ref[hi, lo]
+
+
+def spill_by_core(where, full, refs, rows):
+    for c_rel, ref in enumerate(refs):
+        for y_rel in BITS:
+            for hi in BITS:
+                for lo in BITS:
+                    at = place_at(where, hi, lo, y_rel, c_rel, rows)
+                    ref[y_rel, hi, lo] = full[pl.ds(at, rows), :]
+
+
+def expand_kernel(rows, where, second, bias, w0, w1, active, slope, full):
+    fill_by_core(where, full, (w0, w1), rows)
+    for start in range(0, second.shape[0], CHUNK):
+        part = slice(start, start + CHUNK)
+        hidden = nn(second[part, :], full[...]) + bias[...]
+        value, rate = gelu_both(hidden)
+        active[part, :] = value.astype(jnp.bfloat16)
+        slope[part, :] = rate.astype(jnp.bfloat16)
+
+
+def expand_forward(where, second, bias, pieces, block=512):
+    rows, d = second.shape
+    *_, r, half = pieces[0].shape
+    weight = pl.BlockSpec((2, 2, 2, r, block), lambda j, s: (0, 0, 0, 0, j))
+    out = pl.BlockSpec((rows, block), lambda j, s: (0, j))
+    return call(
+        functools.partial(expand_kernel, r),
+        (half // block,),
+        where,
+        [(second, resident((rows, d))), (bias, pl.BlockSpec((1, block), lambda j, s: (0, j)))]
+        + [(p, weight) for p in pieces],
+        [((rows, half), jnp.bfloat16, out)] * 2,
+        [pltpu.VMEM((d, block), jnp.bfloat16)],
+        "expand_forward",
+    )
+
+
+def contract_kernel(rows, steps, where, alive, a0, a1, after, mentor, vec, w00, w01, w10, w11,
+                    out, upstream, grad, sums, energy, full, total):
+    step = pl.program_id(0)
+    fill_by_core_and_y(where, full, ((w00, w01), (w10, w11)), rows)
+    count = after.shape[0]
+
+    @pl.when(step == 0)
+    def _():
+        total[...] = nt(a0[...], full[...])
+
+    @pl.when((step > 0) & (step < steps))
+    def _():
+        total[...] += nt(a0[...], full[...])
+
+    @pl.when((step >= steps) & (step < 2 * steps - 1))
+    def _():
+        total[...] += nt(a1[...], full[...])
+
+    @pl.when(step == 2 * steps - 1)
+    def _():
+        live = alive[0]
+        column, squares = 0.0, 0.0
+        for start in range(0, count, CHUNK):
+            part = slice(start, start + CHUNK)
+            final = after[part, :] + (total[part, :] + nt(a1[part, :], full[...])) + vec[6:7, :]
+            missing = final - mentor[part, :].astype(jnp.float32)
+            slope = live * missing
+            out[part, :] = (live * final).astype(jnp.bfloat16)
+            upstream[part, :] = slope.astype(jnp.bfloat16)
+            grad[part, :] = slope
+            column += jnp.sum(slope, axis=0, keepdims=True)
+            squares += jnp.sum(slope * missing, axis=0, keepdims=True)
+        sums[...] = jnp.broadcast_to(column, sums.shape)
+        energy[...] = jnp.broadcast_to(0.5 * jnp.sum(squares, axis=1, keepdims=True), energy.shape)
+
+
+def contract_forward(where, alive, active, after, mentor, vec, pieces, block=1024):
+    rows, d = after.shape
+    *_, r, half = pieces[0].shape
+    steps = half // block
+    weight = pl.BlockSpec((pl.squeezed, 2, 2, r, block), lambda j, s: (j // steps, 0, 0, 0, j % steps))
+    f32, bf16 = jnp.float32, jnp.bfloat16
+    whole = resident((rows, d))
+    return call(
+        functools.partial(contract_kernel, r, steps),
+        (2 * steps,),
+        where,
+        [
+            (alive, pl.BlockSpec(memory_space=pltpu.SMEM)),
+            (active[0], pl.BlockSpec((rows, block), lambda j, s: (0, jnp.minimum(j, steps - 1)))),
+            (active[1], pl.BlockSpec((rows, block), lambda j, s: (0, jnp.maximum(j - steps, 0)))),
+            (after, whole),
+            (mentor, whole),
+            (vec, resident(vec.shape)),
+        ]
+        + [(p, weight) for p in pieces],
+        [
+            ((rows, d), bf16, whole),
+            ((rows, d), bf16, whole),
+            ((rows, d), f32, whole),
+            ((8, d), f32, resident((8, d))),
+            ((8, 128), f32, resident((8, 128))),
+        ],
+        [pltpu.VMEM((d, block), bf16), pltpu.VMEM((rows, d), f32)],
+        "contract_forward",
+    )
+
+
+def feed_backward_kernel(rows, where, upstream, second, active, slope, v00, v01, v10, v11, w0, w1,
+                         grad_second, e0, e1, d0, d1, bias, down, up, result):
+    step = pl.program_id(0)
+    fill_by_core_and_y(where, down, ((v00, v01), (v10, v11)), rows)
+    fill_by_core(where, up, (w0, w1), rows)
+    grad_active = nn(upstream[...], down[...])
+    grad_hidden = grad_active * slope[...].astype(jnp.float32)
+    bias[...] = jnp.broadcast_to(jnp.sum(grad_hidden, axis=0, keepdims=True), bias.shape)
+    grad_hidden = grad_hidden.astype(jnp.bfloat16)
+    result[...] = tn(upstream[...], active[...]).astype(jnp.bfloat16)
+    spill_by_core(where, result, (d0, d1), rows)
+    back = nt(grad_hidden, up[...])
+
+    @pl.when(step == 0)
+    def _():
+        grad_second[...] = back
+
+    @pl.when(step > 0)
+    def _():
+        grad_second[...] += back
+
+    result[...] = tn(second[...], grad_hidden).astype(jnp.bfloat16)
+    spill_by_core(where, result, (e0, e1), rows)
+
+
+def feed_backward(where, upstream, second, active, slope, down, up, x_rel, block=512):
+    rows, d = upstream.shape
+    *_, r, half = up[0].shape
+    f32, bf16 = jnp.float32, jnp.bfloat16
+    whole = resident((rows, d))
+    part = pl.BlockSpec((rows, block), lambda j, s: (0, j))
+    piece = pl.BlockSpec((2, 2, 2, r, block), lambda j, s: (0, 0, 0, 0, j))
+    quarter = pl.BlockSpec((pl.squeezed, 2, 2, r, block), lambda j, s: (x_rel, 0, 0, 0, j))
+    return call(
+        functools.partial(feed_backward_kernel, r),
+        (half // block,),
+        where,
+        [(upstream, whole), (second, whole), (active, part), (slope, part)]
+        + [(p, quarter) for p in down]
+        + [(p, piece) for p in up],
+        [((rows, d), f32, whole)]
+        + [((2, 2, 2, r, half), bf16, piece)] * 4
+        + [((8, half), f32, pl.BlockSpec((8, block), lambda j, s: (0, j)))],
+        [pltpu.VMEM((d, block), bf16)] * 3,
+        "feed_backward",
+    )
+
+
+def norm_backward_kernel(count, gain_row, where, value, base, vec, *refs):
+    grads, extra, (total, low, sums) = refs[:count], refs[count:-3], refs[-3:]
+    upstream = grads[0][...]
+    for ref in grads[1:]:
+        upstream = upstream + ref[...]
+    norm, inverse = normalized(value[...])
+    e = upstream * vec[gain_row : gain_row + 1, :]
+    mean_e = jnp.mean(e, axis=-1, keepdims=True)
+    mean_en = jnp.mean(e * norm, axis=-1, keepdims=True)
+    result = base[...] + inverse * (e - mean_e - norm * mean_en)
+    total[...] = result
+    low[...] = result.astype(jnp.bfloat16)
+
+    @pl.when(pl.program_id(0) == 0)
+    def _():
+        sums[...] = jnp.zeros_like(sums)
+        if extra:
+            column, energy, alive, own, other = extra
+            d = sums.shape[1]
+            sums[3:4, :] = column[0:1, :]
+            sums[4:5, :] = jnp.broadcast_to(energy[0:1, 0:1], (1, d))
+            sums[5:6, :] = jnp.full((1, d), alive[0] * (value.shape[0] * pl.num_programs(0)), jnp.float32)
+            here = where[2] == 0
+            for i in BITS:
+                part = slice(i * d, (i + 1) * d)
+                sums[8 + i : 9 + i, :] = jnp.where(here, own[0:1, part], other[0:1, part])
+                sums[10 + i : 11 + i, :] = jnp.where(here, other[0:1, part], own[0:1, part])
+
+    for row, item in enumerate((upstream * norm, upstream, result)):
+        sums[row : row + 1, :] += jnp.sum(item, axis=0, keepdims=True)
+
+
+def norm_backward(where, value, base, vec, gain_row, grads, extra=()):
+    rows, d = value.shape
+    part = pl.BlockSpec((CHUNK, d), lambda i, s: (i, 0))
+    height = 16 if extra else 8
+    carried = [
+        (x, pl.BlockSpec(memory_space=pltpu.SMEM) if x.ndim == 1 else resident(x.shape)) for x in extra
+    ]
+    return call(
+        functools.partial(norm_backward_kernel, len(grads), gain_row),
+        (rows // CHUNK,),
+        where,
+        [(value, part), (base, part), (vec, resident(vec.shape))] + [(g, part) for g in grads] + carried,
+        [
+            ((rows, d), jnp.float32, part),
+            ((rows, d), jnp.bfloat16, part),
+            ((height, d), jnp.float32, resident((height, d))),
+        ],
+        [],
+        "norm_backward",
+    )
+
+
+def result_backward_kernel(rows, where, branch, attended, weight, grad, o0, o1, full):
+    grad[...] = nn(branch[...], weight[...]).astype(jnp.bfloat16)
+    full[...] = tn(branch[...], attended[...]).astype(jnp.bfloat16)
+    spill_by_core(where, full, (o0, o1), rows)
+
+
+def result_backward(where, branch, attended, natural, r):
+    rows, d = branch.shape
+    col = natural.shape[-1]
+    bf16 = jnp.bfloat16
+    part = pl.BlockSpec((rows, col), lambda x, s: (0, x))
+    piece = pl.BlockSpec((pl.squeezed, 2, 2, 2, r, col), lambda x, s: (x, 0, 0, 0, 0, 0))
+    return call(
+        functools.partial(result_backward_kernel, r),
+        (2,),
+        where,
+        [
+            (branch, resident((rows, d))),
+            (attended, part),
+            (natural, pl.BlockSpec((pl.squeezed, d, col), lambda x, s: (x, 0, 0))),
+        ],
+        [((rows, d), bf16, part)] + [((2, 2, 2, 2, r, col), bf16, piece)] * 2,
+        [pltpu.VMEM((d, col), bf16)],
+        "result_backward",
+    )
+
+
+def project_weight_kernel(rows, where, first, grad, o0, o1, full):
+    full[...] = tn(first[...], grad[...]).astype(jnp.bfloat16)
+    spill_by_core(where, full, (o0, o1), rows)
+
+
+def project_weight(where, first, grads, r, col):
+    rows, d = first.shape
+    bf16 = jnp.bfloat16
+    part = pl.BlockSpec((pl.squeezed, rows, col), lambda w, x, s: (w, 0, x))
+    piece = pl.BlockSpec((pl.squeezed, pl.squeezed, 2, 2, 2, r, col), lambda w, x, s: (w, x, 0, 0, 0, 0, 0))
+    return call(
+        functools.partial(project_weight_kernel, r),
+        (3, 2),
+        where,
+        [(first, resident((rows, d))), (grads, part)],
+        [((3, 2, 2, 2, 2, r, col), bf16, piece)] * 2,
+        [pltpu.VMEM((d, col), bf16)],
+        "project_weight",
+    )
+
+
+def project_backward_kernel(where, grad, weight, out):
+    part = nt(grad[...], weight[...])
+    begin = (pl.program_id(0) == 0) & (pl.program_id(1) == 0)
+
+    @pl.when(begin)
+    def _():
+        out[...] = part
+
+    @pl.when(jnp.logical_not(begin))
+    def _():
+        out[...] += part
+
+
+def project_backward(where, grads, natural):
+    _, rows, d = grads.shape
+    col = natural.shape[-1]
+    return call(
+        project_backward_kernel,
+        (3, 2),
+        where,
+        [
+            (grads, pl.BlockSpec((pl.squeezed, rows, col), lambda w, x, s: (w, 0, x))),
+            (natural, pl.BlockSpec((pl.squeezed, pl.squeezed, d, col), lambda w, x, s: (w, x, 0, 0))),
+        ],
+        [((rows, d), jnp.float32, resident((rows, d)))],
+        [],
+        "project_backward",
+    )[0]
+
+
+def merge_weight_kernel(where, ent, byp, grad, o0, o1, full):
+    half = ent.shape[1]
+    full[:half, :] = tn(ent[...], grad[...]).astype(jnp.bfloat16)
+    full[half:, :] = tn(byp[...], grad[...]).astype(jnp.bfloat16)
+    for c_rel, ref in enumerate((o0, o1)):
+        for x_rel in BITS:
+            x = jnp.bitwise_xor(where[2], x_rel)
+            for y_rel in BITS:
+                for hi in BITS:
+                    for lo in BITS:
+                        at = place_at(where, hi, lo, y_rel, c_rel, 128) + x * 64
+                        ref[x_rel, y_rel, hi, lo] = full[pl.ds(pl.multiple_of(at, 64), 64), :]
+
+
+def merge_weight(where, ent, byp, grad, r, part):
+    rows, d = ent.shape
+    half = d // 2
+    bf16 = jnp.bfloat16
+    whole = resident((rows, d))
+    piece = resident((2, 2, 2, 2, r, half))
+    return call(
+        merge_weight_kernel,
+        (1,),
+        where,
+        [(ent, whole), (byp, whole), (grad, once((rows, half), lambda j, s: (0, part)))],
+        [((2, 2, 2, 2, r, half), bf16, piece)] * 2,
+        [pltpu.VMEM((2 * d, half), bf16)],
+        "merge_weight",
+    )
+
+
+def merge_backward_kernel(where, grad, full, left, right):
+    half = left.shape[1]
+    weight = full[...].reshape(2 * half, half)
+    left[...] = nt(grad[...], weight[:half, :])
+    right[...] = nt(grad[...], weight[half:, :])
+
+
+def merge_backward(where, grad, gathered, r, after):
+    rows, d = grad.shape
+    part = pl.BlockSpec((CHUNK, d), lambda i, w: (i, 0))
+    return call(
+        merge_backward_kernel,
+        (rows // CHUNK,),
+        where,
+        [(grad, part), (gathered, resident((2, 2, 2, 2, 2, r, d)))],
+        [((rows, d), jnp.float32, part)] * 2,
+        [],
+        "merge_backward",
+        after,
+    )
+
+
+def swap(value, axis):
+    return lax.ppermute(value, axis, [(0, 1), (1, 0)])
+
+
+def swap_line(value, bit):
+    return lax.ppermute(value, "z", [(i, i ^ bit) for i in range(4)])
+
+
+def plus(*parts):
+    total = parts[0].astype(jnp.float32)
+    for part in parts[1:]:
+        total = total + part.astype(jnp.float32)
+    return total
+
+
+def send(value, axis):
+    return swap(value.astype(jnp.bfloat16), axis)
+
+
+def line_parts(total, index, dim):
+    mine = lax.dynamic_index_in_dim(total, index, dim, keepdims=False)
+    other = lax.dynamic_index_in_dim(total, 1 - index, dim, keepdims=False)
+    return mine, other.astype(jnp.bfloat16)
 
 
 def one_sequence_plan(
@@ -478,13 +1083,13 @@
 ):
     f32, bf16 = jnp.float32, jnp.bfloat16
     rows, d = entering_states.shape
-    col = asking_map_matrix.shape[1]
-    ffl = expand_layer_matrix.shape[1]
-    r = asking_map_matrix.shape[0]
-    nf = d // r
-    nt = d // col
+    r, col = asking_map_matrix.shape
+    half = expand_layer_matrix.shape[1]
     everyone = ("z", "y", "c", "x")
-    at = {axis: lax.axis_index(axis) for axis in everyone}
+    z, y, c, x = (lax.axis_index(axis) for axis in everyone)
+    hi, lo = z // 2, z % 2
+    device = ((z * 2 + y) * 2 + c) * 2 + x
+    where = jnp.stack([y, c, x, hi, lo]).astype(jnp.int32)
     small = (
         bypass_merge_offset,
         mixer_layernorm_scale,
@@ -496,161 +1101,172 @@
         expand_layer_offset,
     )
     flat = jnp.concatenate(small)
-    flat = jnp.pad(flat, (0, 16 * col - flat.shape[0])).reshape(16, col)
-    early = jnp.concatenate(
-        [
-            bypass_merge_matrix.reshape(-1, col),
-            asking_map_matrix,
-            lookup_map_matrix,
-            content_map_matrix,
-            mixer_result_matrix.T,
-            flat,
-        ],
-        axis=0,
-    )
-    early = lax.all_gather(early, everyone, axis=0, tiled=False)
-    late = jnp.concatenate([expand_layer_matrix, contract_layer_matrix.T], axis=0)
-    late = lax.all_gather(late, everyone, axis=0, tiled=False)
-    mrows = bypass_merge_matrix.size // col
-    merge_full = early[:, :mrows].reshape(-1, d)
-
-    def columns(block, start, count):
-        part = block.reshape((nf, nt) + block.shape[1:])[:, :, start : start + count]
-        return part.transpose(0, 2, 1, 3).reshape(nf * count, -1)
-
-    project = jnp.concatenate([columns(early, mrows + i * r, r) for i in range(3)], axis=1)
-    output_t = columns(early, mrows + 3 * r, r)
-    hidden_full = columns(late, 0, r)
-    down_t = columns(late, r, r)
-    vec = early[:, mrows + 4 * r :].reshape(nf * nt, -1)
-    vectors, offset = [], 0
-    for item in small:
-        n = item.shape[0]
-        vectors.append(vec[:, offset : offset + n].reshape(-1).astype(f32))
-        offset += n
-    merge_add, gain_one, shift_one, output_add, gain_two, shift_two, down_add, hidden_add = vectors
-
-    alive = lax.dynamic_index_in_dim(occupancy_mask, at["x"], keepdims=False).astype(f32)
-    joined = jnp.concatenate([entering_states, bypass_states], axis=1)
-    merged = jnp.dot(joined, merge_full, preferred_element_type=f32) + merge_add
-    first = layer_norm(merged, gain_one, shift_one).astype(bf16)
-    projected = jnp.dot(first, project, preferred_element_type=f32).astype(bf16)
-    attended, summary = attention_forward(projected)
-    after_attn = merged + contract_cols(attended, output_t) + output_add
-    second = layer_norm(after_attn, gain_two, shift_two).astype(bf16)
-    hidden = jnp.dot(second, hidden_full, preferred_element_type=f32) + hidden_add
-    active = gelu_exact(hidden).astype(bf16)
-    final = after_attn + contract_cols(active, down_t) + down_add
-    missing = final - mentor_states.astype(f32)
-    grad_final = alive * missing
-    block_out = (final * alive).astype(bf16)
-    energy, counted = lax.psum(
-        (0.5 * jnp.sum(grad_final * missing), alive * float(rows)), everyone
-    )
-    loss_value = energy / (counted * d)
-    grad_down_bias = jnp.sum(grad_final, axis=0)
-    upstream = grad_final.astype(bf16)
-
-    def exchange(value, axis):
-        return lax.ppermute(value, axis, [(0, 1), (1, 0)])
-
-    def pick(value, index, dim):
-        return lax.dynamic_index_in_dim(value, index, dim, keepdims=False)
-
-    def halve(value, axis, dim):
-        here = at[axis]
-        got = exchange(pick(value, 1 - here, dim), axis)
-        return (pick(value, here, dim).astype(f32) + got.astype(f32)).astype(value.dtype)
-
-    def line(value, dim):
-        here = at["z"]
-        total = pick(value, here, dim).astype(f32)
-        for k in range(1, 4):
-            target = lax.rem(here + k, 4)
-            got = lax.ppermute(
-                pick(value, target, dim), "z", [(i, (i + k) % 4) for i in range(4)]
-            )
-            total = total + got.astype(f32)
-        return total
-
-    def shared(value):
-        value = halve(value, "c", 2)
-        half = value.shape[-1] // 2
-        left = halve(halve(value[..., :half], "x", 2), "y", 1)
-        right = halve(halve(value[..., half:], "y", 1), "x", 1)
-        return line(jnp.concatenate([left, right], axis=-1), 0)
-
-    def blocks(value):
-        return value.reshape(4, 2, 2, r, nt, -1).transpose(0, 1, 2, 4, 3, 5)
-
-    grad_down = shared(blocks(contract_rows(upstream, active).astype(bf16)))
-    grad_active = jnp.dot(upstream, down_t, preferred_element_type=f32)
-    gelu_value, gelu_pull = jax.vjp(gelu_exact, hidden)
-    grad_hidden = gelu_pull(grad_active)[0].astype(bf16)
-    hidden_bias_term = jnp.sum(grad_hidden.astype(f32), axis=0)
-    grad_hidden_weight = shared(blocks(contract_rows(second, grad_hidden).astype(bf16)))
-    grad_second = contract_cols(grad_hidden, hidden_full)
-    norm_value, second_pull = jax.vjp(layer_norm, after_attn, gain_two, shift_two)
-    back_after, grad_gain_two, grad_shift_two = second_pull(grad_second)
-    grad_after = grad_final + back_after
-    grad_output_bias = jnp.sum(grad_after, axis=0)
-    branch = grad_after.astype(bf16)
-    grad_output_t = contract_rows(branch, attended).astype(bf16)
-    grad_attended = jnp.dot(branch, output_t, preferred_element_type=f32).astype(bf16)
-    grad_qkv = attention_backward(projected, attended, summary, grad_attended)
-    grad_projected = jnp.concatenate([grad_qkv[i] for i in range(3)], axis=1)
-    grad_project = contract_rows(first, grad_projected).astype(bf16)
-    four = jnp.concatenate(
-        [blocks(grad_project[:, i * d : (i + 1) * d]) for i in range(3)] + [blocks(grad_output_t)],
-        axis=-1,
-    )
-    four = shared(four)
-    grad_first = contract_cols(grad_projected, project)
-    first_value, first_pull = jax.vjp(layer_norm, merged, gain_one, shift_one)
-    back_merged, grad_gain_one, grad_shift_one = first_pull(grad_first)
-    grad_merged = grad_after + back_merged
-    grad_merge_bias = jnp.sum(grad_merged, axis=0)
-    merge_grad = grad_merged.astype(bf16)
-    grad_joined = contract_cols(merge_grad, merge_full)
-    merge_weight = shared(
-        contract_rows(joined, merge_grad).astype(bf16).reshape(4, 2, 2, nt, -1, d)
-    )
-    terms = (
-        grad_merge_bias,
-        grad_gain_one,
-        grad_shift_one,
-        grad_output_bias,
-        grad_gain_two,
-        grad_shift_two,
-        grad_down_bias,
-        hidden_bias_term,
-    )
-    stacked = jnp.concatenate([item.reshape(nf * nt, -1) for item in terms], axis=1)
-    stacked = lax.psum_scatter(stacked, everyone, scatter_dimension=0, tiled=True).reshape(-1)
-    sums, offset = [], 0
-    for item in small:
-        n = item.shape[0]
-        sums.append(stacked[offset : offset + n])
-        offset += n
+    flat = jnp.pad(flat, (0, 16 * d - flat.shape[0])).reshape(16, d)
+    pack = lax.all_gather(jnp.concatenate([bypass_merge_matrix, flat]), everyone, axis=0, tiled=False)
+    gathered = pack.reshape((2,) * 5 + pack.shape[1:])
+
+    matrices = (
+        jnp.concatenate([asking_map_matrix, lookup_map_matrix]),
+        jnp.concatenate([content_map_matrix, mixer_result_matrix.T]),
+        expand_layer_matrix,
+        contract_layer_matrix.T,
+    )
+    orders = (("x", "y"), ("y", "x"), ("y", "x"), ("x", "y"))
+    far = [swap_line(m, 2) for m in matrices[:2]]
+    early = [pile(where, 3, m, f, 0) for m, f in zip(matrices[:2], far)]
+    near = [swap_line(m, 1) for m in early]
+    late = gate(where, matrices[2:], early)
+    far = [swap_line(m, 2) for m in late]
+    early = [pile(where, 4, m, f, 1) for m, f in zip(early, near)]
+    third = [swap(m, o[0]) for m, o in zip(early, orders[:2])]
+    late = [pile(where, 3, m, f, 0, after=early) for m, f in zip(late, far)]
+    near = [swap_line(m, 1) for m in late]
+    early = [pile(where, None, m, f, 0, after=late) for m, f in zip(early, third)]
+    fourth = [swap(m, o[1]) for m, o in zip(early, orders[:2])]
+    late = [pile(where, 4, m, f, 1, after=early) for m, f in zip(late, near)]
+    third = [swap(m, o[0]) for m, o in zip(late, orders[2:])]
+    own = gate(where, [early[0], fourth[0], early[1], fourth[1]], late)
+    away = [swap(m, "c") for m in own]
+    early = [(own[0], own[1], away[0], away[1]), (own[2], own[3], away[2], away[3])]
+    raw = merge_forward(where, entering_states, bypass_states, gathered, r)
+    late = [pile(where, None, m, f, 0, after=(raw,)) for m, f in zip(late, third)]
+    fourth = [swap(m, o[1]) for m, o in zip(late, orders[2:])]
+
+    rest = pack[:, r].astype(f32)
+    count = pack.shape[0]
+    vec = rest[:, : 7 * d // count].reshape(count, 7, d // count).transpose(1, 0, 2).reshape(7, d)
+    vec = jnp.pad(vec, ((0, 1), (0, 0)))
+    hidden_add = rest[:, 7 * d // count : 7 * d // count + 2 * half // count].reshape(2, 1, half)
+    alive = lax.dynamic_index_in_dim(occupancy_mask, x, keepdims=True).astype(f32)
+
+    merged, first, projected, project_natural = project_forward(where, raw, vec, early[0], early[1], r, col)
+    attended, logs = attention_forward(where, projected)
+    own = gate(where, [late[0], fourth[0], late[1], fourth[1]], (attended,))
+    away = [swap(m, "c") for m in own]
+    expand_pieces = ((own[0], away[0]), (own[1], away[1]))
+    contract_pieces = (own[2], own[3], away[2], away[3])
+    after_attn, second, result_natural = result_forward(where, attended, merged, vec, early[1], r, col)
+    active, slope = [], []
+    for x_rel in BITS:
+        bias = lax.dynamic_index_in_dim(hidden_add, jnp.bitwise_xor(x, x_rel), keepdims=False)
+        value, rate = expand_forward(where, second, bias, expand_pieces[x_rel])
+        active.append(value)
+        slope.append(rate)
+    block_out, upstream, grad_final, down_bias, energy = contract_forward(
+        where, alive, active, after_attn, mentor_states, vec, contract_pieces
+    )
+
+    def feed(x_rel):
+        return feed_backward(
+            where, upstream, second, active[x_rel], slope[x_rel], contract_pieces, expand_pieces[x_rel], x_rel
+        )
+
+    gs1, e1, e1s, d1, d1s, hb1 = feed(1)
+    e1c, d1c = swap(e1s, "c"), swap(d1s, "c")
+    gs0, e0, e0s, d0, d0s, hb0 = feed(0)
+    e0c, d0c = swap(e0s, "c"), swap(d0s, "c")
+    e1, d1 = gate(where, [e1, d1], (gs0,))
+    e1x = send(plus(e1, e1c), "x")
+    d1y = send(plus(d1[1], d1c[1]), "y")
+    grad_after, branch, sums_two = norm_backward(
+        where, after_attn, grad_final, vec, 4, [gs0, gs1], (down_bias, energy, alive, hb0, hb1)
+    )
+    parcel = lax.all_gather(sums_two, everyone, axis=0, tiled=False)
+    e0, d0 = gate(where, [e0, d0], (branch,))
+    d0y = send(plus(d0[1], d0c[1]), "y")
+    grad_attended, o0, o1 = result_backward(where, branch, attended, result_natural, r)
+
+    def attend(part, grads):
+        return attention_backward(where, projected, attended, logs, grad_attended, part, 2, grads)
+
+    grads = attend(0, None)
+    e0, d0, d1, grads = gate(where, [e0, d0, d1, grads], ())
+    e_far = send(plus(e0[1], e0c[1], e1x[1]), "y")
+    d_far = send(plus(d1[0], d1c[0], d1y), "x")
+    grads = attend(1, grads)
+    e0, d0, grads = gate(where, [e0, d0, grads], ())
+    own = jnp.sum(parcel, axis=0)
+    e_mine, e_other = line_parts(plus(e0[0], e0c[0], e1x[0], e_far), lo, 1)
+    d_mine, d_other = line_parts(plus(d0[0], d0c[0], d0y, d_far), lo, 1)
+    e_near, d_near = swap_line(e_other, 1), swap_line(d_other, 1)
+    p0, p1 = project_weight(where, first, grads, r, col)
+    qk_c = swap(p1[:2], "c")
+    vo0, vo1 = jnp.stack([p0[2], o0]), jnp.stack([p1[2], o1])
+    vo_c = swap(vo1, "c")
+    grad_first = project_backward(where, grads, project_natural)
+    p0, vo0 = gate(where, [p0, vo0], (grad_first,))
+    qk_x = send(plus(p0[:2, 1], qk_c[:, 1]), "x")
+    vo_y = send(plus(vo0[:, :, 1], vo_c[:, :, 1]), "y")
+    e_mine, e_other = line_parts(plus(e_mine, e_near), hi, 0)
+    d_mine, d_other = line_parts(plus(d_mine, d_near), hi, 0)
+    e_end, d_end = swap_line(e_other, 2), swap_line(d_other, 2)
+    grad_merged, merge_grad, sums_one = norm_backward(where, merged, grad_after, vec, 1, [grad_first])
+    l0, l1 = merge_weight(where, entering_states, bypass_states, merge_grad, r, 0)
+    l_c = swap(l1, "c")
+    p0, vo0 = gate(where, [p0, vo0], (l0,))
+    qk = plus(p0[:2, 0], qk_c[:, 0], qk_x)
+    vo = plus(vo0[:, :, 0], vo_c[:, :, 0], vo_y)
+    qk_y, vo_x = send(qk[:, 1], "y"), send(vo[:, 1], "x")
+    r0, r1 = merge_weight(where, entering_states, bypass_states, merge_grad, r, 1)
+    r_c = swap(r1, "c")
+    l0, r0 = gate(where, [l0, r0], ())
+    l_sum = plus(l0[1], l_c[1]).astype(bf16)
+    l_x = swap(l_sum, "x")
+    r_sum = plus(r0[:, 1], r_c[:, 1]).astype(bf16)
+    r_y = swap(r_sum, "y")
+    grad_expand, grad_contract = plus(e_mine, e_end), plus(d_mine, d_end)
+    grad_tokens, grad_shortcut = merge_backward(
+        where, merge_grad, gathered, r, (r_sum[0, 0, 0, :16, :128], l_sum[0, 0, 0, :16, :128])
+    )
+    l0, r0 = gate(where, [l0, r0], (grad_tokens,))
+    qk = plus(qk[:, 0], qk_y)
+    vo = plus(vo[:, 0], vo_x)
+    four = jnp.concatenate([qk[0], qk[1], vo[0], vo[1]], axis=-1)
+    four, other = line_parts(four, lo, 1)
+    four_near = swap_line(other, 1)
+    left = plus(l0[0], l_c[0], l_x)
+    right = plus(r0[:, 0], r_c[:, 0], r_y)
+    left_y, right_x = send(left[1], "y"), send(right[1], "x")
+    four, other = line_parts(plus(four, four_near), hi, 0)
+    four_far = swap_line(other, 2)
+    grad_merge = jnp.concatenate([plus(left[0], left_y), plus(right[0], right_x)], axis=-1)
+    grad_merge, other = line_parts(grad_merge, lo, 1)
+    grad_merge, other = line_parts(plus(grad_merge, swap_line(other, 1)), hi, 0)
+    four = plus(four, four_far)
+    grad_merge = plus(grad_merge, swap_line(other, 2))
+    grad_query, grad_key, grad_value, grad_result = (four[:, i * col : (i + 1) * col] for i in range(4))
+
+    (three,) = gate(where, [sums_one], (grad_tokens,))
+    for axis in ("c", "x", "y"):
+        three = three + swap(three, axis)
+    for bit in (1, 2):
+        three = three + swap_line(three, bit)
+    share = d // count
+    three = lax.dynamic_slice_in_dim(three, device * share, share, 1)
+    four_rows = lax.dynamic_slice_in_dim(own[:4], device * share, share, 1)
+    loss_value = own[4, 0] / (own[5, 0] * d)
+    share = 2 * half // count
+    hidden_row = lax.dynamic_slice_in_dim(own[8:12].reshape(-1), device * share, share, 0)
+    sums = (three[2], three[0], three[1], four_rows[2], four_rows[0], four_rows[1], four_rows[3], hidden_row)
     return (
         block_out,
         loss_value,
-        grad_joined[:, :d],
-        grad_joined[:, d:],
-        merge_weight,
+        grad_tokens,
+        grad_shortcut,
+        grad_merge,
         sums[0],
         sums[1],
         sums[2],
-        four[:, :col],
-        four[:, col : 2 * col],
-        four[:, 2 * col : 3 * col],
-        four[:, 3 * col :].T,
+        grad_query,
+        grad_key,
+        grad_value,
+        grad_result.T,
         sums[3],
         sums[4],
         sums[5],
-        grad_hidden_weight,
+        grad_expand,
         sums[7],
-        grad_down.T,
+        grad_contract.T,
         sums[6],
     )
 

time: 923 us -> 695 us (0.75)
  Pallas kernels: 103 us -> 389 us
  matrix products: 219 us -> 0 us
  local copies, waits for them, and re-layouts: 227 us -> 44.3 us
  waiting for transfers between devices: 223 us -> 132 us
  blocking collectives: 40.1 us -> 0 us
  starting transfers between devices: 44.3 us -> 53.6 us
    pallas_call x2 -> x43, Pallas kernels: 103 us -> 389 us  [call(): pl.pallas_call(ordered_kernel, grid_spec=pltpu.PrefetchScalarGridSpec(num...]
    dot_general x15 -> x0, matrix products: 219 us -> none  [the longest x5 61.6 us: contract_rows(): lax.dot_general(left, right, (((0,), (0,)), ((), ())), preferred_element_...]
    all_gather x2, waiting for transfers between devices: 110 us -> 0.03 us  [the longest x1 0.02 us: one_sequence_plan(): lax.all_gather(jnp.concatenate([bypass_merge_matrix, flat]), everyone, ax...]
    unnamed x131 -> x73, local copies, waits for them, and re-layouts: 80.7 us -> 20.1 us
    reshape x16 -> x4, local copies, waits for them, and re-layouts: 56.1 us -> 0.22 us  [the longest x2 0.18 us: one_sequence_plan(): rest[:, :7 * d // count].reshape(count, 7, d // count).transpose(1, 0, 2)]
    psum x1 -> x0, blocking collectives: 40.1 us -> none  [one_sequence_plan(): lax.psum((0.5 * jnp.sum(grad_final * missing), alive * float(rows)), ever...]
    slice x11 -> x8, local copies, waits for them, and re-layouts: 30.7 us -> 4.56 us  [the longest x1 1.53 us: one_sequence_plan(): qk_c = swap(p1[:2], 'c')]
    dynamic_slice x4 -> x3, local copies, waits for them, and re-layouts: 20.9 us -> 1.25 us  [the longest x1 0.59 us: one_sequence_plan(): lax.dynamic_slice_in_dim(own[8:12].reshape(-1), device * share, share, 0)]
  transfers between devices with their start and end apart: 34 -> 60, of which waited for: 17 -> 19; matrix products, arithmetic and copies ran while one was open for 18% -> 10% of each run, Pallas kernels for 4% -> 49%
where the time goes in v3:
time: 695 us; the launch traced here: 685 us
  Pallas kernels  389 us (56%)
  waiting for transfers between devices  132 us (19%)
  starting transfers between devices  53.6 us (8%)
  other arithmetic  48.5 us (7%)
  local copies, waits for them, and re-layouts  44.3 us (6%)
  between operations  18.1 us (3%)
    pallas_call x43, Pallas kernels, call(): pl.pallas_call(ordered_kernel, grid_spec=pltpu.PrefetchScalarGridSpec(num...  389 us
    ppermute x40, waiting for transfers between devices, swap(): return lax.ppermute(value, axis, [(0, 1), (1, 0)])  73.2 us
    ppermute x18, waiting for transfers between devices, swap_line(): return lax.ppermute(value, 'z', [(i, i ^ bit) for i in range(4)])  58.3 us
    ppermute x40, starting transfers between devices, swap(): return lax.ppermute(value, axis, [(0, 1), (1, 0)])  28.6 us
    ppermute x18, starting transfers between devices, swap_line(): return lax.ppermute(value, 'z', [(i, i ^ bit) for i in range(4)])  24.9 us
    convert_element_type x7, other arithmetic, send(): return swap(value.astype(jnp.bfloat16), axis)  20.1 us
    unnamed x73, local copies, waits for them, and re-layouts  20.1 us
    add x17, other arithmetic, plus(): total = total + part.astype(jnp.float32)  16.3 us
  transfers between devices with their start and end apart: 60, of which 19 were waited for; matrix products, arithmetic and copies ran while one was open for 10% of the time, Pallas kernels for 49%

profile of v3, /device:TPU:0, one launch (start us, length us, event | category | flops | bytes accessed | tf_op | source)
XLA Modules:
  0.0 684.9 jit_solution(14532713947264568653)
XLA Ops:
  10.6 5.4 concatenate.18
  18.6 4.1 collective-permute-start.3
  25.0 7.7 %collective-permute-done.3.refs_1_ = bf16[128,512]{1,0:T(8,128)(2,1)S(1)} collective-permute-done((bf16[128,512]{1,0:T(8,128)(2,1)S(1)}, bf16[128,512]{1,0:T(8,128)(2,1)S(1)}, u32[]{:S(2)}, u32[]{:S(2)}) %collective-permute-start.3) | collective-permute-done | bytes 131104 | tf_op jit(solution)/shard_map/ppermute | solution.py:1043
  33.4 2.4 pile.14.refs_3_.refs_0_
  37.5 2.4 pile.12.refs_0_.refs_2_
  41.4 3.3 collective-permute-start.4
  44.8 10.4 %collective-permute-done.5.refs_1_ = bf16[2,128,512]{2,1,0:T(8,128)(2,1)S(1)} collective-permute-done((bf16[2,128,512]{2,1,0:T(8,128)(2,1)}, bf16[2,128,512]{2,1,0:T(8,128)(2,1)S(1)}, u32[]{:S(2)}, u32[]{:S(2)}) %collective-permute-start.5) | collective-permute-done | bytes 262176 | tf_op jit(solution)/shard_map/ppermute | solution.py:1043
  55.9 2.5 pile.15.refs_3_.refs_0_
  59.8 3.7 collective-permute-done.1.refs_1_
  64.2 2.5 pile.13.refs_2_.refs_0_
  68.4 2.5 pile.16.refs_2_.refs_0_
  70.9 2.4 collective-permute-start.10
  75.7 2.5 pile.17.refs_3_.refs_0_
  79.3 2.9 pile.19.refs_3_.refs_2_
  84.5 2.9 pile.18.refs_2_.refs_0_
  88.9 6.9 %collective-permute-done.10.refs_1_ = bf16[2,64,2048]{2,1,0:T(8,128)(2,1)S(1)} collective-permute-done((bf16[2,64,2048]{2,1,0:T(8,128)(2,1)}, bf16[2,64,2048]{2,1,0:T(8,128)(2,1)S(1)}, u32[]{:S(2)}, u32[]{:S(2)}) %collective-permute-start.10) | collective-permute-done | bytes 524320 | tf_op jit(solution)/shard_map/ppermute | solution.py:1043
  96.6 2.9 pile.20.refs_4_.refs_0_
  101.2 9.8 %collective-permute-done.11.refs_1_ = bf16[2,64,2048]{2,1,0:T(8,128)(2,1)S(1)} collective-permute-done((bf16[2,64,2048]{2,1,0:T(8,128)(2,1)}, bf16[2,64,2048]{2,1,0:T(8,128)(2,1)S(1)}, u32[]{:S(2)}, u32[]{:S(2)}) %collective-permute-start.11) | collective-permute-done | bytes 524320 | tf_op jit(solution)/shard_map/ppermute | solution.py:1043
  111.9 2.9 pile.21.refs_5_.refs_0_
  119.0 9.8 %merge_forward.1.refs_0_.refs_2_ = f32[1104,1024]{1,0:T(8,128)} custom-call(s32[5]{0:T(128)} %stack.35.where_ref, bf16[1104,1024]{1,0:T(8,128)(2,1)} %refs_0_.6, bf16[1104,1024]{1,0:T(8,128)(2,1)} %refs_1_.5, bf16[2,2,2,2,2,80,1024]{6,5,4,3,2,1,0:T(8,128)(2,1)} %bitcast.168), custom_call_target="tpu_custom_call" | custom-call | tf_op jit(solution)/shard_map/merge_forward/pallas_call | solution.py:447
  128.8 6.0 collective-permute-done.16.refs_1_
  135.8 3.7 pile.22.refs_0_
  140.9 3.7 pile.23.refs_2_
  147.8 1.8 collective-permute-done.13.refs_5_
  151.2 17.4 %project_forward.1 = (f32[1104,1024]{1,0:T(8,128)}, bf16[1104,1024]{1,0:T(8,128)(2,1)}, bf16[1104,3072]{1,0:T(8,128)(2,1)}, bf16[3,2,1024,512]{3,2,1,0:T(8,128)(2,1)}) custom-call(s32[5]{0:T(128)} %stack.35.where_ref, f32[1104,1024]{1,0:T(8,128)} %merge_forward.1.refs_0_.refs_2_, f32[8,1024]{1,0:T(8,128)} %pad.9.refs_1_.refs_2_.refs_5_, ...), custom_call_target="tpu_custom_call" | custom-call | tf_op jit(solution)/shard_map/project_forward/pallas_call | solution.py:447
  168.6 34.7 %attention_forward.1 = (bf16[1104,1024]{1,0:T(8,128)(2,1)}, f32[1104,1024]{1,0:T(8,128)}) custom-call(s32[5]{0:T(128)} %stack.35.where_ref, bf16[1104,3072]{1,0:T(8,128)(2,1)} %get-tuple-element.100.refs_0_.refs_1_.refs_2_, bf16[1104,3072]{1,0:T(8,128)(2,1)} %get-tuple-element.100.refs_0_.refs_1_.refs_2_, ...), custom_call_target="tpu_custom_call" | custom-call | tf_op jit(solution)/shard_map/attention_forward/pallas_call | solution.py:447
  207.9 11.2 %result_forward.1 = (f32[1104,1024]{1,0:T(8,128)}, bf16[1104,1024]{1,0:T(8,128)(2,1)}, bf16[2,1024,512]{2,1,0:T(8,128)(2,1)}) custom-call(s32[5]{0:T(128)} %stack.35.where_ref, bf16[1104,1024]{1,0:T(8,128)(2,1)} %get-tuple-element.101.refs_0_.refs_4_.refs_1_.refs_3_, f32[1104,1024]{1,0:T(8,128)} %get-tuple-element.102.refs_1_.refs_0_, ...), custom_call_target="tpu_custom_call" | custom-call | tf_op jit(solution)/shard_map/result_forward/pallas_call | solution.py:447
  219.7 16.6 %expand_forward.3 = (bf16[1104,2048]{1,0:T(8,128)(2,1)}, bf16[1104,2048]{1,0:T(8,128)(2,1)}) custom-call(s32[5]{0:T(128)} %stack.35.where_ref, bf16[1104,1024]{1,0:T(8,128)(2,1)} %get-tuple-element.103.refs_0_.refs_1_, f32[1,2048]{1,0:T(1,128)} %get-tuple-element.181.refs_1_, bf16[2,2,2,64,2048]{4,3,2,1,0:T(8,128)(2,1)} %get-tuple-element.106.refs_2_.refs_8_, ...), custom_call_target="tpu_custom_call" | custom-call | tf_op jit(solution)/shard_map/expand_forward/pallas_call | solution.py:447
  236.3 16.5 %expand_forward.2 = (bf16[1104,2048]{1,0:T(8,128)(2,1)}, bf16[1104,2048]{1,0:T(8,128)(2,1)}) custom-call(s32[5]{0:T(128)} %stack.35.where_ref, bf16[1104,1024]{1,0:T(8,128)(2,1)} %get-tuple-element.103.refs_0_.refs_1_, f32[1,2048]{1,0:T(1,128)} %get-tuple-element.182.refs_1_, bf16[2,2,2,64,2048]{4,3,2,1,0:T(8,128)(2,1)} %get-tuple-element.104.refs_2_.refs_8_, ...), custom_call_target="tpu_custom_call" | custom-call | tf_op jit(solution)/shard_map/expand_forward/pallas_call | solution.py:447
  254.2 22.2 %contract_forward.1 = (bf16[1104,1024]{1,0:T(8,128)(2,1)}, bf16[1104,1024]{1,0:T(8,128)(2,1)}, f32[1104,1024]{1,0:T(8,128)}, f32[8,1024]{1,0:T(8,128)}, f32[8,128]{1,0:T(8,128)}) custom-call(s32[5]{0:T(128)} %stack.35.where_ref, f32[1]{0:T(128)S(6)} %convert_element_type.311.refs_0_.refs_7_, bf16[1104,2048]{1,0:T(8,128)(2,1)} %get-tuple-element.105.refs_1_.refs_2_, ...), custom_call_target="tpu_custom_call" | custom-call | tf_op jit(solution)/shard_map/contract_forward/pallas_call | solution.py:447
  276.4 30.5 %feed_backward.3 = (f32[1104,1024]{1,0:T(8,128)}, bf16[2,2,2,64,2048]{4,3,2,1,0:T(8,128)(2,1)}, bf16[2,2,2,64,2048]{4,3,2,1,0:T(8,128)(2,1)}, bf16[2,2,2,64,2048...) custom-call(s32[5]{0:T(128)} %stack.35.where_ref, ...), custom_call_target="tpu_custom_call" | custom-call | tf_op jit(solution)/shard_map/feed_backward/pallas_call | solution.py:447
  307.5 30.3 %feed_backward.2 = (f32[1104,1024]{1,0:T(8,128)}, bf16[2,2,2,64,2048]{4,3,2,1,0:T(8,128)(2,1)}, bf16[2,2,2,64,2048]{4,3,2,1,0:T(8,128)(2,1)}, bf16[2,2,2,64,2048...) custom-call(s32[5]{0:T(128)} %stack.35.where_ref, ...), custom_call_target="tpu_custom_call" | custom-call | tf_op jit(solution)/shard_map/feed_backward/pallas_call | solution.py:447
  337.8 12.0 %norm_backward.2 = (f32[1104,1024]{1,0:T(8,128)}, bf16[1104,1024]{1,0:T(8,128)(2,1)}, f32[16,1024]{1,0:T(8,128)}) custom-call(s32[5]{0:T(128)} %stack.35.where_ref, f32[1104,1024]{1,0:T(8,128)} %get-tuple-element.108.refs_3_.refs_0_, f32[1104,1024]{1,0:T(8,128)} %get-tuple-element.112.refs_1_, f32[8,1024]{1,0:T(8,128)} %pad.9.refs_1_.refs_2_.refs_5_, ...), custom_call_target="tpu_custom_call" | custom-call | tf_op jit(solution)/shard_map/norm_backward/pallas_call | solution.py:447
  351.1 3.8 add_convert_fusion
  358.6 9.5 %result_backward.1 = (bf16[1104,1024]{1,0:T(8,128)(2,1)}, bf16[2,2,2,2,64,512]{5,4,3,2,1,0:T(8,128)(2,1)}, bf16[2,2,2,2,64,512]{5,4,3,2,1,0:T(8,128)(2,1)}) custom-call(s32[5]{0:T(128)} %stack.35.where_ref, bf16[1104,1024]{1,0:T(8,128)(2,1)} %get-tuple-element.126.refs_2_.refs_0_, bf16[1104,1024]{1,0:T(8,128)(2,1)} %get-tuple-element.101.refs_0_.refs_4_.refs_1_.refs_3_, ...), custom_call_target="tpu_custom_call" | custom-call | tf_op jit(solution)/shard_map/result_backward/pallas_call | solution.py:447
  368.8 35.6 %attention_backward.2.refs_3_ = bf16[3,1104,1024]{2,1,0:T(8,128)(2,1)} custom-call(s32[5]{0:T(128)} %stack.35.where_ref, bf16[1104,3072]{1,0:T(8,128)(2,1)} %get-tuple-element.100.refs_0_.refs_1_.refs_2_, bf16[1104,3072]{1,0:T(8,128)(2,1)} %get-tuple-element.100.refs_0_.refs_1_.refs_2_, bf16[1104,3072]{1,0:T(8,128)(2,1)} %get-tuple-element.100.refs_0_.refs_1_.refs_2_, ...), custom_call_target="tpu_custom_call" | custom-call | tf_op jit(solution)/shard_map/attention_backward/pallas_call | solution.py:447
  404.4 2.6 fusion.7
  408.8 3.5 fusion.2
  413.4 35.9 %attention_backward.3.refs_2_ = bf16[3,1104,1024]{2,1,0:T(8,128)(2,1)} custom-call(s32[5]{0:T(128)} %stack.35.where_ref, bf16[1104,3072]{1,0:T(8,128)(2,1)} %get-tuple-element.100.refs_0_.refs_1_.refs_2_, bf16[1104,3072]{1,0:T(8,128)(2,1)} %get-tuple-element.100.refs_0_.refs_1_.refs_2_, ...), custom_call_target="tpu_custom_call", output_to_operand_aliasing={{}: (7, {})} | custom-call | tf_op jit(solution)/shard_map/attention_backward/pallas_call | solution.py:447
  449.2 1.9 reduce_sum.9
  451.4 3.1 fusion.6
  456.6 13.5 %project_weight.1 = (bf16[3,2,2,2,2,64,512]{6,5,4,3,2,1,0:T(8,128)(2,1)}, bf16[3,2,2,2,2,64,512]{6,5,4,3,2,1,0:T(8,128)(2,1)}) custom-call(s32[5]{0:T(128)} %stack.35.where_ref, bf16[1104,1024]{1,0:T(8,128)(2,1)} %get-tuple-element.152.refs_0_, bf16[3,1104,1024]{2,1,0:T(8,128)(2,1)} %get-tuple-element.138.refs_0_.refs_1_), custom_call_target="tpu_custom_call" | custom-call | tf_op jit(solution)/shard_map/project_weight/pallas_call | solution.py:447
  470.1 2.4 copy.88
  477.0 2.6 fusion.3
  484.0 15.2 %project_backward.1.refs_3_.refs_2_ = f32[1104,1024]{1,0:T(8,128)} custom-call(s32[5]{0:T(128)} %stack.35.where_ref, bf16[3,1104,1024]{2,1,0:T(8,128)(2,1)} %get-tuple-element.138.refs_0_.refs_1_, bf16[3,2,1024,512]{3,2,1,0:T(8,128)(2,1)} %get-tuple-element.139.refs_1_), custom_call_target="tpu_custom_call" | custom-call | tf_op jit(solution)/shard_map/project_backward/pallas_call | solution.py:447
  499.2 11.3 %norm_backward.3 = (f32[1104,1024]{1,0:T(8,128)}, bf16[1104,1024]{1,0:T(8,128)(2,1)}, f32[8,1024]{1,0:T(8,128)}) custom-call(s32[5]{0:T(128)} %stack.35.where_ref, f32[1104,1024]{1,0:T(8,128)} %get-tuple-element.102.refs_1_.refs_0_, f32[1104,1024]{1,0:T(8,128)} %get-tuple-element.123.refs_1_, f32[8,1024]{1,0:T(8,128)} %pad.9.refs_1_.refs_2_.refs_5_, ...), custom_call_target="tpu_custom_call" | custom-call | tf_op jit(solution)/shard_map/norm_backward/pallas_call | solution.py:447
  510.4 7.6 %merge_weight.3 = (bf16[2,2,2,2,64,512]{5,4,3,2,1,0:T(8,128)(2,1)}, bf16[2,2,2,2,64,512]{5,4,3,2,1,0:T(8,128)(2,1)}) custom-call(s32[5]{0:T(128)} %stack.35.where_ref, bf16[1104,1024]{1,0:T(8,128)(2,1)} %refs_0_.6, bf16[1104,1024]{1,0:T(8,128)(2,1)} %refs_1_.5, bf16[1104,1024]{1,0:T(8,128)(2,1)} %get-tuple-element.140.refs_2_.refs_0_), custom_call_target="tpu_custom_call" | custom-call | tf_op jit(solution)/shard_map/merge_weight/pallas_call | solution.py:447
  518.0 7.7 %merge_weight.2 = (bf16[2,2,2,2,64,512]{5,4,3,2,1,0:T(8,128)(2,1)}, bf16[2,2,2,2,64,512]{5,4,3,2,1,0:T(8,128)(2,1)}) custom-call(s32[5]{0:T(128)} %stack.35.where_ref, bf16[1104,1024]{1,0:T(8,128)(2,1)} %refs_0_.6, bf16[1104,1024]{1,0:T(8,128)(2,1)} %refs_1_.5, bf16[1104,1024]{1,0:T(8,128)(2,1)} %get-tuple-element.140.refs_2_.refs_0_), custom_call_target="tpu_custom_call" | custom-call | tf_op jit(solution)/shard_map/merge_weight/pallas_call | solution.py:447
  532.8 2.4 collective-permute-start.57
  535.2 2.5 bitcast_add_fusion.2
  539.1 2.9 fusion.4
  542.1 2.6 fusion.5
  550.1 9.7 %merge_backward.1 = (f32[1104,1024]{1,0:T(8,128)}, f32[1104,1024]{1,0:T(8,128)}) custom-call(s32[5]{0:T(128)} %stack.35.where_ref, bf16[1104,1024]{1,0:T(8,128)(2,1)} %get-tuple-element.140.refs_2_.refs_0_, bf16[2,2,2,2,2,80,1024]{6,5,4,3,2,1,0:T(8,128)(2,1)} %bitcast.170, bf16[16,128]{1,0:T(8,128)(2,1)} %slice_bitcast_fusion.13.refs_2_, ...), custom_call_target="tpu_custom_call" | custom-call | tf_op jit(solution)/shard_map/merge_backward/pallas_call | solution.py:447
  565.9 2.4 collective-permute-done.33
  573.7 4.6 collective-permute-done.34
  582.0 26.5 %collective-permute-done.26 = bf16[2,2,2,64,512]{4,3,2,1,0:T(8,128)(2,1)S(1)} collective-permute-done((bf16[2,2,2,64,512]{4,3,2,1,0:T(8,128)(2,1)S(1)}, bf16[2,2,2,64,512]{4,3,2,1,0:T(8,128)(2,1)S(1)}, u32[]{:S(2)}, u32[]{:S(2)}) %collective-permute-start.26) | collective-permute-done | bytes 524320 | tf_op jit(solution)/shard_map/ppermute | solution.py:1039
  612.5 2.4 collective-permute-start.36
  615.1 4.0 collective-permute-done.27
  620.8 2.2 bitcast_add_fusion.3
  623.7 17.9 %collective-permute-done.41 = bf16[2,2,2,2,64,512]{5,4,3,2,1,0:T(8,128)(2,1)S(1)} collective-permute-done((bf16[2,2,2,2,64,512]{5,4,3,2,1,0:T(8,128)(2,1)S(1)}, bf16[2,2,2,2,64,512]{5,4,3,2,1,0:T(8,128)(2,1)S(1)}, u32[]{:S(2)}, u32[]{:S(2)}) %collective-permute-start.41) | collective-permute-done | bytes 1048608 | tf_op jit(solution)/shard_map/ppermute | solution.py:1039
  644.0 4.2 collective-permute-done.39
  648.5 4.1 collective-permute-done.42
  656.3 10.3 %collective-permute-done.43 = bf16[2,64,2048]{2,1,0:T(8,128)(2,1)S(1)} collective-permute-done((bf16[2,64,2048]{2,1,0:T(8,128)(2,1)S(1)}, bf16[2,64,2048]{2,1,0:T(8,128)(2,1)S(1)}, u32[]{:S(2)}, u32[]{:S(2)}) %collective-permute-start.43) | collective-permute-done | bytes 524320 | tf_op jit(solution)/shard_map/ppermute | solution.py:1043
  668.1 7.8 %collective-permute-done.44 = bf16[64,2048]{1,0:T(8,128)(2,1)S(1)} collective-permute-done((bf16[64,2048]{1,0:T(8,128)(2,1)S(1)}, bf16[64,2048]{1,0:T(8,128)(2,1)S(1)}, u32[]{:S(2)}, u32[]{:S(2)}) %collective-permute-start.44) | collective-permute-done | bytes 262176 | tf_op jit(solution)/shard_map/ppermute | solution.py:1043
  (258 shorter events, 107.7 us)
Async XLA Ops:
  7.2 111.8 %all-gather.5.cloned.1.call-start = ((), (), s32[]{:S(2)}) async-start(), calls=%async_computation | async-start | bytes 5406720 | tf_op jit(solution)/shard_map/all_gather | solution.py:1105
  17.7 431.6 %all-gather.7.cloned.1.call-start = ((), (), s32[]{:S(2)}) async-start(), calls=%async_computation.1 | async-start | bytes 2162688 | tf_op jit(solution)/shard_map/all_gather | solution.py:1174
  18.6 14.1 %collective-permute-start.3 = (bf16[128,512]{1,0:T(8,128)(2,1)S(1)}, bf16[128,512]{1,0:T(8,128)(2,1)S(1)}, u32[]{:S(2)}, u32[]{:S(2)}) collective-permute-start(bf16[128,512]{1,0:T(8,128)(2,1)S(1)} %pad_maximum_fusion.4.refs_0_), channel_id=1, source_target_pairs={{0,16},{8,24},{16,0},{24,8},{1,17},{9,25},{17,1},{25,9},{2,18},{10... | collective-permute-start | bytes 393224 | tf_op jit(solution)/shard_map/ppermute | solution.py:1043
  24.4 12.4 %collective-permute-start = (bf16[128,512]{1,0:T(8,128)(2,1)S(1)}, bf16[128,512]{1,0:T(8,128)(2,1)S(1)}, u32[]{:S(2)}, u32[]{:S(2)}) collective-permute-start(bf16[128,512]{1,0:T(8,128)(2,1)S(1)} %constant_dynamic-update-slice_fusion.refs_0_), channel_id=1, source_target_pairs={{0,16},{8,24},{16,0},{24,8},{1,17},{9,25},{17,1},{25,9},{2,18},{10... | collective-permute-start | bytes 393224 | tf_op jit(solution)/shard_map/ppermute | solution.py:1043
  35.7 19.4 %collective-permute-start.5 = (bf16[2,128,512]{2,1,0:T(8,128)(2,1)}, bf16[2,128,512]{2,1,0:T(8,128)(2,1)S(1)}, u32[]{:S(2)}, u32[]{:S(2)}) collective-permute-start(bf16[2,128,512]{2,1,0:T(8,128)(2,1)} %pile.14.refs_3_.refs_0_), channel_id=1, source_target_pairs={{0,8},{8,0},{16,24},{24,16},{1,9},{9,1},{17,25},{25,17},{2,10},{10... | collective-permute-start | bytes 786440 | tf_op jit(solution)/shard_map/ppermute | solution.py:1043
  39.8 23.6 %collective-permute-start.1 = (bf16[2,128,512]{2,1,0:T(8,128)(2,1)}, bf16[2,128,512]{2,1,0:T(8,128)(2,1)S(1)}, u32[]{:S(2)}, u32[]{:S(2)}) collective-permute-start(bf16[2,128,512]{2,1,0:T(8,128)(2,1)} %pile.12.refs_0_.refs_2_), channel_id=1, source_target_pairs={{0,8},{8,0},{16,24},{24,16},{1,9},{9,1},{17,25},{25,17},{2,10},{10... | collective-permute-start | bytes 786440 | tf_op jit(solution)/shard_map/ppermute | solution.py:1043
  41.4 26.2 %collective-permute-start.4 = (bf16[64,2048]{1,0:T(8,128)(2,1)}, bf16[64,2048]{1,0:T(8,128)(2,1)S(1)}, u32[]{:S(2)}, u32[]{:S(2)}) collective-permute-start(bf16[64,2048]{1,0:T(8,128)(2,1)} %get-tuple-element.94.refs_0_), channel_id=1, source_target_pairs={{0,16},{8,24},{16,0},{24,8},{1,17},{9,25},{17,1},{25,9},{2,18},{10... | collective-permute-start | bytes 786440 | tf_op jit(solution)/shard_map/ppermute | solution.py:1043
  44.7 30.3 %collective-permute-start.6 = (bf16[64,2048]{1,0:T(8,128)(2,1)}, bf16[64,2048]{1,0:T(8,128)(2,1)S(1)}, u32[]{:S(2)}, u32[]{:S(2)}) collective-permute-start(bf16[64,2048]{1,0:T(8,128)(2,1)} %get-tuple-element.95.refs_0_), channel_id=1, source_target_pairs={{0,16},{8,24},{16,0},{24,8},{1,17},{9,25},{17,1},{25,9},{2,18},{10... | collective-permute-start | bytes 786440 | tf_op jit(solution)/shard_map/ppermute | solution.py:1043
  58.4 20.2 %collective-permute-start.8 = (bf16[2,2,128,512]{3,2,1,0:T(8,128)(2,1)}, bf16[2,2,128,512]{3,2,1,0:T(8,128)(2,1)S(1)}, u32[]{:S(2)}, u32[]{:S(2)}) collective-permute-start(bf16[2,2,128,512]{3,2,1,0:T(8,128)(2,1)} %pile.15.refs_3_.refs_0_), channel_id=1, source_target_pairs={{0,4},{4,0},{1,5},{5,1},{2,6},{6,2},{3,7},{7,3},{8,12},{12,8},{9,1... | collective-permute-start | bytes 1572872 | tf_op jit(solution)/shard_map/ppermute | solution.py:1039
  66.7 17.1 %collective-permute-start.2 = (bf16[2,2,128,512]{3,2,1,0:T(8,128)(2,1)}, bf16[2,2,128,512]{3,2,1,0:T(8,128)(2,1)S(1)}, u32[]{:S(2)}, u32[]{:S(2)}) collective-permute-start(bf16[2,2,128,512]{3,2,1,0:T(8,128)(2,1)} %pile.13.refs_2_.refs_0_), channel_id=1, source_target_pairs={{0,1},{1,0},{2,3},{3,2},{4,5},{5,4},{6,7},{7,6},{8,9},{9,8},{10,11... | collective-permute-start | bytes 1572872 | tf_op jit(solution)/shard_map/ppermute | solution.py:1039
  70.9 24.9 %collective-permute-start.10 = (bf16[2,64,2048]{2,1,0:T(8,128)(2,1)}, bf16[2,64,2048]{2,1,0:T(8,128)(2,1)S(1)}, u32[]{:S(2)}, u32[]{:S(2)}) collective-permute-start(bf16[2,64,2048]{2,1,0:T(8,128)(2,1)} %pile.16.refs_2_.refs_0_), channel_id=1, source_target_pairs={{0,8},{8,0},{16,24},{24,16},{1,9},{9,1},{17,25},{25,17},{2,10},{10... | collective-permute-start | bytes 1572872 | tf_op jit(solution)/shard_map/ppermute | solution.py:1043
  78.2 32.8 %collective-permute-start.11 = (bf16[2,64,2048]{2,1,0:T(8,128)(2,1)}, bf16[2,64,2048]{2,1,0:T(8,128)(2,1)S(1)}, u32[]{:S(2)}, u32[]{:S(2)}) collective-permute-start(bf16[2,64,2048]{2,1,0:T(8,128)(2,1)} %pile.17.refs_3_.refs_0_), channel_id=1, source_target_pairs={{0,8},{8,0},{16,24},{24,16},{1,9},{9,1},{17,25},{25,17},{2,10},{10... | collective-permute-start | bytes 1572872 | tf_op jit(solution)/shard_map/ppermute | solution.py:1043
  82.2 34.0 %collective-permute-start.9 = (bf16[2,2,2,128,512]{4,3,2,1,0:T(8,128)(2,1)}, bf16[2,2,2,128,512]{4,3,2,1,0:T(8,128)(2,1)S(1)}, u32[]{:S(2)}, u32[]{:S(2)}) collective-permute-start(bf16[2,2,2,128,512]{4,3,2,1,0:T(8,128)(2,1)} %pile.19.refs_3_.refs_2_), channel_id=1, source_target_pairs={{0,1},{1,0},{2,3},{3,2},{4,5},{5,4},{6,7},{7,6},{8,9},{9,8},{10,11... | collective-permute-start | bytes 3145736 | tf_op jit(solution)/shard_map/ppermute | solution.py:1039
  87.4 28.8 %collective-permute-start.7 = (bf16[2,2,2,128,512]{4,3,2,1,0:T(8,128)(2,1)}, bf16[2,2,2,128,512]{4,3,2,1,0:T(8,128)(2,1)S(1)}, u32[]{:S(2)}, u32[]{:S(2)}) collective-permute-start(bf16[2,2,2,128,512]{4,3,2,1,0:T(8,128)(2,1)} %pile.18.refs_2_.refs_0_), channel_id=1, source_target_pairs={{0,4},{4,0},{1,5},{5,1},{2,6},{6,2},{3,7},{7,3},{8,12},{12,8},{9,1... | collective-permute-start | bytes 3145736 | tf_op jit(solution)/shard_map/ppermute | solution.py:1039
  99.5 35.3 %collective-permute-start.16 = (bf16[2,2,64,2048]{3,2,1,0:T(8,128)(2,1)}, bf16[2,2,64,2048]{3,2,1,0:T(8,128)(2,1)S(1)}, u32[]{:S(2)}, u32[]{:S(2)}) collective-permute-start(bf16[2,2,64,2048]{3,2,1,0:T(8,128)(2,1)} %pile.20.refs_4_.refs_0_), channel_id=1, source_target_pairs={{0,4},{4,0},{1,5},{5,1},{2,6},{6,2},{3,7},{7,3},{8,12},{12,8},{9,1... | collective-permute-start | bytes 3145736 | tf_op jit(solution)/shard_map/ppermute | solution.py:1039
  114.8 26.2 %collective-permute-start.18 = (bf16[2,2,64,2048]{3,2,1,0:T(8,128)(2,1)}, bf16[2,2,64,2048]{3,2,1,0:T(8,128)(2,1)}, u32[]{:S(2)}, u32[]{:S(2)}) collective-permute-start(bf16[2,2,64,2048]{3,2,1,0:T(8,128)(2,1)} %pile.21.refs_5_.refs_0_), channel_id=1, source_target_pairs={{0,1},{1,0},{2,3},{3,2},{4,5},{5,4},{6,7},{7,6},{8,9},{9,8},{10,11... | collective-permute-start | bytes 3145736 | tf_op jit(solution)/shard_map/ppermute | solution.py:1039
  118.9 26.8 %collective-permute-start.12 = (bf16[2,2,2,128,512]{4,3,2,1,0:T(8,128)(2,1)}, bf16[2,2,2,128,512]{4,3,2,1,0:T(8,128)(2,1)}, u32[]{:S(2)}, u32[]{:S(2)}) collective-permute-start(bf16[2,2,2,128,512]{4,3,2,1,0:T(8,128)(2,1)} %get-tuple-element.96.refs_2_), channel_id=1, source_target_pairs={{0,2},{2,0},{1,3},{3,1},{4,6},{6,4},{5,7},{7,5},{8,10},{10,8},{9,1... | collective-permute-start | bytes 3145736 | tf_op jit(solution)/shard_map/ppermute | solution.py:1039
  139.5 63.8 %collective-permute-start.17 = (bf16[2,2,2,64,2048]{4,3,2,1,0:T(8,128)(2,1)}, bf16[2,2,2,64,2048]{4,3,2,1,0:T(8,128)(2,1)}, u32[]{:S(2)}, u32[]{:S(2)}) collective-permute-start(bf16[2,2,2,64,2048]{4,3,2,1,0:T(8,128)(2,1)} %pile.22.refs_0_), channel_id=1, source_target_pairs={{0,1},{1,0},{2,3},{3,2},{4,5},{5,4},{6,7},{7,6},{8,9},{9,8},{10,11... | collective-permute-start | bytes 6291464 | tf_op jit(solution)/shard_map/ppermute | solution.py:1039
  144.6 58.7 %collective-permute-start.19 = (bf16[2,2,2,64,2048]{4,3,2,1,0:T(8,128)(2,1)}, bf16[2,2,2,64,2048]{4,3,2,1,0:T(8,128)(2,1)S(1)}, u32[]{:S(2)}, u32[]{:S(2)}) collective-permute-start(bf16[2,2,2,64,2048]{4,3,2,1,0:T(8,128)(2,1)} %pile.23.refs_2_), channel_id=1, source_target_pairs={{0,4},{4,0},{1,5},{5,1},{2,6},{6,2},{3,7},{7,3},{8,12},{12,8},{9,1... | collective-permute-start | bytes 6291464 | tf_op jit(solution)/shard_map/ppermute | solution.py:1039
  145.2 4.4 collective-permute-start.13
  145.2 5.4 collective-permute-start.14
  145.7 5.5 collective-permute-start.15
  205.4 14.3 %collective-permute-start.21 = (bf16[2,2,2,64,2048]{4,3,2,1,0:T(8,128)(2,1)}, bf16[2,2,2,64,2048]{4,3,2,1,0:T(8,128)(2,1)}, u32[]{:S(2)}, u32[]{:S(2)}) collective-permute-start(bf16[2,2,2,64,2048]{4,3,2,1,0:T(8,128)(2,1)} %get-tuple-element.106.refs_2_.refs_8_), channel_id=1, source_target_pairs={{0,2},{2,0},{1,3},{3,1},{4,6},{6,4},{5,7},{7,5},{8,10},{10,8},{9,1... | collective-permute-start | bytes 6291464 | tf_op jit(solution)/shard_map/ppermute | solution.py:1039
  205.6 30.7 %collective-permute-start.20 = (bf16[2,2,2,64,2048]{4,3,2,1,0:T(8,128)(2,1)}, bf16[2,2,2,64,2048]{4,3,2,1,0:T(8,128)(2,1)}, u32[]{:S(2)}, u32[]{:S(2)}) collective-permute-start(bf16[2,2,2,64,2048]{4,3,2,1,0:T(8,128)(2,1)} %get-tuple-element.104.refs_2_.refs_8_), channel_id=1, source_target_pairs={{0,2},{2,0},{1,3},{3,1},{4,6},{6,4},{5,7},{7,5},{8,10},{10,8},{9,1... | collective-permute-start | bytes 6291464 | tf_op jit(solution)/shard_map/ppermute | solution.py:1039
  206.0 46.8 %collective-permute-start.22 = (bf16[2,2,2,64,2048]{4,3,2,1,0:T(8,128)(2,1)}, bf16[2,2,2,64,2048]{4,3,2,1,0:T(8,128)(2,1)S(1)}, u32[]{:S(2)}, u32[]{:S(2)}) collective-permute-start(bf16[2,2,2,64,2048]{4,3,2,1,0:T(8,128)(2,1)} %get-tuple-element.109.refs_6_.refs_4_), channel_id=1, source_target_pairs={{0,2},{2,0},{1,3},{3,1},{4,6},{6,4},{5,7},{7,5},{8,10},{10,8},{9,1... | collective-permute-start | bytes 6291464 | tf_op jit(solution)/shard_map/ppermute | solution.py:1039
  206.2 46.7 %collective-permute-start.23 = (bf16[2,2,2,64,2048]{4,3,2,1,0:T(8,128)(2,1)}, bf16[2,2,2,64,2048]{4,3,2,1,0:T(8,128)(2,1)}, u32[]{:S(2)}, u32[]{:S(2)}) collective-permute-start(bf16[2,2,2,64,2048]{4,3,2,1,0:T(8,128)(2,1)} %get-tuple-element.110.refs_7_.refs_5_), channel_id=1, source_target_pairs={{0,2},{2,0},{1,3},{3,1},{4,6},{6,4},{5,7},{7,5},{8,10},{10,8},{9,1... | collective-permute-start | bytes 6291464 | tf_op jit(solution)/shard_map/ppermute | solution.py:1039
  306.9 44.1 %collective-permute-start.46 = (bf16[2,2,2,64,2048]{4,3,2,1,0:T(8,128)(2,1)}, bf16[2,2,2,64,2048]{4,3,2,1,0:T(8,128)(2,1)S(1)}, u32[]{:S(2)}, u32[]{:S(2)}) collective-permute-start(bf16[2,2,2,64,2048]{4,3,2,1,0:T(8,128)(2,1)} %get-tuple-element.164), channel_id=1, source_target_pairs={{0,2},{2,0},{1,3},{3,1},{4,6},{6,4},{5,7},{7,5},{8,10},{10,8},{9,1... | collective-permute-start | bytes 6291464 | tf_op jit(solution)/shard_map/ppermute | solution.py:1039
  307.1 48.9 %collective-permute-start.53 = (bf16[2,2,2,64,2048]{4,3,2,1,0:T(8,128)(2,1)}, bf16[2,2,2,64,2048]{4,3,2,1,0:T(8,128)(2,1)}, u32[]{:S(2)}, u32[]{:S(2)}) collective-permute-start(bf16[2,2,2,64,2048]{4,3,2,1,0:T(8,128)(2,1)} %get-tuple-element.168), channel_id=1, source_target_pairs={{0,2},{2,0},{1,3},{3,1},{4,6},{6,4},{5,7},{7,5},{8,10},{10,8},{9,1... | collective-permute-start | bytes 6291464 | tf_op jit(solution)/shard_map/ppermute | solution.py:1039
  349.8 54.6 %collective-permute-start.51 = (bf16[2,2,2,64,2048]{4,3,2,1,0:T(8,128)(2,1)}, bf16[2,2,2,64,2048]{4,3,2,1,0:T(8,128)(2,1)}, u32[]{:S(2)}, u32[]{:S(2)}) collective-permute-start(bf16[2,2,2,64,2048]{4,3,2,1,0:T(8,128)(2,1)} %get-tuple-element.166), channel_id=1, source_target_pairs={{0,2},{2,0},{1,3},{3,1},{4,6},{6,4},{5,7},{7,5},{8,10},{10,8},{9,1... | collective-permute-start | bytes 6291464 | tf_op jit(solution)/shard_map/ppermute | solution.py:1039
  350.0 101.2 %collective-permute-start.45 = (bf16[2,2,2,64,2048]{4,3,2,1,0:T(8,128)(2,1)}, bf16[2,2,2,64,2048]{4,3,2,1,0:T(8,128)(2,1)}, u32[]{:S(2)}, u32[]{:S(2)}) collective-permute-start(bf16[2,2,2,64,2048]{4,3,2,1,0:T(8,128)(2,1)} %get-tuple-element.162), channel_id=1, source_target_pairs={{0,2},{2,0},{1,3},{3,1},{4,6},{6,4},{5,7},{7,5},{8,10},{10,8},{9,1... | collective-permute-start | bytes 6291464 | tf_op jit(solution)/shard_map/ppermute | solution.py:1039
  354.9 96.3 %collective-permute-start.47 = (bf16[2,2,2,64,2048]{4,3,2,1,0:T(8,128)(2,1)}, bf16[2,2,2,64,2048]{4,3,2,1,0:T(8,128)(2,1)}, u32[]{:S(2)}, u32[]{:S(2)}) collective-permute-start(bf16[2,2,2,64,2048]{4,3,2,1,0:T(8,128)(2,1)} %add_convert_fusion), channel_id=1, source_target_pairs={{0,1},{1,0},{2,3},{3,2},{4,5},{5,4},{6,7},{7,6},{8,9},{9,8},{10,11... | collective-permute-start | bytes 6291464 | tf_op jit(solution)/shard_map/ppermute | solution.py:1039
  357.7 51.1 %collective-permute-start.54 = (bf16[2,2,64,2048]{3,2,1,0:T(8,128)(2,1)S(1)}, bf16[2,2,64,2048]{3,2,1,0:T(8,128)(2,1)}, u32[]{:S(2)}, u32[]{:S(2)}) collective-permute-start(bf16[2,2,64,2048]{3,2,1,0:T(8,128)(2,1)S(1)} %fusion.8), channel_id=1, source_target_pairs={{0,4},{4,0},{1,5},{5,1},{2,6},{6,2},{3,7},{7,3},{8,12},{12,8},{9,1... | collective-permute-start | bytes 3145736 | tf_op jit(solution)/shard_map/ppermute | solution.py:1039
  368.8 35.6 %copy-start.4 = (bf16[2,2,2,64,2048]{4,3,2,1,0:T(8,128)(2,1)S(1)}, bf16[2,2,2,64,2048]{4,3,2,1,0:T(8,128)(2,1)}, u32[]{:S(2)}) copy-start(bf16[2,2,2,64,2048]{4,3,2,1,0:T(8,128)(2,1)} %get-tuple-element.128.refs_1_) | copy-start | bytes 6291460
  407.0 69.2 %collective-permute-start.52 = (bf16[2,2,64,2048]{3,2,1,0:T(8,128)(2,1)}, bf16[2,2,64,2048]{3,2,1,0:T(8,128)(2,1)}, u32[]{:S(2)}, u32[]{:S(2)}) collective-permute-start(bf16[2,2,64,2048]{3,2,1,0:T(8,128)(2,1)} %fusion.7), channel_id=1, source_target_pairs={{0,4},{4,0},{1,5},{5,1},{2,6},{6,2},{3,7},{7,3},{8,12},{12,8},{9,1... | collective-permute-start | bytes 3145736 | tf_op jit(solution)/shard_map/ppermute | solution.py:1039
  412.4 63.8 %collective-permute-start.55 = (bf16[2,2,64,2048]{3,2,1,0:T(8,128)(2,1)}, bf16[2,2,64,2048]{3,2,1,0:T(8,128)(2,1)}, u32[]{:S(2)}, u32[]{:S(2)}) collective-permute-start(bf16[2,2,64,2048]{3,2,1,0:T(8,128)(2,1)} %fusion.2), channel_id=1, source_target_pairs={{0,1},{1,0},{2,3},{3,2},{4,5},{5,4},{6,7},{7,6},{8,9},{9,8},{10,11... | collective-permute-start | bytes 3145736 | tf_op jit(solution)/shard_map/ppermute | solution.py:1039
  454.5 78.3 %collective-permute-start.48 = (bf16[2,2,64,2048]{3,2,1,0:T(8,128)(2,1)}, bf16[2,2,64,2048]{3,2,1,0:T(8,128)(2,1)}, u32[]{:S(2)}, u32[]{:S(2)}) collective-permute-start(bf16[2,2,64,2048]{3,2,1,0:T(8,128)(2,1)} %fusion.6), channel_id=1, source_target_pairs={{0,4},{4,0},{1,5},{5,1},{2,6},{6,2},{3,7},{7,3},{8,12},{12,8},{9,1... | collective-permute-start | bytes 3145736 | tf_op jit(solution)/shard_map/ppermute | solution.py:1039
  476.2 62.4 %collective-permute-start.37 = (bf16[2,2,2,2,2,64,512]{6,5,4,3,0,2,1:T(8,128)(2,1)}, bf16[2,2,2,2,2,64,512]{6,5,4,3,0,2,1:T(8,128)(2,1)}, u32[]{:S(2)}, u32[]{:S(2)}) collective-permute-start(bf16[2,2,2,2,2,64,512]{6,5,4,3,0,2,1:T(8,128)(2,1)} %slice.281), channel_id=1, source_target_pairs={{0,2},{2,0},{1,3},{3,1},{4,6},{6,4},{5,7},{7,5},{8,10},{10,8},{9,1... | collective-permute-start | bytes 6291464 | tf_op jit(solution)/shard_map/ppermute | solution.py:1039
  480.4 50.4 %collective-permute-start.56 = (bf16[2,64,2048]{2,1,0:T(8,128)(2,1)}, bf16[2,64,2048]{2,1,0:T(8,128)(2,1)}, u32[]{:S(2)}, u32[]{:S(2)}) collective-permute-start(bf16[2,64,2048]{2,1,0:T(8,128)(2,1)} %fusion.17), channel_id=1, source_target_pairs={{0,8},{8,0},{16,24},{24,16},{1,9},{9,1},{17,25},{25,17},{2,10},{10... | collective-permute-start | bytes 1572872 | tf_op jit(solution)/shard_map/ppermute | solution.py:1043
  483.5 58.6 %collective-permute-start.40 = (bf16[2,2,2,2,2,64,512]{6,5,4,3,1,0,2:T(8,128)(2,1)}, bf16[2,2,2,2,2,64,512]{6,5,4,3,1,0,2:T(8,128)(2,1)}, u32[]{:S(2)}, u32[]{:S(2)}) collective-permute-start(bf16[2,2,2,2,2,64,512]{6,5,4,3,1,0,2:T(8,128)(2,1)} %pad_maximum_fusion.1), channel_id=1, source_target_pairs={{0,2},{2,0},{1,3},{3,1},{4,6},{6,4},{5,7},{7,5},{8,10},{10,8},{9,1... | collective-permute-start | bytes 6291464 | tf_op jit(solution)/shard_map/ppermute | solution.py:1039
  530.2 15.8 %collective-permute-start.24 = (bf16[2,2,2,2,64,512]{5,4,3,2,0,1:T(8,128)(2,1)}, bf16[2,2,2,2,64,512]{5,4,3,2,0,1:T(8,128)(2,1)}, u32[]{:S(2)}, u32[]{:S(2)}) collective-permute-start(bf16[2,2,2,2,64,512]{5,4,3,2,0,1:T(8,128)(2,1)} %copy.83), channel_id=1, source_target_pairs={{0,2},{2,0},{1,3},{3,1},{4,6},{6,4},{5,7},{7,5},{8,10},{10,8},{9,1... | collective-permute-start | bytes 3145736 | tf_op jit(solution)/shard_map/ppermute | solution.py:1039
  530.8 17.2 %collective-permute-start.25 = (bf16[2,2,2,2,64,512]{5,4,3,2,1,0:T(8,128)(2,1)}, bf16[2,2,2,2,64,512]{5,4,3,2,1,0:T(8,128)(2,1)}, u32[]{:S(2)}, u32[]{:S(2)}) collective-permute-start(bf16[2,2,2,2,64,512]{5,4,3,2,1,0:T(8,128)(2,1)} %get-tuple-element.146), channel_id=1, source_target_pairs={{0,2},{2,0},{1,3},{3,1},{4,6},{6,4},{5,7},{7,5},{8,10},{10,8},{9,1... | collective-permute-start | bytes 3145736 | tf_op jit(solution)/shard_map/ppermute | solution.py:1039
  532.8 32.2 %collective-permute-start.57 = (bf16[64,2048]{1,0:T(8,128)(2,1)}, bf16[64,2048]{1,0:T(8,128)(2,1)S(1)}, u32[]{:S(2)}, u32[]{:S(2)}) collective-permute-start(bf16[64,2048]{1,0:T(8,128)(2,1)} %fusion.30), channel_id=1, source_target_pairs={{0,16},{8,24},{16,0},{24,8},{1,17},{9,25},{17,1},{25,9},{2,18},{10... | collective-permute-start | bytes 786440 | tf_op jit(solution)/shard_map/ppermute | solution.py:1043
  538.6 31.1 %collective-permute-start.49 = (bf16[2,64,2048]{2,1,0:T(8,128)(2,1)}, bf16[2,64,2048]{2,1,0:T(8,128)(2,1)}, u32[]{:S(2)}, u32[]{:S(2)}) collective-permute-start(bf16[2,64,2048]{2,1,0:T(8,128)(2,1)} %fusion.16), channel_id=1, source_target_pairs={{0,8},{8,0},{16,24},{24,16},{1,9},{9,1},{17,25},{25,17},{2,10},{10... | collective-permute-start | bytes 1572872 | tf_op jit(solution)/shard_map/ppermute | solution.py:1043
  560.5 3.1 collective-permute-start.32
  563.0 16.7 %collective-permute-start.28 = (bf16[2,2,2,64,512]{4,3,2,1,0:T(8,128)(2,1)}, bf16[2,2,2,64,512]{4,3,2,1,0:T(8,128)(2,1)}, u32[]{:S(2)}, u32[]{:S(2)}) collective-permute-start(bf16[2,2,2,64,512]{4,3,2,1,0:T(8,128)(2,1)} %copy-done.20), channel_id=1, source_target_pairs={{0,4},{4,0},{1,5},{5,1},{2,6},{6,2},{3,7},{7,3},{8,12},{12,8},{9,1... | collective-permute-start | bytes 1572872 | tf_op jit(solution)/shard_map/ppermute | solution.py:1039
  564.4 3.9 collective-permute-start.33
  568.3 10.0 %collective-permute-start.34 = (f32[8,1024]{1,0:T(8,128)S(1)}, f32[8,1024]{1,0:T(8,128)S(1)}, u32[]{:S(2)}, u32[]{:S(2)}) collective-permute-start(f32[8,1024]{1,0:T(8,128)S(1)} %add.240), channel_id=1, source_target_pairs={{0,4},{4,0},{1,5},{5,1},{2,6},{6,2},{3,7},{7,3},{8,12},{12,8},{9,1... | collective-permute-start | bytes 98312 | tf_op jit(solution)/shard_map/ppermute | solution.py:1039
  570.9 49.9 %collective-permute-start.38 = (bf16[2,2,2,2,64,512]{5,4,3,2,0,1:T(8,128)(2,1)}, bf16[2,2,2,2,64,512]{5,4,3,2,0,1:T(8,128)(2,1)S(1)}, u32[]{:S(2)}, u32[]{:S(2)}) collective-permute-start(bf16[2,2,2,2,64,512]{5,4,3,2,0,1:T(8,128)(2,1)} %fusion.4), channel_id=1, source_target_pairs={{0,1},{1,0},{2,3},{3,2},{4,5},{5,4},{6,7},{7,6},{8,9},{9,8},{10,11... | collective-permute-start | bytes 3145736 | tf_op jit(solution)/shard_map/ppermute | solution.py:1039
  571.5 37.0 %collective-permute-start.26 = (bf16[2,2,2,64,512]{4,3,2,1,0:T(8,128)(2,1)S(1)}, bf16[2,2,2,64,512]{4,3,2,1,0:T(8,128)(2,1)S(1)}, u32[]{:S(2)}, u32[]{:S(2)}) collective-permute-start(bf16[2,2,2,64,512]{4,3,2,1,0:T(8,128)(2,1)S(1)} %fusion.14), channel_id=1, source_target_pairs={{0,1},{1,0},{2,3},{3,2},{4,5},{5,4},{6,7},{7,6},{8,9},{9,8},{10,11... | collective-permute-start | bytes 1572872 | tf_op jit(solution)/shard_map/ppermute | solution.py:1039
  573.7 34.9 %copy-start.10 = (bf16[2,2,2,2,64,512]{5,4,3,2,1,0:T(8,128)(2,1)S(1)}, bf16[2,2,2,2,64,512]{5,4,3,2,1,0:T(8,128)(2,1)}, u32[]{:S(2)}) copy-start(bf16[2,2,2,2,64,512]{5,4,3,2,1,0:T(8,128)(2,1)} %get-tuple-element.149) | copy-start | bytes 3145732
  578.3 32.8 %collective-permute-start.35 = (f32[8,1024]{1,0:T(8,128)S(1)}, f32[8,1024]{1,0:T(8,128)S(1)}, u32[]{:S(2)}, u32[]{:S(2)}) collective-permute-start(f32[8,1024]{1,0:T(8,128)S(1)} %add.241), channel_id=1, source_target_pairs={{0,8},{8,0},{16,24},{24,16},{1,9},{9,1},{17,25},{25,17},{2,10},{10... | collective-permute-start | bytes 98312 | tf_op jit(solution)/shard_map/ppermute | solution.py:1043
  581.3 29.8 %copy-start.15 = (bf16[2,2,2,2,64,512]{5,4,3,2,1,0:T(8,128)(2,1)S(1)}, bf16[2,2,2,2,64,512]{5,4,3,2,1,0:T(8,128)(2,1)}, u32[]{:S(2)}) copy-start(bf16[2,2,2,2,64,512]{5,4,3,2,1,0:T(8,128)(2,1)} %fusion.5) | copy-start | bytes 3145732
  581.4 31.2 %collective-permute-start.29 = (bf16[2,2,64,512]{3,2,1,0:T(8,128)(2,1)S(1)}, bf16[2,2,64,512]{3,2,1,0:T(8,128)(2,1)S(1)}, u32[]{:S(2)}, u32[]{:S(2)}) collective-permute-start(bf16[2,2,64,512]{3,2,1,0:T(8,128)(2,1)S(1)} %fusion.32), channel_id=1, source_target_pairs={{0,1},{1,0},{2,3},{3,2},{4,5},{5,4},{6,7},{7,6},{8,9},{9,8},{10,11... | collective-permute-start | bytes 786440 | tf_op jit(solution)/shard_map/ppermute | solution.py:1039
  609.8 9.3 %collective-permute-start.27 = (bf16[2,2,64,512]{3,2,1,0:T(8,128)(2,1)S(1)}, bf16[2,2,64,512]{3,2,1,0:T(8,128)(2,1)S(1)}, u32[]{:S(2)}, u32[]{:S(2)}) collective-permute-start(bf16[2,2,64,512]{3,2,1,0:T(8,128)(2,1)S(1)} %fusion.31), channel_id=1, source_target_pairs={{0,4},{4,0},{1,5},{5,1},{2,6},{6,2},{3,7},{7,3},{8,12},{12,8},{9,1... | collective-permute-start | bytes 786440 | tf_op jit(solution)/shard_map/ppermute | solution.py:1039
  610.5 44.2 %collective-permute-start.50 = (bf16[64,2048]{1,0:T(8,128)(2,1)S(1)}, bf16[64,2048]{1,0:T(8,128)(2,1)S(1)}, u32[]{:S(2)}, u32[]{:S(2)}) collective-permute-start(bf16[64,2048]{1,0:T(8,128)(2,1)S(1)} %fusion.29), channel_id=1, source_target_pairs={{0,16},{8,24},{16,0},{24,8},{1,17},{9,25},{17,1},{25,9},{2,18},{10... | collective-permute-start | bytes 786440 | tf_op jit(solution)/shard_map/ppermute | solution.py:1043
  611.1 30.5 %collective-permute-start.41 = (bf16[2,2,2,2,64,512]{5,4,3,2,1,0:T(8,128)(2,1)S(1)}, bf16[2,2,2,2,64,512]{5,4,3,2,1,0:T(8,128)(2,1)S(1)}, u32[]{:S(2)}, u32[]{:S(2)}) collective-permute-start(bf16[2,2,2,2,64,512]{5,4,3,2,1,0:T(8,128)(2,1)S(1)} %copy-done.15), channel_id=1, source_target_pairs={{0,4},{4,0},{1,5},{5,1},{2,6},{6,2},{3,7},{7,3},{8,12},{12,8},{9,1... | collective-permute-start | bytes 3145736 | tf_op jit(solution)/shard_map/ppermute | solution.py:1039
  612.5 43.0 %collective-permute-start.36 = (f32[8,1024]{1,0:T(8,128)S(1)}, f32[8,1024]{1,0:T(8,128)S(1)}, u32[]{:S(2)}, u32[]{:S(2)}) collective-permute-start(f32[8,1024]{1,0:T(8,128)S(1)} %add.242), channel_id=1, source_target_pairs={{0,16},{8,24},{16,0},{24,8},{1,17},{9,25},{17,1},{25,9},{2,18},{10... | collective-permute-start | bytes 98312 | tf_op jit(solution)/shard_map/ppermute | solution.py:1043
  619.2 36.4 %collective-permute-start.30 = (bf16[2,64,1024]{2,1,0:T(8,128)(2,1)S(1)}, bf16[2,64,1024]{2,1,0:T(8,128)(2,1)S(1)}, u32[]{:S(2)}, u32[]{:S(2)}) collective-permute-start(bf16[2,64,1024]{2,1,0:T(8,128)(2,1)S(1)} %fusion.33), channel_id=1, source_target_pairs={{0,8},{8,0},{16,24},{24,16},{1,9},{9,1},{17,25},{25,17},{2,10},{10... | collective-permute-start | bytes 786440 | tf_op jit(solution)/shard_map/ppermute | solution.py:1043
  620.8 20.8 %copy-start.2 = (bf16[2,2,2,2,2,64,512]{6,5,4,3,2,1,0:T(8,128)(2,1)S(1)}, bf16[2,2,2,2,2,64,512]{6,5,4,3,2,1,0:T(8,128)(2,1)}, u32[]{:S(2)}) copy-start(bf16[2,2,2,2,2,64,512]{6,5,4,3,2,1,0:T(8,128)(2,1)} %get-tuple-element.159) | copy-start | bytes 6291460
  623.0 25.1 %collective-permute-start.39 = (bf16[2,2,2,64,512]{4,3,2,1,0:T(8,128)(2,1)S(1)}, bf16[2,2,2,64,512]{4,3,2,1,0:T(8,128)(2,1)S(1)}, u32[]{:S(2)}, u32[]{:S(2)}) collective-permute-start(bf16[2,2,2,64,512]{4,3,2,1,0:T(8,128)(2,1)S(1)} %fusion.18), channel_id=1, source_target_pairs={{0,4},{4,0},{1,5},{5,1},{2,6},{6,2},{3,7},{7,3},{8,12},{12,8},{9,1... | collective-permute-start | bytes 1572872 | tf_op jit(solution)/shard_map/ppermute | solution.py:1039
  643.3 9.2 %collective-permute-start.42 = (bf16[2,2,2,64,512]{4,3,2,1,0:T(8,128)(2,1)S(1)}, bf16[2,2,2,64,512]{4,3,2,1,0:T(8,128)(2,1)S(1)}, u32[]{:S(2)}, u32[]{:S(2)}) collective-permute-start(bf16[2,2,2,64,512]{4,3,2,1,0:T(8,128)(2,1)S(1)} %fusion.19), channel_id=1, source_target_pairs={{0,1},{1,0},{2,3},{3,2},{4,5},{5,4},{6,7},{7,6},{8,9},{9,8},{10,11... | collective-permute-start | bytes 1572872 | tf_op jit(solution)/shard_map/ppermute | solution.py:1039
  653.1 13.5 %collective-permute-start.43 = (bf16[2,64,2048]{2,1,0:T(8,128)(2,1)S(1)}, bf16[2,64,2048]{2,1,0:T(8,128)(2,1)S(1)}, u32[]{:S(2)}, u32[]{:S(2)}) collective-permute-start(bf16[2,64,2048]{2,1,0:T(8,128)(2,1)S(1)} %fusion.15), channel_id=1, source_target_pairs={{0,8},{8,0},{16,24},{24,16},{1,9},{9,1},{17,25},{25,17},{2,10},{10... | collective-permute-start | bytes 1572872 | tf_op jit(solution)/shard_map/ppermute | solution.py:1043
  655.7 11.7 %collective-permute-start.31 = (bf16[64,1024]{1,0:T(8,128)(2,1)S(1)}, bf16[64,1024]{1,0:T(8,128)(2,1)S(1)}, u32[]{:S(2)}, u32[]{:S(2)}) collective-permute-start(bf16[64,1024]{1,0:T(8,128)(2,1)S(1)} %fusion.34), channel_id=1, source_target_pairs={{0,16},{8,24},{16,0},{24,8},{1,17},{9,25},{17,1},{25,9},{2,18},{10... | collective-permute-start | bytes 393224 | tf_op jit(solution)/shard_map/ppermute | solution.py:1043
  666.8 9.1 %collective-permute-start.44 = (bf16[64,2048]{1,0:T(8,128)(2,1)S(1)}, bf16[64,2048]{1,0:T(8,128)(2,1)S(1)}, u32[]{:S(2)}, u32[]{:S(2)}) collective-permute-start(bf16[64,2048]{1,0:T(8,128)(2,1)S(1)} %fusion.28), channel_id=1, source_target_pairs={{0,16},{8,24},{16,0},{24,8},{1,17},{9,25},{17,1},{25,9},{2,18},{10... | collective-permute-start | bytes 786440 | tf_op jit(solution)/shard_map/ppermute | solution.py:1043
  (31 other events, 90.7 us)
Sparse Core Ops, SparseCore 0:
  17.8 89.0 all-gather.4
  349.9 60.6 all-gather.6
